TPU v7x, 512 devices: a whole 4x8x8 slice. The times are simulated.
512 devices in a mesh: tm: 16 (over y, core), grp: 32 (over z, x).
Axes of the slice: x: 4, y: 8, z: 8, core: 2. Of those that a mesh axis runs over, the one named last changes fastest.
Arguments:
- locations: float32 [16, 2, 65536], P(None, None, ('tm', 'grp')), may hold values from 0 to 32
- times: float32 [65536], P(('tm', 'grp')), may hold values from 0 to 65536, as said below
- background: float32 [65536], P(('tm', 'grp')), may hold values from 0.0005 to 0.005
- weights: float32 [16, 65536], P(None, ('tm', 'grp')), may hold values from -6 to 6
- window_start: int32 [1024], P(('tm', 'grp')), may hold values from 1 to 127, as said below
- live: int32 [512], P(('tm', 'grp')), may hold values from 1 to 128, 49152 in all
Outputs:
- grad: float32 [16, 2, 65536], P(None, None, ('tm', 'grp'))
- log_intensity: float32 [16, 65536], P(None, ('tm', 'grp'))
Inputs may be any that keep to these rules, and one draw needn't show every extreme that they name: `window_start`: for block b of children, with k = b mod 64, the value lies in k + 1 to 64 + k; the first block of every shard has 1, the last 127. `times`: times_i - i lies in 0 to 1. Some device holds 128 live events in every draw.
All inputs are finite; a program needn't handle non-finite values.
Results may differ from a plain program's by a relative error of at most 0.0003.
Values sent between devices are 32-bit elements; how exact they have to be, the bound alone decides.
No kernel may reach another device: no remote copies, remote signals or barrier semaphores. Data moves between devices by JAX's collectives and lax.ppermute only.
A program may use at most 192 MiB of HBM per device.

v0:
```python
import math

import jax
import jax.numpy as jnp
from jax import lax
from jax.sharding import PartitionSpec as P

offspring = 0.8
fast_rate = 0.125
slow_rate = 0.0009765625


def from_behind(value, axis, by):
    count = lax.axis_size(axis)
    pairs = [(i, i + by) for i in range(count) if 0 <= i + by < count]
    return lax.ppermute(value, axis, pairs)


def time_kernel(delta, allowed):
    safe_delta = jnp.where(allowed, delta, 0.0)
    value = (
        offspring
        * (
            0.5 * fast_rate * jnp.exp(-fast_rate * safe_delta)
            + 0.5 * slow_rate * jnp.exp(-slow_rate * safe_delta)
        )
        / (2.0 * math.pi)
    )
    return jnp.where(allowed, value, 0.0)


def per_device(locations, times, background, weights, window_start, live):
    chains = locations.shape[0]
    dev_events = times.shape[0]
    group_size = lax.axis_size("grp")
    shard_events = dev_events * group_size
    block_rows = dev_events // window_start.shape[0]
    slot_ids = jnp.arange(dev_events, dtype=jnp.int32)
    alive_mask = (slot_ids < live[0]).astype(jnp.float32)
    flat_locs = locations.reshape(chains * 2, dev_events)
    own_locs, own_times, own_alive = (
        lax.all_gather(flat_locs, "grp", axis=1, tiled=True),
        lax.all_gather(times, "grp", axis=0, tiled=True),
        lax.all_gather(alive_mask, "grp", axis=0, tiled=True),
    )
    prev_locs, prev_times, prev_alive = from_behind((own_locs, own_times, own_alive), "tm", 1)
    all_locs = jnp.concatenate([prev_locs, own_locs], axis=1).reshape(chains, 2, 2 * shard_events)
    all_times = jnp.concatenate([prev_times, own_times])
    all_alive = jnp.concatenate([prev_alive, own_alive])
    first_pos = lax.axis_index("grp") * dev_events
    child_pos = shard_events + first_pos + slot_ids
    window_limit = jnp.repeat(window_start, block_rows) * block_rows
    child_x = locations[:, 0, :]
    child_y = locations[:, 1, :]
    turns = group_size + 1

    def pair_tile(turn):
        base_pos = first_pos + turn * dev_events
        parent_locs = lax.dynamic_slice_in_dim(all_locs, base_pos, dev_events, 2)
        parent_times = lax.dynamic_slice_in_dim(all_times, base_pos, dev_events, 0)
        parent_alive = lax.dynamic_slice_in_dim(all_alive, base_pos, dev_events, 0)
        parent_pos = base_pos + slot_ids
        allowed = (
            (parent_pos[None, :] < child_pos[:, None])
            & (parent_pos[None, :] >= window_limit[:, None])
            & (parent_alive[None, :] > 0)
        )
        temporal = time_kernel(times[:, None] - parent_times[None, :], allowed)
        diff_x = child_x[:, :, None] - parent_locs[:, 0, None, :]
        diff_y = child_y[:, :, None] - parent_locs[:, 1, None, :]
        kernel = temporal[None] * jnp.exp(-0.5 * (diff_x * diff_x + diff_y * diff_y))
        return (base_pos, kernel, diff_x, diff_y)

    def first_pass(turn, running):
        summed, pull_x, pull_y = running
        base_pos, kernel, diff_x, diff_y = pair_tile(turn)
        return (
            summed + jnp.sum(kernel, axis=2),
            pull_x + jnp.sum(kernel * diff_x, axis=2),
            pull_y + jnp.sum(kernel * diff_y, axis=2),
        )

    empty_rows = jnp.zeros((chains, dev_events), jnp.float32)
    summed, pull_x, pull_y = lax.fori_loop(
        0, turns, first_pass, (empty_rows, empty_rows, empty_rows)
    )
    intensity = background[None, :] + summed
    log_intensity = alive_mask[None, :] * jnp.log(intensity)
    ratio = weights * alive_mask[None, :] / intensity

    def second_pass(turn, collected):
        base_pos, kernel, diff_x, diff_y = pair_tile(turn)
        weighted = ratio[:, :, None] * kernel
        pushed = jnp.stack(
            [jnp.sum(weighted * diff_x, axis=1), jnp.sum(weighted * diff_y, axis=1)], axis=1
        )
        current = lax.dynamic_slice_in_dim(collected, base_pos, dev_events, 2)
        return lax.dynamic_update_slice_in_dim(collected, current + pushed, base_pos, 2)

    partial_terms = lax.fori_loop(
        0, turns, second_pass, jnp.zeros((chains, 2, 2 * shard_events), jnp.float32)
    )
    prev_half = partial_terms[:, :, :shard_events]
    own_half = partial_terms[:, :, shard_events:]
    reduced = lax.psum_scatter(
        jnp.stack([prev_half, own_half]), "grp", scatter_dimension=3, tiled=True
    )
    returned = from_behind(reduced[0], "tm", -1)
    parent_side = reduced[1] + returned
    child_side = -ratio[:, None, :] * jnp.stack([pull_x, pull_y], axis=1)
    grad = child_side + parent_side
    return (grad, log_intensity)


def solution(mesh):
    return jax.shard_map(
        per_device,
        mesh=mesh,
        in_specs=(
            P(None, None, ("tm", "grp")),
            P(("tm", "grp")),
            P(("tm", "grp")),
            P(None, ("tm", "grp")),
            P(("tm", "grp")),
            P(("tm", "grp")),
        ),
        out_specs=(P(None, None, ("tm", "grp")), P(None, ("tm", "grp"))),
        check_vma=False,
    )
```

profile of v0, /device:TPU:25, one launch (start us, length us, event | category | flops | bytes accessed | tf_op | source)
XLA Modules:
  0.0 600.3 jit_solution(5191485831767681448)
XLA Ops:
  7.2 35.6 %all-gather.1 = f32[32,1,128]{2,1,0:T(1,128)S(1)} all-gather(f32[1,1,128]{2,1,0:T(1,128)} %bitcast.66), channel_id=1, replica_groups=mesh['tm'=16,'grp'=32] {'grp'}, dimensions={0}, use_global_device_ids=true | all-gather | bytes 16896 | tf_op jit(solution)/shard_map/all_gather | solution.py:43
  42.8 13.5 %collective-permute-start.1 = (f32[4096]{0:T(1024)S(1)}, f32[4096]{0:T(1024)S(1)}, u32[]{:S(2)}, u32[]{:S(2)}) collective-permute-start(f32[4096]{0:T(1024)S(1)} %bitcast.62), channel_id=1, source_target_pairs={{0,32},{32,64},{64,96},{96,128},{128,160},{160,192},{192,224},{224... | collective-permute-start | bytes 49160 | tf_op jit(solution)/shard_map/ppermute | solution.py:16
  57.0 28.4 %all-gather = f32[32,1,128]{2,1,0:T(1,128)S(1)} all-gather(f32[1,1,128]{2,1,0:T(1,128)S(1)} %fusion.27), channel_id=1, replica_groups=mesh['tm'=16,'grp'=32] {'grp'}, dimensions={0}, use_global_device_ids=true | all-gather | bytes 16896 | tf_op jit(solution)/shard_map/all_gather | solution.py:44
  85.4 10.7 %collective-permute-start = (f32[4096]{0:T(1024)S(1)}, f32[4096]{0:T(1024)S(1)}, u32[]{:S(2)}, u32[]{:S(2)}) collective-permute-start(f32[4096]{0:T(1024)S(1)} %bitcast.64), channel_id=1, source_target_pairs={{0,32},{32,64},{64,96},{96,128},{128,160},{160,192},{192,224},{224... | collective-permute-start | bytes 49160 | tf_op jit(solution)/shard_map/ppermute | solution.py:16
  96.0 33.0 %all_gather.11 = f32[32,4096]{1,0:T(8,128)S(1)} all-gather(f32[32,128]{1,0:T(8,128)} %bitcast.61), channel_id=1, replica_groups=mesh['tm'=16,'grp'=32] {'grp'}, dimensions={1}, use_global_device_ids=true | all-gather | bytes 540672 | tf_op jit(solution)/shard_map/all_gather | solution.py:42
  129.0 11.0 %collective-permute-start.2 = (f32[32,4096]{1,0:T(8,128)S(1)}, f32[32,4096]{1,0:T(8,128)S(1)}, u32[]{:S(2)}, u32[]{:S(2)}) collective-permute-start(f32[32,4096]{1,0:T(8,128)S(1)} %all_gather.11), channel_id=1, source_target_pairs={{0,32},{32,64},{64,96},{96,128},{128,160},{160,192},{192,224},{224... | collective-permute-start | bytes 1572872 | tf_op jit(solution)/shard_map/ppermute | solution.py:16
  141.6 4.6 collective-permute-done.2
  147.5 71.2 %while.37 = (s32[]{:T(128)}, f32[16,128]{1,0:T(8,128)S(1)}, f32[16,128]{1,0:T(8,128)S(1)}, f32[16,128]{1,0:T(8,128)S(1)}, s32[]{:T(128)}, /*index=5*/f32[8192]{0...) while((s32[]{:T(128)}, f32[16,128]{1,0:T(8,128)S(1)}, ...), condition=%wide.region_4.5_spmd.clone, body=%wide.region_0.4_spmd.clone.sunk | while | flops 3365257 | bytes 302110 | solution.py:84
  148.0 1.6 fusion.34
  150.2 1.6 fusion.34
  152.3 1.6 fusion.34
  154.5 1.6 fusion.34
  156.6 1.6 fusion.34
  158.8 1.6 fusion.34
  160.9 1.6 fusion.34
  163.1 1.6 fusion.34
  165.3 1.6 fusion.34
  171.7 1.6 fusion.34
  180.3 1.6 fusion.34
  182.5 1.6 fusion.34
  191.1 1.6 fusion.34
  193.3 1.6 fusion.34
  201.9 1.6 fusion.34
  212.7 1.6 fusion.34
  219.7 51.3 %while.36 = (s32[]{:T(128)}, f32[16,2,8192]{2,1,0:T(2,128)S(1)}, s32[]{:T(128)}, f32[16,128]{1,0:T(8,128)S(1)}, f32[8192]{0:T(1024)S(1)}, /*index=5*/f32[128]{0:...) while((s32[]{:T(128)}, f32[16,2,8192]{2,1,0:T(2,128)S(1)}, ...), condition=%wide.region_8.9_spmd.clone, body=%wide.region_5.8_spmd.clone.sunk | while | flops 3363208 | bytes 343051 | solution.py:100
  271.9 33.8 %copy.18 = f32[2,16,2,4096]{2,1,0,3:T(8,128)} copy(f32[2,16,2,4096]{3,2,1,0:T(2,128)S(1)} %pad_maximum_fusion.1) | data formatting | bytes 2097152
  305.7 54.9 %reshape.270 = f32[4096,64]{1,0:T(8,128)} reshape(f32[4096,2,16,2]{3,2,1,0:T(8,128)} %bitcast) | data formatting | bytes 2097152
  360.7 214.8 %reduce-scatter.4.cloned.1.call-done = f32[128,64]{1,0:T(8,128)} async-done(((f32[4096,64]{1,0:T(8,128)}), f32[128,64]{1,0:T(8,128)}) %reduce-scatter.4.cloned.1.call-update) | async-done | bytes 32784
  575.5 3.0 reshape.271
  579.6 1.6 copy.26
  581.3 7.8 %collective-permute-start.3 = (f32[16,2,128]{2,1,0:T(2,128)S(1)}, f32[16,2,128]{2,1,0:T(2,128)S(1)}, u32[]{:S(2)}, u32[]{:S(2)}) collective-permute-start(f32[16,2,128]{2,1,0:T(2,128)S(1)} %bitcast.67), channel_id=1, source_target_pairs={{32,0},{64,32},{96,64},{128,96},{160,128},{192,160},{224,192},{256... | collective-permute-start | bytes 49160 | tf_op jit(solution)/shard_map/ppermute | solution.py:16
  589.5 3.3 collective-permute-done.3
  (739 shorter events, 99.3 us)
Async XLA Ops:
  7.2 568.3 %reduce-scatter.4.cloned.1.call-start = ((), (), s32[]{:S(2)}) async-start(), calls=%async_computation.1 | async-start | bytes 2162688
  42.8 98.7 %collective-permute-start.1 = (f32[4096]{0:T(1024)S(1)}, f32[4096]{0:T(1024)S(1)}, u32[]{:S(2)}, u32[]{:S(2)}) collective-permute-start(f32[4096]{0:T(1024)S(1)} %bitcast.62), channel_id=1, source_target_pairs={{0,32},{32,64},{64,96},{96,128},{128,160},{160,192},{192,224},{224... | collective-permute-start | bytes 49160 | tf_op jit(solution)/shard_map/ppermute | solution.py:16
  85.4 56.2 %collective-permute-start = (f32[4096]{0:T(1024)S(1)}, f32[4096]{0:T(1024)S(1)}, u32[]{:S(2)}, u32[]{:S(2)}) collective-permute-start(f32[4096]{0:T(1024)S(1)} %bitcast.64), channel_id=1, source_target_pairs={{0,32},{32,64},{64,96},{96,128},{128,160},{160,192},{192,224},{224... | collective-permute-start | bytes 49160 | tf_op jit(solution)/shard_map/ppermute | solution.py:16
  129.0 17.1 %collective-permute-start.2 = (f32[32,4096]{1,0:T(8,128)S(1)}, f32[32,4096]{1,0:T(8,128)S(1)}, u32[]{:S(2)}, u32[]{:S(2)}) collective-permute-start(f32[32,4096]{1,0:T(8,128)S(1)} %all_gather.11), channel_id=1, source_target_pairs={{0,32},{32,64},{64,96},{96,128},{128,160},{160,192},{192,224},{224... | collective-permute-start | bytes 1572872 | tf_op jit(solution)/shard_map/ppermute | solution.py:16
  146.2 1.3 copy-start
  147.5 71.2 %copy-start.1 = (f32[16,128]{1,0:T(8,128)S(1)}, f32[16,128]{1,0:T(8,128)}, u32[]{:S(2)}) copy-start(f32[16,128]{1,0:T(8,128)} %param.13) | copy-start | bytes 24580
  147.5 71.2 %copy-start.2 = (f32[128]{0:T(128)S(1)}, f32[128]{0:T(128)}, u32[]{:S(2)}) copy-start(f32[128]{0:T(128)} %param.12) | copy-start | bytes 1540
  581.3 11.5 %collective-permute-start.3 = (f32[16,2,128]{2,1,0:T(2,128)S(1)}, f32[16,2,128]{2,1,0:T(2,128)S(1)}, u32[]{:S(2)}, u32[]{:S(2)}) collective-permute-start(f32[16,2,128]{2,1,0:T(2,128)S(1)} %bitcast.67), channel_id=1, source_target_pairs={{32,0},{64,32},{96,64},{128,96},{160,128},{192,160},{224,192},{256... | collective-permute-start | bytes 49160 | tf_op jit(solution)/shard_map/ppermute | solution.py:16
Sparse Core Ops, SparseCore 0:
  360.8 214.6 reduce-scatter.3
where the time goes:
time: 601 us; the launch traced here: 600 us
  waiting for transfers between devices  223 us (37%)
  local copies, waits for them, and re-layouts  114 us (19%)
  other arithmetic  104 us (17%)
  blocking collectives  97 us (16%)
  starting transfers between devices  43 us (7%)
  between operations  14.9 us (2%)
    unnamed x2, waiting for transfers between devices  215 us
    unnamed x12, local copies, waits for them, and re-layouts  94.5 us
    reduce_sum x33, other arithmetic, first_pass(): jnp.sum(kernel * diff_y, axis=2)  53.5 us
    ppermute x4, starting transfers between devices, from_behind(): return lax.ppermute(value, axis, pairs)  42.9 us
    all_gather x1, blocking collectives, per_device(): lax.all_gather(times, 'grp', axis=0, tiled=True)  35.6 us
    reduce_sum x33, other arithmetic, second_pass(): jnp.sum(weighted * diff_x, axis=1)  33.2 us
    all_gather x1, blocking collectives, per_device(): lax.all_gather(flat_locs, 'grp', axis=1, tiled=True)  33 us
    all_gather x1, blocking collectives, per_device(): lax.all_gather(alive_mask, 'grp', axis=0, tiled=True)  28.4 us
  transfers between devices with their start and end apart: 5, of which 3 were waited for; matrix products, arithmetic and copies ran while one was open for 0% of the time, Pallas kernels for 0%

commit v1 on v0

v1 whole, which is shorter than its diff:
```python
import math

import jax
import jax.numpy as jnp
from jax import lax
from jax.experimental import pallas as pl
from jax.experimental.pallas import tpu as pltpu
from jax.sharding import PartitionSpec as P

offspring = 0.8
fast_rate = 0.125
slow_rate = 0.0009765625

CH = 16
LANES = 128
TILES = 32
ROWS = 40
GROUP = 32
QUAD = 4
DEAD = -1e30

SCALE = math.sqrt(0.5 / math.log(2.0))
UNSCALE = 1.0 / SCALE
LOG2E = 1.0 / math.log(2.0)
LOG2_SLOW = math.log2(offspring * 0.5 * slow_rate / (2.0 * math.pi))


def from_behind(value, axis, by):
    count = lax.axis_size(axis)
    pairs = [(i, i + by) for i in range(count) if 0 <= i + by < count]
    return lax.ppermute(value, axis, pairs)


def log2_time_kernel(delta):
    fast = (fast_rate / slow_rate) * jnp.exp2(delta * (-(fast_rate - slow_rate) * LOG2E))
    return (LOG2_SLOW - delta * (slow_rate * LOG2E)) + jnp.log(1.0 + fast) * LOG2E


def pair_kernel(
    info, prev, own, weights, back, alive, child_side, logs, part_prev, part_own,
    log_t, child_b, kern, sums, ratio_b, total
):
    me = info[0]
    first_tile = (info[1] // LANES) // 2, (info[2] // LANES) // 2
    lane = lax.broadcasted_iota(jnp.int32, (CH, LANES), 1)
    mine = own[me]
    xs, ys = mine[0:CH], mine[CH : 2 * CH]
    pair_of_tiles = ((prev, 0), (own, TILES))

    for child in range(LANES):
        child_b[child] = jnp.broadcast_to(mine[0 : 2 * CH, child : child + 1], (2 * CH, LANES))

    row = lax.broadcasted_iota(jnp.int32, (LANES, LANES), 0)
    col = lax.broadcasted_iota(jnp.int32, (LANES, LANES), 1)
    child_time = jnp.transpose(jnp.broadcast_to(info_time(mine, alive), (LANES, LANES)))
    child_pos = (TILES + me) * LANES + row
    low = jnp.where(row < LANES // 2, info[1], info[2])
    span = child_pos - low

    def time_tiles(ref, offset):
        def body(step, carry):
            for u in range(2):
                q = 2 * step + u
                parent_time = ref[q, 2 * CH : 2 * CH + 1, :]
                value = log2_time_kernel(jnp.maximum(child_time - parent_time, 0.0))
                pos = (offset + q) * LANES + col
                ok = (pos >= low) & (pos < child_pos)
                log_t[offset + q] = jnp.where(ok, value, DEAD)
            return carry

        return body

    first = jnp.minimum(first_tile[0], first_tile[1])
    last_own = (me + 2) // 2
    lax.fori_loop(jnp.minimum(first, TILES // 2), TILES // 2, time_tiles(prev, 0), 0)
    lax.fori_loop(jnp.maximum(first - TILES // 2, 0), last_own, time_tiles(own, TILES), 0)

    def clear(q, carry):
        total[q] = jnp.zeros((3 * CH, LANES), jnp.float32)
        return carry

    lax.fori_loop(0, 2 * TILES, clear, 0)

    for group in range(LANES // GROUP):
        start = first_tile[group * GROUP // (LANES // 2)]
        prev_start = jnp.minimum(start, TILES // 2)
        own_start = jnp.maximum(start - TILES // 2, 0)

        def quad_sums(quad, carry):
            base = group * GROUP + quad * QUAD
            cx = [child_b[base + i, 0:CH] for i in range(QUAD)]
            cy = [child_b[base + i, CH : 2 * CH] for i in range(QUAD)]

            def tiles(ref, offset):
                def body(step, acc):
                    acc = list(acc)
                    for u in range(2):
                        q = 2 * step + u
                        px = ref[q, 0:CH]
                        py = ref[q, CH : 2 * CH]
                        for i in range(QUAD):
                            dx = px - cx[i]
                            dy = py - cy[i]
                            lt = log_t[offset + q, pl.ds(base + i, 1), :]
                            k = jnp.exp2((lt - dx * dx) - dy * dy)
                            kern[quad * QUAD + i, offset + q] = k
                            acc[3 * i] = acc[3 * i] + k
                            acc[3 * i + 1] = acc[3 * i + 1] + k * dx
                            acc[3 * i + 2] = acc[3 * i + 2] + k * dy
                    return tuple(acc)

                return body

            acc = tuple(jnp.zeros((CH, LANES), jnp.float32) for _ in range(3 * QUAD))
            acc = lax.fori_loop(prev_start, TILES // 2, tiles(prev, 0), acc)
            acc = lax.fori_loop(own_start, last_own, tiles(own, TILES), acc)
            for i in range(QUAD):
                for j in range(3):
                    sums[quad * QUAD + i, j * CH : (j + 1) * CH] = acc[3 * i + j]
            return carry

        lax.fori_loop(0, GROUP // QUAD, quad_sums, 0)

        collected = [jnp.zeros((CH, LANES), jnp.float32) for _ in range(3)]
        for i in range(GROUP):
            summed = jnp.sum(sums[i], axis=1, keepdims=True)
            for j in range(3):
                collected[j] = jnp.where(
                    lane == group * GROUP + i, summed[j * CH : (j + 1) * CH], collected[j]
                )
        intensity = back[...] + collected[0]
        ratio = weights[...] * alive[...] / intensity
        log_here = alive[...] * jnp.log(intensity)
        ratio_x, ratio_y = ratio * xs, ratio * ys
        side_x, side_y = ratio * collected[1] * UNSCALE, ratio * collected[2] * UNSCALE
        here = (lane >= group * GROUP) & (lane < (group + 1) * GROUP)
        logs[...] = jnp.where(here, log_here, logs[...])
        child_side[0:CH] = jnp.where(here, side_x, child_side[0:CH])
        child_side[CH : 2 * CH] = jnp.where(here, side_y, child_side[CH : 2 * CH])
        spread = jnp.concatenate([ratio, ratio_x, ratio_y], axis=0)
        for i in range(GROUP):
            at = group * GROUP + i
            ratio_b[i] = jnp.broadcast_to(spread[:, at : at + 1], (3 * CH, LANES))

        def quad_push(quad, carry):
            terms = [ratio_b[quad * QUAD + i] for i in range(QUAD)]

            def tiles(offset):
                def body(step, inner):
                    for u in range(2):
                        q = offset + 2 * step + u
                        ks = [kern[quad * QUAD + i, q] for i in range(QUAD)]
                        for j in range(3):
                            add = [ks[i] * terms[i][j * CH : (j + 1) * CH] for i in range(QUAD)]
                            at = slice(j * CH, (j + 1) * CH)
                            total[q, at] = total[q, at] + ((add[0] + add[1]) + (add[2] + add[3]))
                    return inner

                return body

            lax.fori_loop(prev_start, TILES // 2, tiles(0), 0)
            lax.fori_loop(own_start, last_own, tiles(TILES), 0)
            return carry

        lax.fori_loop(0, GROUP // QUAD, quad_push, 0)

    for ref, out, offset in ((prev, part_prev, 0), (own, part_own, TILES)):

        def finish(q, carry, ref=ref, out=out, offset=offset):
            weight = total[offset + q, 0:CH]
            for j in range(2):
                at = slice(j * CH, (j + 1) * CH)
                pulled = total[offset + q, (j + 1) * CH : (j + 2) * CH]
                out[q, at] = (pulled - ref[q, at] * weight) * UNSCALE
            return carry

        lax.fori_loop(0, TILES, finish, 0)


def info_time(mine, alive):
    return mine[2 * CH + 1 : 2 * CH + 2]


def pairs(info, prev, own, weights, back, alive):
    f32 = jnp.float32
    vmem = pl.BlockSpec(memory_space=pltpu.VMEM)
    return pl.pallas_call(
        pair_kernel,
        out_shape=(
            jax.ShapeDtypeStruct((2 * CH, LANES), f32),
            jax.ShapeDtypeStruct((CH, LANES), f32),
            jax.ShapeDtypeStruct((TILES, 2 * CH, LANES), f32),
            jax.ShapeDtypeStruct((TILES, 2 * CH, LANES), f32),
        ),
        in_specs=[pl.BlockSpec(memory_space=pltpu.SMEM)] + [vmem] * 5,
        out_specs=(vmem,) * 4,
        scratch_shapes=[
            pltpu.VMEM((2 * TILES, LANES, LANES), f32),
            pltpu.VMEM((LANES, 2 * CH, LANES), f32),
            pltpu.VMEM((GROUP, 2 * TILES, CH, LANES), f32),
            pltpu.VMEM((GROUP, 3 * CH, LANES), f32),
            pltpu.VMEM((GROUP, 3 * CH, LANES), f32),
            pltpu.VMEM((2 * TILES, 3 * CH, LANES), f32),
        ],
        compiler_params=pltpu.CompilerParams(vmem_limit_bytes=48 * 2**20),
    )(info, prev, own, weights, back, alive)


def per_device(locations, times, background, weights, window_start, live):
    slot_ids = jnp.arange(LANES, dtype=jnp.int32)
    alive = slot_ids < live[0]
    chunk = jnp.concatenate(
        [
            locations[:, 0, :] * SCALE,
            locations[:, 1, :] * SCALE,
            jnp.where(alive, times, DEAD)[None],
            times[None],
            jnp.zeros((ROWS - 2 * CH - 2, LANES), jnp.float32),
        ]
    )
    own = lax.all_to_all(jnp.broadcast_to(chunk[None], (TILES, ROWS, LANES)), "grp", 0, 0)
    prev = from_behind(own, "tm", 1)
    least = jnp.where(lax.axis_index("tm") == 0, TILES * LANES, 0)
    limit = jnp.maximum(window_start * (LANES // 2), least)
    info = jnp.concatenate([lax.axis_index("grp").astype(jnp.int32)[None], limit])
    child_side, log_intensity, part_prev, part_own = pairs(
        info, prev, own, weights, background[None], alive.astype(jnp.float32)[None]
    )
    part = part_own + from_behind(part_prev, "tm", -1)
    parent_side = jnp.sum(lax.all_to_all(part, "grp", 0, 0), axis=0)
    grad = (child_side + parent_side).reshape(2, CH, LANES).transpose(1, 0, 2)
    return (grad, log_intensity)


def solution(mesh):
    return jax.shard_map(
        per_device,
        mesh=mesh,
        in_specs=(
            P(None, None, ("tm", "grp")),
            P(("tm", "grp")),
            P(("tm", "grp")),
            P(None, ("tm", "grp")),
            P(("tm", "grp")),
            P(("tm", "grp")),
        ),
        out_specs=(P(None, None, ("tm", "grp")), P(None, ("tm", "grp"))),
        check_vma=False,
    )
```

time: 601 us -> 117 us (0.19)
  waiting for transfers between devices: 223 us -> 19.5 us
  local copies, waits for them, and re-layouts: 114 us -> 1.36 us
  other arithmetic: 104 us -> 1.04 us
  blocking collectives: 97 us -> 56.8 us
  starting transfers between devices: 43 us -> 10.4 us
  Pallas kernels: 0 us -> 25.6 us
  between operations: 14.9 us -> 1.39 us
    unnamed x2 -> x0, waiting for transfers between devices: 215 us -> none
    all_gather x3 -> x0, blocking collectives: 97 us -> none  [the longest x1 35.6 us: per_device(): lax.all_gather(times, 'grp', axis=0, tiled=True)]
    unnamed x12 -> x8, local copies, waits for them, and re-layouts: 94.5 us -> 0.67 us
    reduce_sum x66 -> x1, other arithmetic: 86.7 us -> 0.05 us  [per_device(): parent_side = jnp.sum(lax.all_to_all(part, 'grp', 0, 0), axis=0)]
    all_to_all x0 -> x2, blocking collectives: none -> 56.8 us  [the longest x1 31.4 us: per_device(): lax.all_to_all(jnp.broadcast_to(chunk[None], (TILES, ROWS, LANES)), 'grp'...]
    ppermute x4 -> x2, starting transfers between devices: 42.9 us -> 10.4 us  [from_behind(): return lax.ppermute(value, axis, pairs)]
    pallas_call x0 -> x1, Pallas kernels: none -> 25.6 us  [pairs(): pl.pallas_call(pair_kernel, out_shape=(jax.ShapeDtypeStruct((2 * CH, LANE...]
    ppermute x4 -> x2, waiting for transfers between devices: 7.87 us -> 19.5 us  [from_behind(): return lax.ppermute(value, axis, pairs)]
  transfers between devices with their start and end apart: 5 -> 2, of which waited for: 3 -> 2; matrix products, arithmetic and copies ran while one was open for 0% -> 0% of each run, Pallas kernels for 0% -> 0%
where the time goes in v1:
time: 117 us; the launch traced here: 116 us
  blocking collectives  56.8 us (49%)
  Pallas kernels  25.6 us (22%)
  waiting for transfers between devices  19.5 us (17%)
  starting transfers between devices  10.4 us (9%)
  between operations  1.39 us (1%)
  local copies, waits for them, and re-layouts  1.36 us (1%)
    all_to_all x1, blocking collectives, per_device(): lax.all_to_all(jnp.broadcast_to(chunk[None], (TILES, ROWS, LANES)), 'grp'...  31.4 us
    pallas_call x1, Pallas kernels, pairs(): pl.pallas_call(pair_kernel, out_shape=(jax.ShapeDtypeStruct((2 * CH, LANE...  25.6 us
    all_to_all x1, blocking collectives, per_device(): parent_side = jnp.sum(lax.all_to_all(part, 'grp', 0, 0), axis=0)  25.4 us
    ppermute x2, waiting for transfers between devices, from_behind(): return lax.ppermute(value, axis, pairs)  19.5 us
    ppermute x2, starting transfers between devices, from_behind(): return lax.ppermute(value, axis, pairs)  10.4 us
  transfers between devices with their start and end apart: 2, of which 2 were waited for; matrix products, arithmetic and copies ran while one was open for 0% of the time, Pallas kernels for 0%

profile of v1, /device:TPU:25, one launch (start us, length us, event | category | flops | bytes accessed | tf_op | source)
XLA Modules:
  0.0 116.1 jit_solution(8637462798550881739)
XLA Ops:
  1.3 0.8 slice_multiply_fusion
  2.1 0.0 copy-start.2
  2.1 0.6 copy-done.2
  2.9 0.0 copy-start.3
  2.9 31.4 %all_to_all.10.own = f32[32,40,128]{2,1,0:T(8,128)S(1)} all-to-all(f32[32,40,128]{2,1,0:T(8,128)S(1)} %broadcast_in_dim.31), channel_id=1, replica_groups=mesh['tm'=16,'grp'=32] {'grp'}, dimensions={0} | all-to-all | bytes 1310720 | tf_op jit(solution)/shard_map/all_to_all | solution.py:221
  34.3 6.7 %collective-permute-start = (f32[32,40,128]{2,1,0:T(8,128)S(1)}, f32[32,40,128]{2,1,0:T(8,128)S(1)}, u32[]{:S(2)}, u32[]{:S(2)}) collective-permute-start(f32[32,40,128]{2,1,0:T(8,128)S(1)} %all_to_all.10.own), channel_id=1, source_target_pairs={{0,32},{32,64},{64,96},{96,128},{128,160},{160,192},{192,224},{224... | collective-permute-start | bytes 1966088 | tf_op jit(solution)/shard_map/ppermute | solution.py:31
  41.0 0.0 copy-start
  41.0 0.0 copy-done.3
  41.1 0.1 pad_add_fusion.info
  41.1 0.0 copy-start.1
  41.1 7.4 %collective-permute-done.prev = f32[32,40,128]{2,1,0:T(8,128)S(1)} collective-permute-done((f32[32,40,128]{2,1,0:T(8,128)S(1)}, f32[32,40,128]{2,1,0:T(8,128)S(1)}, u32[]{:S(2)}, u32[]{:S(2)}) %collective-permute-start) | collective-permute-done | bytes 655392 | tf_op jit(solution)/shard_map/ppermute | solution.py:31
  48.5 0.0 copy-done
  48.5 0.0 copy-done.1
  48.5 25.6 %shard_map.77 = (f32[32,128]{1,0:T(8,128)S(1)}, f32[16,128]{1,0:T(8,128)}, f32[32,32,128]{2,1,0:T(8,128)S(1)}, f32[32,32,128]{2,1,0:T(8,128)S(1)}) custom-call(s32[3]{0:T(128)S(1)} %pad_add_fusion.info, f32[32,40,128]{2,1,0:T(8,128)S(1)} %collective-permute-done.prev, f32[32,40,128]{2,1,0:T(8,128)S(1)} %all_to_all.10.own, f32[16,128]{1,0:T(8,128)S(1)} %copy-done, ...), custom_call_target="tpu_custom_call" | custom-call | tf_op jit(solution)/shard_map/pallas_call | solution.py:187
  74.1 3.7 %collective-permute-start.1 = (f32[32,32,128]{2,1,0:T(8,128)S(1)}, f32[32,32,128]{2,1,0:T(8,128)S(1)}, u32[]{:S(2)}, u32[]{:S(2)}) collective-permute-start(f32[32,32,128]{2,1,0:T(8,128)S(1)} %get-tuple-element.8), channel_id=1, source_target_pairs={{32,0},{64,32},{96,64},{128,96},{160,128},{192,160},{224,192},{256... | collective-permute-start | bytes 1572872 | tf_op jit(solution)/shard_map/ppermute | solution.py:31
  77.8 12.1 %collective-permute-done.1 = f32[32,32,128]{2,1,0:T(8,128)S(1)} collective-permute-done((f32[32,32,128]{2,1,0:T(8,128)S(1)}, f32[32,32,128]{2,1,0:T(8,128)S(1)}, u32[]{:S(2)}, u32[]{:S(2)}) %collective-permute-start.1) | collective-permute-done | bytes 524320 | tf_op jit(solution)/shard_map/ppermute | solution.py:31
  89.9 0.1 add.6
  90.0 25.4 %all_to_all.11 = f32[32,32,128]{2,1,0:T(8,128)S(1)} all-to-all(f32[32,32,128]{2,1,0:T(8,128)S(1)} %add.6), channel_id=1, replica_groups=mesh['tm'=16,'grp'=32] {'grp'}, dimensions={0} | all-to-all | bytes 1048576 | tf_op jit(solution)/shard_map/all_to_all | solution.py:230
  115.5 0.6 copy.13
  (10 shorter events, 0.1 us)
Async XLA Ops:
  2.1 0.7 copy-start.2
  2.9 38.2 %copy-start.3 = (s32[2]{0:T(128)S(1)}, s32[2]{0:T(128)}, u32[]{:S(2)}) copy-start(s32[2]{0:T(128)} %param.10) | copy-start | bytes 28
  34.3 14.3 %collective-permute-start = (f32[32,40,128]{2,1,0:T(8,128)S(1)}, f32[32,40,128]{2,1,0:T(8,128)S(1)}, u32[]{:S(2)}, u32[]{:S(2)}) collective-permute-start(f32[32,40,128]{2,1,0:T(8,128)S(1)} %all_to_all.10.own), channel_id=1, source_target_pairs={{0,32},{32,64},{64,96},{96,128},{128,160},{160,192},{192,224},{224... | collective-permute-start | bytes 1966088 | tf_op jit(solution)/shard_map/ppermute | solution.py:31
  41.0 7.5 %copy-start = (f32[16,128]{1,0:T(8,128)S(1)}, f32[16,128]{1,0:T(8,128)}, u32[]{:S(2)}) copy-start(f32[16,128]{1,0:T(8,128)} %weights.1) | copy-start | bytes 24580
  41.1 7.4 %copy-start.1 = (f32[128]{0:T(128)S(1)}, f32[128]{0:T(128)}, u32[]{:S(2)}) copy-start(f32[128]{0:T(128)} %param.8) | copy-start | bytes 1540
  74.1 15.8 %collective-permute-start.1 = (f32[32,32,128]{2,1,0:T(8,128)S(1)}, f32[32,32,128]{2,1,0:T(8,128)S(1)}, u32[]{:S(2)}, u32[]{:S(2)}) collective-permute-start(f32[32,32,128]{2,1,0:T(8,128)S(1)} %get-tuple-element.8), channel_id=1, source_target_pairs={{32,0},{64,32},{96,64},{128,96},{160,128},{192,160},{224,192},{256... | collective-permute-start | bytes 1572872 | tf_op jit(solution)/shard_map/ppermute | solution.py:31

commit v2 on v1

v2 whole, which is shorter than its diff:
```python
import math

import jax
import jax.numpy as jnp
from jax import lax
from jax.experimental import pallas as pl
from jax.experimental.pallas import tpu as pltpu
from jax.sharding import PartitionSpec as P

offspring = 0.8
fast_rate = 0.125
slow_rate = 0.0009765625

CH = 16
LANES = 128
TILES = 32
BLK = 64
QUAD = 4
SLOTS = 32
DEAD = -1e30

DEAD_ROW, TIME_ROW, BACK_ROW, ALIVE_ROW, META_ROW = range(2 * CH, 2 * CH + 5)
W_ROW = 40
ROWS = W_ROW + CH
TILE, LANE0, LOW = 1, 1 + SLOTS, 1 + 2 * SLOTS

SCALE = math.sqrt(0.5 / math.log(2.0))
UNSCALE = 1.0 / SCALE
LOG2E = 1.0 / math.log(2.0)
LOG2_SLOW = math.log2(offspring * 0.5 * slow_rate / (2.0 * math.pi))


def from_behind(value, axis, by):
    count = lax.axis_size(axis)
    pairs = [(i, i + by) for i in range(count) if 0 <= i + by < count]
    return lax.ppermute(value, axis, pairs)


def log2_time_kernel(delta):
    fast = (fast_rate / slow_rate) * jnp.exp2(delta * (-(fast_rate - slow_rate) * LOG2E))
    return (LOG2_SLOW - delta * (slow_rate * LOG2E)) + jnp.log(1.0 + fast) * LOG2E


def pair_kernel(
    info, prev, own, part_prev, part_own, log_t, child_b, kern, sums, ratio_b, total, times_q, child_t
):
    count = info[0]
    lane = lax.broadcasted_iota(jnp.int32, (1, LANES), 1)

    packed = jnp.zeros((ROWS, LANES), jnp.float32)
    for s in range(SLOTS):
        shift = lax.rem(QUAD * s + LANES - info[LANE0 + s], LANES)
        moved = pltpu.roll(own[info[TILE + s]], shift, 1)
        packed = jnp.where((lane >= QUAD * s) & (lane < QUAD * (s + 1)), moved, packed)
    xs, ys, weights = packed[0:CH], packed[CH : 2 * CH], packed[W_ROW : W_ROW + CH]
    back, alive = packed[BACK_ROW : BACK_ROW + 1], packed[ALIVE_ROW : ALIVE_ROW + 1]
    for child in range(LANES):
        child_b[child] = jnp.broadcast_to(packed[0 : 2 * CH, child : child + 1], (2 * CH, LANES))
    child_t[...] = jnp.transpose(jnp.broadcast_to(packed[TIME_ROW : TIME_ROW + 1], (LANES, LANES)))
    for q in range(TILES):
        times_q[q : q + 1] = prev[q, DEAD_ROW : DEAD_ROW + 1]
        times_q[TILES + q : TILES + q + 1] = own[q, DEAD_ROW : DEAD_ROW + 1]

    pos = lax.broadcasted_iota(jnp.int32, (2 * TILES, LANES), 0) * LANES
    pos = pos + lax.broadcasted_iota(jnp.int32, (2 * TILES, LANES), 1)

    def time_rows(s, carry):
        low = info[LOW + s]
        for i in range(QUAD):
            at = QUAD * s + i
            delta = jnp.maximum(child_t[pl.ds(at, 1)] - times_q[...], 0.0)
            child_pos = (TILES + info[TILE + s]) * LANES + info[LANE0 + s] + i
            ok = (pos >= low) & (pos < child_pos)
            log_t[at] = jnp.where(ok, log2_time_kernel(delta), DEAD)
        return carry

    lax.fori_loop(0, count, time_rows, 0)

    def clear(q, carry):
        total[q] = jnp.zeros((3 * CH, LANES), jnp.float32)
        return carry

    lax.fori_loop(0, 2 * TILES, clear, 0)

    half = TILES // 2

    def steps_of(s):
        start = info[LOW + s] // (2 * LANES)
        return start, half + (info[TILE + s] + 2) // 2

    def slot_sums(s, carry):
        start, end = steps_of(s)
        cx = [child_b[QUAD * s + i, 0:CH] for i in range(QUAD)]
        cy = [child_b[QUAD * s + i, CH : 2 * CH] for i in range(QUAD)]

        def tiles(ref, offset):
            def body(step, acc):
                acc = list(acc)
                for u in range(2):
                    q = 2 * step + u
                    px = ref[q - offset, 0:CH]
                    py = ref[q - offset, CH : 2 * CH]
                    for i in range(QUAD):
                        dx = px - cx[i]
                        dy = py - cy[i]
                        lt = log_t[QUAD * s + i, pl.ds(q, 1), :]
                        k = jnp.exp2((lt - dx * dx) - dy * dy)
                        kern[QUAD * s + i, q - 2 * start] = k
                        acc[3 * i] = acc[3 * i] + k
                        acc[3 * i + 1] = acc[3 * i + 1] + k * dx
                        acc[3 * i + 2] = acc[3 * i + 2] + k * dy
                return tuple(acc)

            return body

        acc = tuple(jnp.zeros((CH, LANES), jnp.float32) for _ in range(3 * QUAD))
        acc = lax.fori_loop(jnp.minimum(start, half), half, tiles(prev, 0), acc)
        acc = lax.fori_loop(jnp.maximum(start, half), end, tiles(own, TILES), acc)
        for i in range(QUAD):
            for j in range(3):
                sums[QUAD * s + i, j * CH : (j + 1) * CH] = acc[3 * i + j]
        return carry

    lax.fori_loop(0, count, slot_sums, 0)

    collected = [jnp.zeros((CH, LANES), jnp.float32) for _ in range(3)]
    for child in range(LANES):
        summed = jnp.sum(sums[child], axis=1, keepdims=True)
        for j in range(3):
            collected[j] = jnp.where(lane == child, summed[j * CH : (j + 1) * CH], collected[j])
    intensity = back + collected[0]
    ratio = weights / intensity
    spread = jnp.concatenate([ratio, ratio * xs, ratio * ys], axis=0)
    for child in range(LANES):
        ratio_b[child] = jnp.broadcast_to(spread[:, child : child + 1], (3 * CH, LANES))
    result = jnp.concatenate(
        [
            ratio * collected[1] * UNSCALE,
            ratio * collected[2] * UNSCALE,
            jnp.where(alive > 0.0, jnp.log(intensity), 0.0),
        ],
        axis=0,
    )

    def slot_push(s, carry):
        start, end = steps_of(s)
        terms = [ratio_b[QUAD * s + i] for i in range(QUAD)]

        def body(step, inner):
            for u in range(2):
                q = 2 * step + u
                ks = [kern[QUAD * s + i, q - 2 * start] for i in range(QUAD)]
                for j in range(3):
                    add = [ks[i] * terms[i][j * CH : (j + 1) * CH] for i in range(QUAD)]
                    at = slice(j * CH, (j + 1) * CH)
                    total[q, at] = total[q, at] + ((add[0] + add[1]) + (add[2] + add[3]))
            return inner

        lax.fori_loop(start, end, body, 0)
        return carry

    lax.fori_loop(0, count, slot_push, 0)

    for ref, out, offset in ((prev, part_prev, 0), (own, part_own, TILES)):

        def finish(q, carry, ref=ref, out=out, offset=offset):
            weight = total[offset + q, 0:CH]
            for j in range(2):
                at = slice(j * CH, (j + 1) * CH)
                pulled = total[offset + q, (j + 1) * CH : (j + 2) * CH]
                out[q, at] = (pulled - ref[q, at] * weight) * UNSCALE
            if out is part_own:
                out[q, 2 * CH : 3 * CH] = jnp.zeros((CH, LANES), jnp.float32)
            return carry

        lax.fori_loop(0, TILES, finish, 0)

    for s in range(SLOTS):
        tile, first = info[TILE + s], info[LANE0 + s]
        moved = pltpu.roll(result, lax.rem(first + LANES - QUAD * s, LANES), 1)
        here = (lane >= first) & (lane < jnp.where(s < count, first + QUAD, first))
        part_own[tile] = part_own[tile] + jnp.where(here, moved, 0.0)


def pairs(info, prev, own):
    f32 = jnp.float32
    vmem = pl.BlockSpec(memory_space=pltpu.VMEM)
    return pl.pallas_call(
        pair_kernel,
        out_shape=(
            jax.ShapeDtypeStruct((TILES, 2 * CH, LANES), f32),
            jax.ShapeDtypeStruct((TILES, 3 * CH, LANES), f32),
        ),
        in_specs=[pl.BlockSpec(memory_space=pltpu.SMEM)] + [vmem] * 2,
        out_specs=(vmem,) * 2,
        scratch_shapes=[
            pltpu.VMEM((LANES, 2 * TILES, LANES), f32),
            pltpu.VMEM((LANES, 2 * CH, LANES), f32),
            pltpu.VMEM((LANES, TILES + 4, CH, LANES), f32),
            pltpu.VMEM((LANES, 3 * CH, LANES), f32),
            pltpu.VMEM((LANES, 3 * CH, LANES), f32),
            pltpu.VMEM((2 * TILES, 3 * CH, LANES), f32),
            pltpu.VMEM((2 * TILES, LANES), f32),
            pltpu.VMEM((LANES, LANES), f32),
        ],
        compiler_params=pltpu.CompilerParams(vmem_limit_bytes=58 * 2**20),
    )(info, prev, own)


def plan(meta, me, no_prev):
    live = meta[:, 0].astype(jnp.int32)
    window = meta[:, 1:3].astype(jnp.int32).reshape(-1)
    blocks = 2 * TILES
    block = jnp.arange(blocks, dtype=jnp.int32)
    low = jnp.maximum(window * BLK, jnp.where(no_prev, TILES * LANES, 0))
    quads = jnp.clip((jnp.repeat(live, 2) - BLK * (block % 2) + QUAD - 1) // QUAD, 0, BLK // QUAD)
    cost = block * BLK - low
    order = (cost[:, None] > cost[None, :]) | ((cost[:, None] == cost[None, :]) & (block[:, None] < block[None, :]))
    before = jnp.sum(jnp.where(order, quads[:, None], 0), axis=0)
    rounds = jnp.arange(SLOTS, dtype=jnp.int32)
    number = rounds * TILES + (me + TILES // 2 * (rounds % 2)) % TILES
    mine = (before[None, :] <= number[:, None]) & (number[:, None] < (before + quads)[None, :])

    def pick(value):
        return jnp.sum(jnp.where(mine, value, 0), axis=1)

    count = jnp.sum((number < jnp.sum(quads)).astype(jnp.int32))
    which = pick(block[None, :])
    first = (which % 2) * BLK + QUAD * pick(number[:, None] - before[None, :])
    return jnp.concatenate([count[None], which // 2, first, pick(low[None, :])])


def per_device(locations, times, background, weights, window_start, live):
    slot_ids = jnp.arange(LANES, dtype=jnp.int32)
    alive = slot_ids < live[0]
    alive_mask = alive.astype(jnp.float32)
    meta = jnp.pad(jnp.concatenate([live, window_start]).astype(jnp.float32), (0, LANES - 3))
    chunk = jnp.concatenate(
        [
            locations[:, 0, :] * SCALE,
            locations[:, 1, :] * SCALE,
            jnp.stack([jnp.where(alive, times, DEAD), times, background, alive_mask, meta]),
            jnp.zeros((W_ROW - META_ROW - 1, LANES), jnp.float32),
            weights * alive_mask,
        ]
    )
    own = lax.all_to_all(jnp.broadcast_to(chunk[None], (TILES, ROWS, LANES)), "grp", 0, 0)
    prev = from_behind(own[:, 0:W_ROW], "tm", 1)
    info = plan(own[:, META_ROW, 0:3], lax.axis_index("grp").astype(jnp.int32), lax.axis_index("tm") == 0)
    part_prev, part_own = pairs(info, prev, own)
    back = from_behind(part_prev, "tm", -1)
    part = jnp.concatenate([part_own[:, 0 : 2 * CH] + back, part_own[:, 2 * CH :]], axis=1)
    result = jnp.sum(lax.all_to_all(part, "grp", 0, 0), axis=0)
    grad = result[0 : 2 * CH].reshape(2, CH, LANES).transpose(1, 0, 2)
    return (grad, result[2 * CH :])


def solution(mesh):
    return jax.shard_map(
        per_device,
        mesh=mesh,
        in_specs=(
            P(None, None, ("tm", "grp")),
            P(("tm", "grp")),
            P(("tm", "grp")),
            P(None, ("tm", "grp")),
            P(("tm", "grp")),
            P(("tm", "grp")),
        ),
        out_specs=(P(None, None, ("tm", "grp")), P(None, ("tm", "grp"))),
        check_vma=False,
    )
```

time: 117 us -> 124 us (1.060)
  the two profiles are of different devices: /device:TPU:25 before, /device:TPU:27 now
where the time goes in v2:
time: 124 us; the launch traced here: 123 us
  waiting for transfers between devices  37.5 us (30%)
  blocking collectives  27.1 us (22%)
  starting transfers between devices  23.8 us (19%)
  Pallas kernels  21.8 us (18%)
  local copies, waits for them, and re-layouts  6.7 us (5%)
  other arithmetic  4.96 us (4%)
  between operations  1.46 us (1%)
    all_to_all x1, blocking collectives, per_device(): result = jnp.sum(lax.all_to_all(part, 'grp', 0, 0), axis=0)  27.1 us
    all_to_all x1, waiting for transfers between devices, per_device(): lax.all_to_all(jnp.broadcast_to(chunk[None], (TILES, ROWS, LANES)), 'grp'...  23.9 us
    pallas_call x1, Pallas kernels, pairs(): pl.pallas_call(pair_kernel, out_shape=(jax.ShapeDtypeStruct((TILES, 2 * C...  21.8 us
    ppermute x2, waiting for transfers between devices, from_behind(): return lax.ppermute(value, axis, pairs)  13.7 us
    all_to_all x1, starting transfers between devices, per_device(): lax.all_to_all(jnp.broadcast_to(chunk[None], (TILES, ROWS, LANES)), 'grp'...  12.9 us
    ppermute x2, starting transfers between devices, from_behind(): return lax.ppermute(value, axis, pairs)  10.9 us
  transfers between devices with their start and end apart: 3, of which 3 were waited for; matrix products, arithmetic and copies ran while one was open for 2% of the time, Pallas kernels for 0%

profile of v2, /device:TPU:27, one launch (start us, length us, event | category | flops | bytes accessed | tf_op | source)
XLA Modules:
  0.0 123.3 jit_solution(10367171497379703241)
XLA Ops:
  1.3 0.1 add_convert_fusion
  1.4 0.0 copy-start.2
  1.4 0.8 fusion.17
  2.3 0.0 copy-start.3
  2.3 0.6 copy-done.3
  2.9 0.7 copy-done.4
  3.6 1.0 broadcast_in_dim.69
  4.6 12.9 %all-to-all-start = ((f32[32,56,128]{2,1,0:T(8,128)}), f32[32,56,128]{2,1,0:T(8,128)S(1)}, u32[]{:S(2)}, u32[]{:S(2)}) async-start(f32[32,56,128]{2,1,0:T(8,128)} %broadcast_in_dim.69), calls=%async_computation | async-start | bytes 1835008 | tf_op jit(solution)/shard_map/all_to_all | solution.py:247
  17.5 23.9 %all-to-all-done.own = f32[32,56,128]{2,1,0:T(8,128)S(1)} async-done(((f32[32,56,128]{2,1,0:T(8,128)}), f32[32,56,128]{2,1,0:T(8,128)S(1)}, u32[]{:S(2)}, u32[]{:S(2)}) %all-to-all-start) | async-done | bytes 917536 | tf_op jit(solution)/shard_map/all_to_all | solution.py:247
  41.4 0.1 copy.22
  41.5 0.7 clamp_reduce_fusion
  42.2 1.3 %fusion.10 = s32[]{:T(128)} fusion(s32[]{:T(128)} %clamp_reduce_fusion, s32[]{:T(128)S(6)} %axis_index.22), kind=kLoop, calls=%fused_computation.49 | loop fusion | flops 767 | bytes 12 | tf_op jit(solution)/shard_map/reduce_sum | solution.py:227
  43.5 0.1 copy.23
  43.6 0.1 max.31
  43.7 0.1 broadcast_in_dim.70.clone
  43.8 0.1 reshape.151
  44.0 6.9 %collective-permute-start = (f32[32,40,128]{2,1,0:T(8,128)S(1)}, f32[32,40,128]{2,1,0:T(8,128)S(1)}, u32[]{:S(2)}, u32[]{:S(2)}) collective-permute-start(f32[32,40,128]{2,1,0:T(8,128)S(1)} %slice.41), channel_id=1, source_target_pairs={{0,32},{32,64},{64,96},{96,128},{128,160},{160,192},{192,224},{224... | collective-permute-start | bytes 1966088 | tf_op jit(solution)/shard_map/ppermute | solution.py:36
  50.9 0.1 select_reduce_fusion
  51.0 0.2 select_reduce_fusion.3
  51.2 1.2 %pad_add_fusion.info = s32[97]{0:T(128)} fusion(s32[32]{0:T(128)S(1)} %get-tuple-element.7, s32[32]{0:T(128)S(1)} %get-tuple-element.12, s32[32]{0:T(128)S(1)} %get-tuple-element.11, s32[1]{0:T(128)} %bitcast.9), kind=kLoop, calls=%fused_computation.56 | loop fusion | flops 291 | bytes 776 | tf_op jit(solution)/shard_map/concatenate | solution.py:230
  52.5 5.9 %collective-permute-done.prev = f32[32,40,128]{2,1,0:T(8,128)S(1)} collective-permute-done((f32[32,40,128]{2,1,0:T(8,128)S(1)}, f32[32,40,128]{2,1,0:T(8,128)S(1)}, u32[]{:S(2)}, u32[]{:S(2)}) %collective-permute-start) | collective-permute-done | bytes 655392 | tf_op jit(solution)/shard_map/ppermute | solution.py:36
  58.4 0.8 copy-done.1
  59.2 21.8 %shard_map.77 = (f32[32,32,128]{2,1,0:T(8,128)}, f32[32,48,128]{2,1,0:T(8,128)}) custom-call(s32[97]{0:T(128)} %pad_add_fusion.info, f32[32,40,128]{2,1,0:T(8,128)} %copy-done.1, f32[32,56,128]{2,1,0:T(8,128)} %copy-done), custom_call_target="tpu_custom_call" | custom-call | tf_op jit(solution)/shard_map/pallas_call | solution.py:188
  81.0 4.0 %collective-permute-start.1 = (f32[32,32,128]{2,1,0:T(8,128)}, f32[32,32,128]{2,1,0:T(8,128)S(1)}, u32[]{:S(2)}, u32[]{:S(2)}) collective-permute-start(f32[32,32,128]{2,1,0:T(8,128)} %get-tuple-element.5), channel_id=1, source_target_pairs={{32,0},{64,32},{96,64},{128,96},{160,128},{192,160},{224,192},{256... | collective-permute-start | bytes 1572872 | tf_op jit(solution)/shard_map/ppermute | solution.py:36
  85.0 1.0 slice.37
  86.0 7.7 %collective-permute-done.1 = f32[32,32,128]{2,1,0:T(8,128)S(1)} collective-permute-done((f32[32,32,128]{2,1,0:T(8,128)}, f32[32,32,128]{2,1,0:T(8,128)S(1)}, u32[]{:S(2)}, u32[]{:S(2)}) %collective-permute-start.1) | collective-permute-done | bytes 524320 | tf_op jit(solution)/shard_map/ppermute | solution.py:36
  93.8 1.1 slice_add_fusion
  94.9 0.1 pad_maximum_fusion
  94.9 27.1 %all_to_all.10 = f32[32,48,128]{2,1,0:T(8,128)S(1)} all-to-all(f32[32,48,128]{2,1,0:T(8,128)S(1)} %pad_maximum_fusion), channel_id=1, replica_groups=mesh['tm'=16,'grp'=32] {'grp'}, dimensions={0} | all-to-all | bytes 1572864 | tf_op jit(solution)/shard_map/all_to_all | solution.py:253
  122.0 0.1 reduce_sum.69
  122.1 0.6 slice.43
  122.7 0.6 copy.29
  (24 shorter events, 0.2 us)
Async XLA Ops:
  0.6 0.7 copy-start.5
  1.4 0.8 copy-start.2
  2.3 0.7 copy-start.3
  2.9 0.7 copy-start.4
  4.6 36.8 %all-to-all-start = ((f32[32,56,128]{2,1,0:T(8,128)}), f32[32,56,128]{2,1,0:T(8,128)S(1)}, u32[]{:S(2)}, u32[]{:S(2)}) async-start(f32[32,56,128]{2,1,0:T(8,128)} %broadcast_in_dim.69), calls=%async_computation | async-start | bytes 1835008 | tf_op jit(solution)/shard_map/all_to_all | solution.py:247
  41.4 17.0 %copy-start = (f32[32,56,128]{2,1,0:T(8,128)}, f32[32,56,128]{2,1,0:T(8,128)S(1)}, u32[]{:S(2)}) copy-start(f32[32,56,128]{2,1,0:T(8,128)S(1)} %all-to-all-done.own) | copy-start | bytes 2752516
  44.0 14.4 %collective-permute-start = (f32[32,40,128]{2,1,0:T(8,128)S(1)}, f32[32,40,128]{2,1,0:T(8,128)S(1)}, u32[]{:S(2)}, u32[]{:S(2)}) collective-permute-start(f32[32,40,128]{2,1,0:T(8,128)S(1)} %slice.41), channel_id=1, source_target_pairs={{0,32},{32,64},{64,96},{96,128},{128,160},{160,192},{192,224},{224... | collective-permute-start | bytes 1966088 | tf_op jit(solution)/shard_map/ppermute | solution.py:36
  58.4 0.9 copy-start.1
  81.0 12.8 %collective-permute-start.1 = (f32[32,32,128]{2,1,0:T(8,128)}, f32[32,32,128]{2,1,0:T(8,128)S(1)}, u32[]{:S(2)}, u32[]{:S(2)}) collective-permute-start(f32[32,32,128]{2,1,0:T(8,128)} %get-tuple-element.5), channel_id=1, source_target_pairs={{32,0},{64,32},{96,64},{128,96},{160,128},{192,160},{224,192},{256... | collective-permute-start | bytes 1572872 | tf_op jit(solution)/shard_map/ppermute | solution.py:36

commit v3 on v0

v3 whole, which is shorter than its diff:
```python
import math

import jax
import jax.numpy as jnp
from jax import lax
from jax.experimental import pallas as pl
from jax.experimental.pallas import tpu as pltpu
from jax.sharding import PartitionSpec as P

offspring = 0.8
fast_rate = 0.125
slow_rate = 0.0009765625

CH = 16
LANES = 128
TILES = 32
BLK = 64
QUAD = 4
SLOTS = 32
DEAD = -1e30

HALF = TILES // 2

TIME_ROW, BACK_ROW, META_ROW = range(2 * CH, 2 * CH + 3)
W_ROW = 40
ROWS = W_ROW + CH
COUNT, FIRST, LOW = range(3)

SCALE = math.sqrt(0.5 / math.log(2.0))
UNSCALE = 1.0 / SCALE
LOG2E = 1.0 / math.log(2.0)
LOG2_SLOW = math.log2(offspring * 0.5 * slow_rate / (2.0 * math.pi))


def from_behind(value, axis, by):
    count = lax.axis_size(axis)
    pairs = [(i, i + by) for i in range(count) if 0 <= i + by < count]
    return lax.ppermute(value, axis, pairs)


def log2_time_kernel(delta):
    fast = (fast_rate / slow_rate) * jnp.exp2(delta * (-(fast_rate - slow_rate) * LOG2E))
    return (LOG2_SLOW - delta * (slow_rate * LOG2E)) + jnp.log(1.0 + fast) * LOG2E


def slot_lanes(lane, s):
    return (lane >= QUAD * s) & (lane < QUAD * (s + 1))


def lane_ids():
    return lax.broadcasted_iota(jnp.int32, (1, LANES), 1)


def spread_lanes(out, values):
    rows = values.shape[0]
    for child in range(LANES):
        out[child] = jnp.broadcast_to(values[:, child : child + 1], (rows, LANES))


def gather_lanes(sums):
    lane = lane_ids()
    collected = jnp.zeros(sums.shape[1:], jnp.float32)
    for child in range(LANES):
        collected = jnp.where(lane == child, jnp.sum(sums[child], axis=1, keepdims=True), collected)
    return collected


def set_times(out, packed, times_q, tiles):
    out[...] = jnp.transpose(jnp.broadcast_to(packed[TIME_ROW : TIME_ROW + 1], (LANES, LANES)))
    for q in range(TILES):
        times_q[q : q + 1] = tiles[q, TIME_ROW : TIME_ROW + 1]


def time_rows(info, s, log_t, child_t, times_q, offset):
    pos = lax.broadcasted_iota(jnp.int32, (TILES, LANES), 0) * LANES + offset
    pos = pos + lax.broadcasted_iota(jnp.int32, (TILES, LANES), 1)
    low = info[LOW, s]
    for i in range(QUAD):
        at = QUAD * s + i
        delta = jnp.maximum(child_t[pl.ds(at, 1)] - times_q[...], 0.0)
        ok = (pos >= low) & (pos < info[FIRST, s] + i)
        log_t[at] = jnp.where(ok, log2_time_kernel(delta), DEAD)


def kernel_of(tiles, q, child_b, log_t, at):
    dx = tiles[q, 0:CH] - child_b[at, 0:CH]
    dy = tiles[q, CH : 2 * CH] - child_b[at, CH : 2 * CH]
    lt = log_t[at, pl.ds(q, 1), :]
    return jnp.exp2((lt - dx * dx) - dy * dy), dx, dy


def slot_sums(tiles, s, start, end, child_b, log_t, sums, kern=None):
    for i in range(QUAD):
        sums[QUAD * s + i] = jnp.zeros((3 * CH, LANES), jnp.float32)

    def body(step, carry):
        for i in range(QUAD):
            at = QUAD * s + i
            k0, dx0, dy0 = kernel_of(tiles, 2 * step, child_b, log_t, at)
            k1, dx1, dy1 = kernel_of(tiles, 2 * step + 1, child_b, log_t, at)
            if kern is not None:
                kern[at, 2 * step] = k0
                kern[at, 2 * step + 1] = k1
            sums[at, 0:CH] = (sums[at, 0:CH] + k0) + k1
            sums[at, CH : 2 * CH] = (sums[at, CH : 2 * CH] + k0 * dx0) + k1 * dx1
            sums[at, 2 * CH :] = (sums[at, 2 * CH :] + k0 * dy0) + k1 * dy1
        return carry

    lax.fori_loop(start, end, body, 0)


def own_steps(info, s):
    return jnp.maximum(info[LOW, s] // (2 * LANES) - HALF, 0), info[FIRST, s] // (2 * LANES) - HALF + 1


def prev_start(info, s):
    return jnp.minimum(info[LOW, s] // (2 * LANES), HALF)


def own_sums_kernel(info, own, packed, collected, log_t, child_b, sums, times_q, child_t):
    count = info[COUNT, 0]
    lane = lane_ids()
    mine = jnp.zeros((ROWS, LANES), jnp.float32)
    for s in range(SLOTS):
        first = info[FIRST, s]
        moved = pltpu.roll(own[first // LANES - TILES], lax.rem(QUAD * s + LANES - lax.rem(first, LANES), LANES), 1)
        mine = jnp.where(slot_lanes(lane, s), moved, mine)
    packed[...] = mine
    spread_lanes(child_b, mine[0 : 2 * CH])
    set_times(child_t, mine, times_q, own)

    def times(s, carry):
        time_rows(info, s, log_t, child_t, times_q, TILES * LANES)
        return carry

    lax.fori_loop(0, count, times, 0)

    def slot(s, carry):
        start, end = own_steps(info, s)
        slot_sums(own, s, start, end, child_b, log_t, sums)
        return carry

    lax.fori_loop(0, count, slot, 0)
    collected[...] = gather_lanes(sums)


def prev_kernel(
    info, prev, packed, own_sums, part, result, ratio_out,
    log_t, child_b, kern, sums, total, times_q, child_t
):
    count = info[COUNT, 0]
    spread_lanes(child_b, packed[0 : 2 * CH])
    set_times(child_t, packed, times_q, prev)

    def times(s, carry):
        @pl.when(info[LOW, s] < TILES * LANES)
        def _():
            time_rows(info, s, log_t, child_t, times_q, 0)

        return carry

    lax.fori_loop(0, count, times, 0)

    def slot(s, carry):
        slot_sums(prev, s, prev_start(info, s), HALF, child_b, log_t, sums, kern)
        return carry

    lax.fori_loop(0, count, slot, 0)

    collected = own_sums[...] + gather_lanes(sums)
    xs, ys, weights = packed[0:CH], packed[CH : 2 * CH], packed[W_ROW : W_ROW + CH]
    intensity = packed[BACK_ROW : BACK_ROW + 1] + collected[0:CH]
    alive = packed[TIME_ROW : TIME_ROW + 1] >= 0.0
    ratio = weights / intensity
    ratio_out[...] = ratio
    result[0:CH] = ratio * collected[CH : 2 * CH] * UNSCALE
    result[CH : 2 * CH] = ratio * collected[2 * CH :] * UNSCALE
    result[2 * CH :] = jnp.where(alive, jnp.log(intensity), 0.0)
    spread_lanes(sums, jnp.concatenate([ratio, ratio * xs, ratio * ys], axis=0))

    def clear(q, carry):
        total[q] = jnp.zeros((3 * CH, LANES), jnp.float32)
        return carry

    lax.fori_loop(0, TILES, clear, 0)

    def push(s, carry):
        def body(step, inner):
            for u in range(2):
                q = 2 * step + u
                ks = [kern[QUAD * s + i, q] for i in range(QUAD)]
                for j in range(3):
                    at = slice(j * CH, (j + 1) * CH)
                    add = [ks[i] * sums[QUAD * s + i, at] for i in range(QUAD)]
                    total[q, at] = total[q, at] + ((add[0] + add[1]) + (add[2] + add[3]))
            return inner

        lax.fori_loop(prev_start(info, s), HALF, body, 0)
        return carry

    lax.fori_loop(0, count, push, 0)

    def finish(q, carry):
        weight = total[q, 0:CH]
        for j in range(2):
            at = slice(j * CH, (j + 1) * CH)
            part[q, at] = (total[q, (j + 1) * CH : (j + 2) * CH] - prev[q, at] * weight) * UNSCALE
        return carry

    lax.fori_loop(0, TILES, finish, 0)


def own_push_kernel(info, own, packed, result, ratio, part, log_t, child_b, ratio_b, times_q, child_t):
    count = info[COUNT, 0]
    lane = lane_ids()
    spread_lanes(child_b, packed[0 : 2 * CH])
    spread_lanes(ratio_b, ratio[...] * -UNSCALE)
    set_times(child_t, packed, times_q, own)

    def times(s, carry):
        time_rows(info, s, log_t, child_t, times_q, TILES * LANES)
        return carry

    lax.fori_loop(0, count, times, 0)

    def clear(q, carry):
        part[q] = jnp.zeros((3 * CH, LANES), jnp.float32)
        return carry

    lax.fori_loop(0, TILES, clear, 0)

    def slot(s, carry):
        start, end = own_steps(info, s)

        def body(step, inner):
            for u in range(2):
                q = 2 * step + u
                xs, ys = [], []
                for i in range(QUAD):
                    k, dx, dy = kernel_of(own, q, child_b, log_t, QUAD * s + i)
                    weighted = k * ratio_b[QUAD * s + i]
                    xs.append(weighted * dx)
                    ys.append(weighted * dy)
                part[q, 0:CH] = part[q, 0:CH] + ((xs[0] + xs[1]) + (xs[2] + xs[3]))
                part[q, CH : 2 * CH] = part[q, CH : 2 * CH] + ((ys[0] + ys[1]) + (ys[2] + ys[3]))
            return inner

        lax.fori_loop(start, end, body, 0)
        return carry

    lax.fori_loop(0, count, slot, 0)

    for s in range(SLOTS):
        first = info[FIRST, s]
        tile, at = first // LANES - TILES, lax.rem(first, LANES)
        moved = pltpu.roll(result[...], lax.rem(at + LANES - QUAD * s, LANES), 1)
        here = (lane >= at) & (lane < jnp.where(s < count, at + QUAD, at))
        part[tile] = part[tile] + jnp.where(here, moved, 0.0)


def call(kernel, out_rows, scratch, *operands):
    vmem = pl.BlockSpec(memory_space=pltpu.VMEM)
    return pl.pallas_call(
        kernel,
        out_shape=[jax.ShapeDtypeStruct(shape, jnp.float32) for shape in out_rows],
        in_specs=[pl.BlockSpec(memory_space=pltpu.SMEM)] + [vmem] * (len(operands) - 1),
        out_specs=[vmem] * len(out_rows),
        scratch_shapes=[pltpu.VMEM(shape, jnp.float32) for shape in scratch],
        compiler_params=pltpu.CompilerParams(vmem_limit_bytes=50 * 2**20),
    )(*operands)


TIMES = [(TILES, LANES), (LANES, LANES)]
LOG_T = (LANES, TILES, LANES)
CHILD_B = (LANES, 2 * CH, LANES)
SUMS = (LANES, 3 * CH, LANES)


def own_sums(info, own):
    return call(own_sums_kernel, [(ROWS, LANES), (3 * CH, LANES)], [LOG_T, CHILD_B, SUMS] + TIMES, info, own)


def prev_pairs(info, prev, packed, collected):
    return call(
        prev_kernel,
        [(TILES, 2 * CH, LANES), (3 * CH, LANES), (CH, LANES)],
        [LOG_T, CHILD_B, (LANES, TILES, CH, LANES), SUMS, (TILES, 3 * CH, LANES)] + TIMES,
        info, prev, packed, collected,
    )


def own_push(info, own, packed, result, ratio):
    return call(
        own_push_kernel,
        [(TILES, 3 * CH, LANES)],
        [LOG_T, CHILD_B, (LANES, CH, LANES)] + TIMES,
        info, own, packed, result, ratio,
    )[0]


def plan(meta, me, no_prev):
    blocks = 2 * TILES
    block = jnp.arange(blocks, dtype=jnp.int32)
    rounds = jnp.arange(SLOTS, dtype=jnp.int32)
    live = jnp.repeat(meta[:, 0], 2).astype(jnp.int32)
    window = meta[:, 1:3].reshape(-1).astype(jnp.int32)
    low = jnp.maximum(window * BLK, jnp.where(no_prev, TILES * LANES, 0))
    quads = jnp.clip((live - BLK * (block % 2) + QUAD - 1) // QUAD, 0, BLK // QUAD)
    key = (low - block * BLK) * blocks + block
    before = jnp.sum(jnp.where(key[:, None] < key[None, :], quads[:, None], 0), axis=0)
    number = rounds * TILES + (me + TILES // 2 * (rounds % 2)) % TILES
    offset = number[:, None] - before[None, :]
    mine = (offset >= 0) & (offset < quads[None, :])
    first = TILES * LANES + block[None, :] * BLK + QUAD * offset
    values = jnp.stack([jnp.ones_like(first), first, jnp.broadcast_to(low[None, :], first.shape)])
    info = jnp.sum(jnp.where(mine[None], values, 0), axis=2)
    count = jnp.sum(info[0])
    return jnp.stack([jnp.full((SLOTS,), count), jnp.maximum(info[1], TILES * LANES), info[2]])


def per_device(locations, times, background, weights, window_start, live):
    slot_ids = jnp.arange(LANES, dtype=jnp.int32)
    alive = slot_ids < live[0]
    meta = jnp.pad(jnp.concatenate([live, window_start]).astype(jnp.float32), (0, LANES - 3))
    chunk = jnp.concatenate(
        [
            locations[:, 0, :] * SCALE,
            locations[:, 1, :] * SCALE,
            jnp.stack([jnp.where(alive, times, DEAD), background, meta]),
            jnp.zeros((W_ROW - META_ROW - 1, LANES), jnp.float32),
            jnp.where(alive, weights, 0.0),
        ]
    )
    own = lax.all_to_all(jnp.broadcast_to(chunk[None], (TILES, ROWS, LANES)), "grp", 0, 0)
    prev = from_behind(own[:, 0:W_ROW], "tm", 1)
    info = plan(own[:, META_ROW, 0:3], lax.axis_index("grp").astype(jnp.int32), lax.axis_index("tm") == 0)
    packed, collected = own_sums(info, own)
    part_prev, result, ratio = prev_pairs(info, prev, packed, collected)
    back = from_behind(part_prev, "tm", -1)
    part_own = own_push(info, own, packed, result, ratio)
    part = jnp.concatenate([part_own[:, 0 : 2 * CH] + back, part_own[:, 2 * CH :]], axis=1)
    total = jnp.sum(lax.all_to_all(part, "grp", 0, 0), axis=0)
    grad = total[0 : 2 * CH].reshape(2, CH, LANES).transpose(1, 0, 2)
    return (grad, total[2 * CH :])


def solution(mesh):
    return jax.shard_map(
        per_device,
        mesh=mesh,
        in_specs=(
            P(None, None, ("tm", "grp")),
            P(("tm", "grp")),
            P(("tm", "grp")),
            P(None, ("tm", "grp")),
            P(("tm", "grp")),
            P(("tm", "grp")),
        ),
        out_specs=(P(None, None, ("tm", "grp")), P(None, ("tm", "grp"))),
        check_vma=False,
    )
```

time: 601 us -> 111 us (0.18)
  the two profiles are of different devices: /device:TPU:25 before, /device:TPU:26 now
where the time goes in v3:
time: 111 us; the launch traced here: 110 us
  blocking collectives  29.5 us (27%)
  Pallas kernels  28 us (25%)
  waiting for transfers between devices  25.2 us (23%)
  starting transfers between devices  19.2 us (17%)
  local copies, waits for them, and re-layouts  5.53 us (5%)
  other arithmetic  1.52 us (1%)
  between operations  1.49 us (1%)
    all_to_all x1, blocking collectives, per_device(): total = jnp.sum(lax.all_to_all(part, 'grp', 0, 0), axis=0)  29.5 us
    pallas_call x3, Pallas kernels, call(): pl.pallas_call(kernel, out_shape=[jax.ShapeDtypeStruct(shape, jnp.float32...  28 us
    all_to_all x1, waiting for transfers between devices, per_device(): lax.all_to_all(jnp.broadcast_to(chunk[None], (TILES, ROWS, LANES)), 'grp'...  25.2 us
    all_to_all x1, starting transfers between devices, per_device(): lax.all_to_all(jnp.broadcast_to(chunk[None], (TILES, ROWS, LANES)), 'grp'...  13.5 us
    ppermute x2, starting transfers between devices, from_behind(): return lax.ppermute(value, axis, pairs)  5.7 us
  transfers between devices with their start and end apart: 3, of which 1 were waited for; matrix products, arithmetic and copies ran while one was open for 2% of the time, Pallas kernels for 16%

profile of v3, /device:TPU:26, one launch (start us, length us, event | category | flops | bytes accessed | tf_op | source)
XLA Modules:
  0.0 110.5 jit_solution(12007265666193930021)
XLA Ops:
  1.3 0.1 add_convert_fusion
  1.4 0.8 fusion.10
  2.2 0.0 copy-start.2
  2.3 0.6 copy-done.2
  2.9 0.7 copy-done.1
  3.6 1.0 broadcast_in_dim.61
  4.6 13.5 %all-to-all-start = ((f32[32,56,128]{2,1,0:T(8,128)}), f32[32,56,128]{2,1,0:T(8,128)S(1)}, u32[]{:S(2)}, u32[]{:S(2)}) async-start(f32[32,56,128]{2,1,0:T(8,128)} %broadcast_in_dim.61), calls=%async_computation | async-start | bytes 1835008 | tf_op jit(solution)/shard_map/all_to_all | solution.py:334
  18.1 25.2 %all-to-all-done.own = f32[32,56,128]{2,1,0:T(8,128)S(1)} async-done(((f32[32,56,128]{2,1,0:T(8,128)}), f32[32,56,128]{2,1,0:T(8,128)S(1)}, u32[]{:S(2)}, u32[]{:S(2)}) %all-to-all-start) | async-done | bytes 917536 | tf_op jit(solution)/shard_map/all_to_all | solution.py:334
  43.3 0.1 copy.20
  43.4 0.1 copy.21
  43.5 0.1 max.32
  43.6 0.1 broadcast_in_dim.62
  43.7 0.1 convert_element_type.39
  43.9 1.9 %collective-permute-start = (f32[32,40,128]{2,1,0:T(8,128)S(1)}, f32[32,40,128]{2,1,0:T(8,128)S(1)}, u32[]{:S(2)}, u32[]{:S(2)}) collective-permute-start(f32[32,40,128]{2,1,0:T(8,128)S(1)} %slice.53), channel_id=1, source_target_pairs={{0,32},{32,64},{64,96},{96,128},{128,160},{160,192},{192,224},{224... | collective-permute-start | bytes 1966088 | tf_op jit(solution)/shard_map/ppermute | solution.py:38
  45.8 0.1 select_reduce_fusion
  45.9 0.1 multiply_add_fusion
  46.0 0.1 fusion.1
  46.1 0.2 fusion
  46.3 0.6 slice_reduce_fusion
  46.9 0.6 pad.7.clone
  47.6 0.1 pad_add_fusion.info
  47.6 8.8 %shard_map.77 = (f32[56,128]{1,0:T(8,128)S(1)}, f32[48,128]{1,0:T(8,128)S(1)}) custom-call(s32[3,32]{1,0:T(4,128)S(1)} %pad_add_fusion.info, f32[32,56,128]{2,1,0:T(8,128)S(1)} %all-to-all-done.own), custom_call_target="tpu_custom_call" | custom-call | tf_op jit(solution)/shard_map/pallas_call | solution.py:263
  56.4 10.3 %shard_map.78 = (f32[32,32,128]{2,1,0:T(8,128)S(1)}, f32[48,128]{1,0:T(8,128)S(1)}, f32[16,128]{1,0:T(8,128)S(1)}) custom-call(s32[3,32]{1,0:T(4,128)S(1)} %pad_add_fusion.info, f32[32,40,128]{2,1,0:T(8,128)S(1)} %collective-permute-done.prev, f32[56,128]{1,0:T(8,128)S(1)} %get-tuple-element.7.packed, f32[48,128]{1,0:T(8,128)S(1)} %get-tuple-element.8.own_sums), custom_call_target="tpu_custom_call" | custom-call | tf_op jit(solution)/shard_map/pallas_call | solution.py:263
  66.7 3.8 %collective-permute-start.1 = (f32[32,32,128]{2,1,0:T(8,128)S(1)}, f32[32,32,128]{2,1,0:T(8,128)S(1)}, u32[]{:S(2)}, u32[]{:S(2)}) collective-permute-start(f32[32,32,128]{2,1,0:T(8,128)S(1)} %get-tuple-element.11), channel_id=1, source_target_pairs={{32,0},{64,32},{96,64},{128,96},{160,128},{192,160},{224,192},{256... | collective-permute-start | bytes 1572872 | tf_op jit(solution)/shard_map/ppermute | solution.py:38
  70.5 9.0 %shard_map.79 = f32[32,48,128]{2,1,0:T(8,128)S(1)} custom-call(s32[3,32]{1,0:T(4,128)S(1)} %pad_add_fusion.info, f32[32,56,128]{2,1,0:T(8,128)S(1)} %all-to-all-done.own, f32[56,128]{1,0:T(8,128)S(1)} %get-tuple-element.7.packed, f32[48,128]{1,0:T(8,128)S(1)} %get-tuple-element.9.result, f32[16,128]{1,0:T(8,128)S(1)} %get-tuple-element.10.ratio), custom_call_target="tpu_custom_call" | custom-call | tf_op jit(solution)/shard_map/pallas_call | solution.py:263
  79.5 0.0 collective-permute-done.1
  79.5 0.1 slice_add_fusion
  79.6 0.1 pad_maximum_fusion
  79.7 29.5 %all_to_all.10 = f32[32,48,128]{2,1,0:T(8,128)S(1)} all-to-all(f32[32,48,128]{2,1,0:T(8,128)S(1)} %pad_maximum_fusion), channel_id=1, replica_groups=mesh['tm'=16,'grp'=32] {'grp'}, dimensions={0} | all-to-all | bytes 1572864 | tf_op jit(solution)/shard_map/all_to_all | solution.py:342
  109.2 0.1 reduce_sum.39
  109.3 0.6 slice.57
  109.9 0.6 copy.26
  (24 shorter events, 0.2 us)
Async XLA Ops:
  0.6 0.7 copy-start.3
  1.4 0.8 copy-start
  2.2 0.7 copy-start.2
  2.9 0.7 copy-start.1
  4.6 38.7 %all-to-all-start = ((f32[32,56,128]{2,1,0:T(8,128)}), f32[32,56,128]{2,1,0:T(8,128)S(1)}, u32[]{:S(2)}, u32[]{:S(2)}) async-start(f32[32,56,128]{2,1,0:T(8,128)} %broadcast_in_dim.61), calls=%async_computation | async-start | bytes 1835008 | tf_op jit(solution)/shard_map/all_to_all | solution.py:334
  43.9 12.6 %collective-permute-start = (f32[32,40,128]{2,1,0:T(8,128)S(1)}, f32[32,40,128]{2,1,0:T(8,128)S(1)}, u32[]{:S(2)}, u32[]{:S(2)}) collective-permute-start(f32[32,40,128]{2,1,0:T(8,128)S(1)} %slice.53), channel_id=1, source_target_pairs={{0,32},{32,64},{64,96},{96,128},{128,160},{160,192},{192,224},{224... | collective-permute-start | bytes 1966088 | tf_op jit(solution)/shard_map/ppermute | solution.py:38
  66.7 12.8 %collective-permute-start.1 = (f32[32,32,128]{2,1,0:T(8,128)S(1)}, f32[32,32,128]{2,1,0:T(8,128)S(1)}, u32[]{:S(2)}, u32[]{:S(2)}) collective-permute-start(f32[32,32,128]{2,1,0:T(8,128)S(1)} %get-tuple-element.11), channel_id=1, source_target_pairs={{32,0},{64,32},{96,64},{128,96},{160,128},{192,160},{224,192},{256... | collective-permute-start | bytes 1572872 | tf_op jit(solution)/shard_map/ppermute | solution.py:38

commit v4 on v3

--- a/solution.py
+++ b/solution.py
@@ -24,7 +24,7 @@
 TIME_ROW, BACK_ROW, META_ROW = range(2 * CH, 2 * CH + 3)
 W_ROW = 40
 ROWS = W_ROW + CH
-COUNT, FIRST, LOW = range(3)
+VALID, FIRST, LOW = range(3)
 
 SCALE = math.sqrt(0.5 / math.log(2.0))
 UNSCALE = 1.0 / SCALE
@@ -62,24 +62,34 @@
     collected = jnp.zeros(sums.shape[1:], jnp.float32)
     for child in range(LANES):
         collected = jnp.where(lane == child, jnp.sum(sums[child], axis=1, keepdims=True), collected)
-    return collected
-
-
-def set_times(out, packed, times_q, tiles):
-    out[...] = jnp.transpose(jnp.broadcast_to(packed[TIME_ROW : TIME_ROW + 1], (LANES, LANES)))
+    return [collected[j * CH : (j + 1) * CH] for j in range(3)]
+
+
+def slots_of(info):
+    count = info[VALID, 0]
+    for s in range(1, SLOTS):
+        count = count + info[VALID, s]
+    return count
+
+
+def first_of(info, s):
+    return jnp.maximum(info[FIRST, s], TILES * LANES)
+
+
+def set_times(times_q, tiles):
     for q in range(TILES):
         times_q[q : q + 1] = tiles[q, TIME_ROW : TIME_ROW + 1]
 
 
-def time_rows(info, s, log_t, child_t, times_q, offset):
-    pos = lax.broadcasted_iota(jnp.int32, (TILES, LANES), 0) * LANES + offset
+def time_rows(info, s, log_t, child_t, times_q, own):
+    pos = lax.broadcasted_iota(jnp.int32, (TILES, LANES), 0) * LANES + (TILES * LANES if own else 0)
     pos = pos + lax.broadcasted_iota(jnp.int32, (TILES, LANES), 1)
-    low = info[LOW, s]
+    ok = pos >= info[LOW, s]
     for i in range(QUAD):
         at = QUAD * s + i
         delta = jnp.maximum(child_t[pl.ds(at, 1)] - times_q[...], 0.0)
-        ok = (pos >= low) & (pos < info[FIRST, s] + i)
-        log_t[at] = jnp.where(ok, log2_time_kernel(delta), DEAD)
+        allowed = ok & (pos < info[FIRST, s] + i) if own else ok
+        log_t[at] = jnp.where(allowed, log2_time_kernel(delta), DEAD)
 
 
 def kernel_of(tiles, q, child_b, log_t, at):
@@ -117,20 +127,21 @@
     return jnp.minimum(info[LOW, s] // (2 * LANES), HALF)
 
 
-def own_sums_kernel(info, own, packed, collected, log_t, child_b, sums, times_q, child_t):
-    count = info[COUNT, 0]
+def own_sums_kernel(info, own, packed, collected, child_b, child_t, log_t, sums, times_q):
+    count = slots_of(info)
     lane = lane_ids()
     mine = jnp.zeros((ROWS, LANES), jnp.float32)
     for s in range(SLOTS):
-        first = info[FIRST, s]
+        first = first_of(info, s)
         moved = pltpu.roll(own[first // LANES - TILES], lax.rem(QUAD * s + LANES - lax.rem(first, LANES), LANES), 1)
         mine = jnp.where(slot_lanes(lane, s), moved, mine)
     packed[...] = mine
     spread_lanes(child_b, mine[0 : 2 * CH])
-    set_times(child_t, mine, times_q, own)
+    child_t[...] = jnp.transpose(jnp.broadcast_to(mine[TIME_ROW : TIME_ROW + 1], (LANES, LANES)))
+    set_times(times_q, own)
 
     def times(s, carry):
-        time_rows(info, s, log_t, child_t, times_q, TILES * LANES)
+        time_rows(info, s, log_t, child_t, times_q, True)
         return carry
 
     lax.fori_loop(0, count, times, 0)
@@ -141,21 +152,21 @@
         return carry
 
     lax.fori_loop(0, count, slot, 0)
-    collected[...] = gather_lanes(sums)
+    for j, part in enumerate(gather_lanes(sums)):
+        collected[j * CH : (j + 1) * CH] = part
 
 
 def prev_kernel(
-    info, prev, packed, own_sums, part, result, ratio_out,
-    log_t, child_b, kern, sums, total, times_q, child_t
+    info, prev, packed, own_sums, child_b, child_t, part, result, ratio_out,
+    log_t, kern, sums, total, times_q
 ):
-    count = info[COUNT, 0]
-    spread_lanes(child_b, packed[0 : 2 * CH])
-    set_times(child_t, packed, times_q, prev)
+    count = slots_of(info)
+    set_times(times_q, prev)
 
     def times(s, carry):
         @pl.when(info[LOW, s] < TILES * LANES)
         def _():
-            time_rows(info, s, log_t, child_t, times_q, 0)
+            time_rows(info, s, log_t, child_t, times_q, False)
 
         return carry
 
@@ -167,14 +178,15 @@
 
     lax.fori_loop(0, count, slot, 0)
 
-    collected = own_sums[...] + gather_lanes(sums)
+    here = gather_lanes(sums)
+    summed, pull_x, pull_y = [own_sums[j * CH : (j + 1) * CH] + here[j] for j in range(3)]
     xs, ys, weights = packed[0:CH], packed[CH : 2 * CH], packed[W_ROW : W_ROW + CH]
-    intensity = packed[BACK_ROW : BACK_ROW + 1] + collected[0:CH]
+    intensity = packed[BACK_ROW : BACK_ROW + 1] + summed
     alive = packed[TIME_ROW : TIME_ROW + 1] >= 0.0
     ratio = weights / intensity
     ratio_out[...] = ratio
-    result[0:CH] = ratio * collected[CH : 2 * CH] * UNSCALE
-    result[CH : 2 * CH] = ratio * collected[2 * CH :] * UNSCALE
+    result[0:CH] = ratio * pull_x * UNSCALE
+    result[CH : 2 * CH] = ratio * pull_y * UNSCALE
     result[2 * CH :] = jnp.where(alive, jnp.log(intensity), 0.0)
     spread_lanes(sums, jnp.concatenate([ratio, ratio * xs, ratio * ys], axis=0))
 
@@ -210,15 +222,14 @@
     lax.fori_loop(0, TILES, finish, 0)
 
 
-def own_push_kernel(info, own, packed, result, ratio, part, log_t, child_b, ratio_b, times_q, child_t):
-    count = info[COUNT, 0]
+def own_push_kernel(info, own, result, ratio, child_b, child_t, part, log_t, ratio_b, times_q):
+    count = slots_of(info)
     lane = lane_ids()
-    spread_lanes(child_b, packed[0 : 2 * CH])
     spread_lanes(ratio_b, ratio[...] * -UNSCALE)
-    set_times(child_t, packed, times_q, own)
+    set_times(times_q, own)
 
     def times(s, carry):
-        time_rows(info, s, log_t, child_t, times_q, TILES * LANES)
+        time_rows(info, s, log_t, child_t, times_q, True)
         return carry
 
     lax.fori_loop(0, count, times, 0)
@@ -251,51 +262,69 @@
     lax.fori_loop(0, count, slot, 0)
 
     for s in range(SLOTS):
-        first = info[FIRST, s]
+        first = first_of(info, s)
         tile, at = first // LANES - TILES, lax.rem(first, LANES)
         moved = pltpu.roll(result[...], lax.rem(at + LANES - QUAD * s, LANES), 1)
         here = (lane >= at) & (lane < jnp.where(s < count, at + QUAD, at))
         part[tile] = part[tile] + jnp.where(here, moved, 0.0)
 
 
-def call(kernel, out_rows, scratch, *operands):
+def call(kernel, out_rows, scratch, scalars, *operands, mib=24):
     vmem = pl.BlockSpec(memory_space=pltpu.VMEM)
     return pl.pallas_call(
         kernel,
         out_shape=[jax.ShapeDtypeStruct(shape, jnp.float32) for shape in out_rows],
-        in_specs=[pl.BlockSpec(memory_space=pltpu.SMEM)] + [vmem] * (len(operands) - 1),
+        in_specs=[pl.BlockSpec(memory_space=pltpu.SMEM)] * len(scalars) + [vmem] * len(operands),
         out_specs=[vmem] * len(out_rows),
         scratch_shapes=[pltpu.VMEM(shape, jnp.float32) for shape in scratch],
-        compiler_params=pltpu.CompilerParams(vmem_limit_bytes=50 * 2**20),
-    )(*operands)
-
-
-TIMES = [(TILES, LANES), (LANES, LANES)]
+        compiler_params=pltpu.CompilerParams(vmem_limit_bytes=mib * 2**20),
+    )(*scalars, *operands)
+
+
+TIMES = (TILES, LANES)
 LOG_T = (LANES, TILES, LANES)
 CHILD_B = (LANES, 2 * CH, LANES)
 SUMS = (LANES, 3 * CH, LANES)
 
 
+def pack_kernel(window, live, locations, times, background, weights, out):
+    lane = lane_ids()
+    alive = lane < live[0]
+    numbers = (live[0], window[0], window[1])
+    meta = jnp.zeros((1, LANES), jnp.float32)
+    for i, number in enumerate(numbers):
+        meta = jnp.where(lane == i, number.astype(jnp.float32), meta)
+    rows = jnp.concatenate([jnp.where(alive, times[...], DEAD), background[...], meta], axis=0)
+    rest = jnp.zeros((W_ROW - META_ROW - 1, LANES), jnp.float32)
+    chunk = jnp.concatenate(
+        [locations[:, 0, :] * SCALE, locations[:, 1, :] * SCALE, rows, rest, jnp.where(alive, weights[...], 0.0)],
+        axis=0,
+    )
+    for to in range(TILES):
+        out[to] = chunk
+
+
+def pack(window, live, *operands):
+    return call(pack_kernel, [(TILES, ROWS, LANES)], [], (window, live), *operands)[0]
+
+
 def own_sums(info, own):
-    return call(own_sums_kernel, [(ROWS, LANES), (3 * CH, LANES)], [LOG_T, CHILD_B, SUMS] + TIMES, info, own)
-
-
-def prev_pairs(info, prev, packed, collected):
+    return call(
+        own_sums_kernel, [(ROWS, LANES), (3 * CH, LANES), CHILD_B, (LANES, LANES)], [LOG_T, SUMS, TIMES], (info,), own
+    )
+
+
+def prev_pairs(info, *operands):
     return call(
         prev_kernel,
         [(TILES, 2 * CH, LANES), (3 * CH, LANES), (CH, LANES)],
-        [LOG_T, CHILD_B, (LANES, TILES, CH, LANES), SUMS, (TILES, 3 * CH, LANES)] + TIMES,
-        info, prev, packed, collected,
+        [LOG_T, (LANES, TILES, CH, LANES), SUMS, (TILES, 3 * CH, LANES), TIMES],
+        (info,), *operands, mib=48,
     )
 
 
-def own_push(info, own, packed, result, ratio):
-    return call(
-        own_push_kernel,
-        [(TILES, 3 * CH, LANES)],
-        [LOG_T, CHILD_B, (LANES, CH, LANES)] + TIMES,
-        info, own, packed, result, ratio,
-    )[0]
+def own_push(info, *operands):
+    return call(own_push_kernel, [(TILES, 3 * CH, LANES)], [LOG_T, (LANES, CH, LANES), TIMES], (info,), *operands)[0]
 
 
 def plan(meta, me, no_prev):
@@ -313,31 +342,18 @@
     mine = (offset >= 0) & (offset < quads[None, :])
     first = TILES * LANES + block[None, :] * BLK + QUAD * offset
     values = jnp.stack([jnp.ones_like(first), first, jnp.broadcast_to(low[None, :], first.shape)])
-    info = jnp.sum(jnp.where(mine[None], values, 0), axis=2)
-    count = jnp.sum(info[0])
-    return jnp.stack([jnp.full((SLOTS,), count), jnp.maximum(info[1], TILES * LANES), info[2]])
+    return jnp.sum(jnp.where(mine[None], values, 0), axis=2)
 
 
 def per_device(locations, times, background, weights, window_start, live):
-    slot_ids = jnp.arange(LANES, dtype=jnp.int32)
-    alive = slot_ids < live[0]
-    meta = jnp.pad(jnp.concatenate([live, window_start]).astype(jnp.float32), (0, LANES - 3))
-    chunk = jnp.concatenate(
-        [
-            locations[:, 0, :] * SCALE,
-            locations[:, 1, :] * SCALE,
-            jnp.stack([jnp.where(alive, times, DEAD), background, meta]),
-            jnp.zeros((W_ROW - META_ROW - 1, LANES), jnp.float32),
-            jnp.where(alive, weights, 0.0),
-        ]
-    )
-    own = lax.all_to_all(jnp.broadcast_to(chunk[None], (TILES, ROWS, LANES)), "grp", 0, 0)
+    sent = pack(window_start, live, locations, times[None], background[None], weights)
+    own = lax.all_to_all(sent, "grp", 0, 0)
     prev = from_behind(own[:, 0:W_ROW], "tm", 1)
     info = plan(own[:, META_ROW, 0:3], lax.axis_index("grp").astype(jnp.int32), lax.axis_index("tm") == 0)
-    packed, collected = own_sums(info, own)
-    part_prev, result, ratio = prev_pairs(info, prev, packed, collected)
+    packed, collected, child_b, child_t = own_sums(info, own)
+    part_prev, result, ratio = prev_pairs(info, prev, packed, collected, child_b, child_t)
     back = from_behind(part_prev, "tm", -1)
-    part_own = own_push(info, own, packed, result, ratio)
+    part_own = own_push(info, own, result, ratio, child_b, child_t)
     part = jnp.concatenate([part_own[:, 0 : 2 * CH] + back, part_own[:, 2 * CH :]], axis=1)
     total = jnp.sum(lax.all_to_all(part, "grp", 0, 0), axis=0)
     grad = total[0 : 2 * CH].reshape(2, CH, LANES).transpose(1, 0, 2)

time: 111 us -> 110 us (level)
  the two profiles are of different devices: /device:TPU:26 before, /device:TPU:40 now
where the time goes in v4:
time: 110 us
  Pallas kernels  30.5 us (28%)
  blocking collectives  27.5 us (25%)
  waiting for transfers between devices  25.5 us (23%)
  starting transfers between devices  18.9 us (17%)
  local copies, waits for them, and re-layouts  5.13 us (5%)
  between operations  1.43 us (1%)
    pallas_call x4, Pallas kernels, call(): pl.pallas_call(kernel, out_shape=[jax.ShapeDtypeStruct(shape, jnp.float32...  30.5 us
    all_to_all x1, blocking collectives, per_device(): total = jnp.sum(lax.all_to_all(part, 'grp', 0, 0), axis=0)  27.5 us
    all_to_all x1, waiting for transfers between devices, per_device(): own = lax.all_to_all(sent, 'grp', 0, 0)  25.5 us
    all_to_all x1, starting transfers between devices, per_device(): own = lax.all_to_all(sent, 'grp', 0, 0)  13.2 us
    ppermute x2, starting transfers between devices, from_behind(): return lax.ppermute(value, axis, pairs)  5.74 us
    unnamed x10, local copies, waits for them, and re-layouts  3.37 us
  transfers between devices with their start and end apart: 3, of which 1 were waited for; matrix products, arithmetic and copies ran while one was open for 0% of the time, Pallas kernels for 18%

profile of v4, /device:TPU:40, one launch (start us, length us, event | category | flops | bytes accessed | tf_op | source)
XLA Modules:
  0.0 109.7 jit_solution(4226469045616392269)
XLA Ops:
  1.3 0.0 copy-start
  1.3 0.7 copy-done
  2.0 0.0 copy-start.1
  2.0 0.7 copy-done.1
  2.7 0.7 copy-done.2
  3.4 0.7 copy-done.3
  4.0 0.7 copy-done.4
  4.7 1.5 %shard_map.77 = f32[32,56,128]{2,1,0:T(8,128)} custom-call(s32[2]{0:T(128)S(1)} %copy-done.2, s32[1]{0:T(128)S(6)} %copy.19.live, f32[16,2,128]{2,1,0:T(2,128)S(1)} %copy-done, f32[1,128]{1,0:T(1,128)S(1)} %bitcast.10, f32[1,128]{1,0:T(1,128)S(1)} %bitcast.11, f32[16,128]{1,0:T(8,128)S(1)} %copy-done.1), custom_call_target="tpu_custom_call" | custom-call | tf_op jit(solution)/shard_map/pallas_call | solution.py:274
  6.2 13.2 %all-to-all-start = ((f32[32,56,128]{2,1,0:T(8,128)}), f32[32,56,128]{2,1,0:T(8,128)S(1)}, u32[]{:S(2)}, u32[]{:S(2)}) async-start(f32[32,56,128]{2,1,0:T(8,128)} %shard_map.77), calls=%async_computation | async-start | bytes 1835008 | tf_op jit(solution)/shard_map/all_to_all | solution.py:350
  19.4 25.5 %all-to-all-done.own = f32[32,56,128]{2,1,0:T(8,128)S(1)} async-done(((f32[32,56,128]{2,1,0:T(8,128)}), f32[32,56,128]{2,1,0:T(8,128)S(1)}, u32[]{:S(2)}, u32[]{:S(2)}) %all-to-all-start) | async-done | bytes 917536 | tf_op jit(solution)/shard_map/all_to_all | solution.py:350
  45.0 0.1 copy.14
  45.1 0.1 copy.15
  45.2 0.1 max.25
  45.3 0.1 broadcast_in_dim.44
  45.3 0.1 convert_element_type.33
  45.5 1.9 %collective-permute-start = (f32[32,40,128]{2,1,0:T(8,128)S(1)}, f32[32,40,128]{2,1,0:T(8,128)S(1)}, u32[]{:S(2)}, u32[]{:S(2)}) collective-permute-start(f32[32,40,128]{2,1,0:T(8,128)S(1)} %slice.33), channel_id=1, source_target_pairs={{0,32},{32,64},{64,96},{96,128},{128,160},{160,192},{192,224},{224... | collective-permute-start | bytes 1966088 | tf_op jit(solution)/shard_map/ppermute | solution.py:38
  47.5 0.1 select_reduce_fusion
  47.6 0.1 fusion.1
  47.6 0.1 multiply_add_fusion
  47.7 0.2 fusion.info
  47.9 10.2 %shard_map.78 = (f32[56,128]{1,0:T(8,128)S(1)}, f32[48,128]{1,0:T(8,128)S(1)}, f32[128,32,128]{2,1,0:T(8,128)S(1)}, f32[128,128]{1,0:T(8,128)S(1)}) custom-call(s32[3,32]{1,0:T(4,128)S(1)} %fusion.info, f32[32,56,128]{2,1,0:T(8,128)S(1)} %all-to-all-done.own), custom_call_target="tpu_custom_call" | custom-call | tf_op jit(solution)/shard_map/pallas_call | solution.py:274
  58.1 0.0 collective-permute-done.prev
  58.1 9.0 %shard_map.79 = (f32[32,32,128]{2,1,0:T(8,128)S(1)}, f32[48,128]{1,0:T(8,128)S(1)}, f32[16,128]{1,0:T(8,128)S(1)}) custom-call(s32[3,32]{1,0:T(4,128)S(1)} %fusion.info, f32[32,40,128]{2,1,0:T(8,128)S(1)} %collective-permute-done.prev, f32[56,128]{1,0:T(8,128)S(1)} %get-tuple-element.9.packed, f32[48,128]{1,0:T(8,128)S(1)} %get-tuple-element.10.own_sums, ...), custom_call_target="tpu_custom_call" | custom-call | tf_op jit(solution)/shard_map/pallas_call | solution.py:274
  67.2 3.8 %collective-permute-start.1 = (f32[32,32,128]{2,1,0:T(8,128)S(1)}, f32[32,32,128]{2,1,0:T(8,128)S(1)}, u32[]{:S(2)}, u32[]{:S(2)}) collective-permute-start(f32[32,32,128]{2,1,0:T(8,128)S(1)} %get-tuple-element.15), channel_id=1, source_target_pairs={{32,0},{64,32},{96,64},{128,96},{160,128},{192,160},{224,192},{256... | collective-permute-start | bytes 1572872 | tf_op jit(solution)/shard_map/ppermute | solution.py:38
  71.0 9.8 %shard_map.80 = f32[32,48,128]{2,1,0:T(8,128)S(1)} custom-call(s32[3,32]{1,0:T(4,128)S(1)} %fusion.info, f32[32,56,128]{2,1,0:T(8,128)S(1)} %all-to-all-done.own, f32[48,128]{1,0:T(8,128)S(1)} %get-tuple-element.13.result, f32[16,128]{1,0:T(8,128)S(1)} %get-tuple-element.14.ratio, f32[128,32,128]{2,1,0:T(8,128)S(1)} %get-tuple-element.11.child_b, ...), custom_call_target="tpu_custom_call" | custom-call | tf_op jit(solution)/shard_map/pallas_call | solution.py:274
  80.8 0.0 collective-permute-done.1
  80.8 0.1 slice_add_fusion
  80.9 0.1 pad_maximum_fusion
  80.9 27.5 %all_to_all.10 = f32[32,48,128]{2,1,0:T(8,128)S(1)} all-to-all(f32[32,48,128]{2,1,0:T(8,128)S(1)} %pad_maximum_fusion), channel_id=1, replica_groups=mesh['tm'=16,'grp'=32] {'grp'}, dimensions={0} | all-to-all | bytes 1572864 | tf_op jit(solution)/shard_map/all_to_all | solution.py:358
  108.4 0.1 reduce_sum.29
  108.5 0.6 slice.37
  109.1 0.6 copy.18
  (14 shorter events, 0.1 us)
Async XLA Ops:
  1.3 0.7 copy-start
  2.0 0.7 copy-start.1
  2.7 0.7 copy-start.2
  3.3 0.7 copy-start.3
  4.0 0.7 copy-start.4
  6.2 38.8 %all-to-all-start = ((f32[32,56,128]{2,1,0:T(8,128)}), f32[32,56,128]{2,1,0:T(8,128)S(1)}, u32[]{:S(2)}, u32[]{:S(2)}) async-start(f32[32,56,128]{2,1,0:T(8,128)} %shard_map.77), calls=%async_computation | async-start | bytes 1835008 | tf_op jit(solution)/shard_map/all_to_all | solution.py:350
  45.5 12.6 %collective-permute-start = (f32[32,40,128]{2,1,0:T(8,128)S(1)}, f32[32,40,128]{2,1,0:T(8,128)S(1)}, u32[]{:S(2)}, u32[]{:S(2)}) collective-permute-start(f32[32,40,128]{2,1,0:T(8,128)S(1)} %slice.33), channel_id=1, source_target_pairs={{0,32},{32,64},{64,96},{96,128},{128,160},{160,192},{192,224},{224... | collective-permute-start | bytes 1966088 | tf_op jit(solution)/shard_map/ppermute | solution.py:38
  67.2 13.6 %collective-permute-start.1 = (f32[32,32,128]{2,1,0:T(8,128)S(1)}, f32[32,32,128]{2,1,0:T(8,128)S(1)}, u32[]{:S(2)}, u32[]{:S(2)}) collective-permute-start(f32[32,32,128]{2,1,0:T(8,128)S(1)} %get-tuple-element.15), channel_id=1, source_target_pairs={{32,0},{64,32},{96,64},{128,96},{160,128},{192,160},{224,192},{256... | collective-permute-start | bytes 1572872 | tf_op jit(solution)/shard_map/ppermute | solution.py:38

commit v5 on v4

--- a/solution.py
+++ b/solution.py
@@ -24,7 +24,9 @@
 TIME_ROW, BACK_ROW, META_ROW = range(2 * CH, 2 * CH + 3)
 W_ROW = 40
 ROWS = W_ROW + CH
-VALID, FIRST, LOW = range(3)
+VALID, FIRST, LOW, BEFORE = range(4)
+LOG_ROW = 2 * CH
+BACK_ROWS = LOG_ROW + 8
 
 SCALE = math.sqrt(0.5 / math.log(2.0))
 UNSCALE = 1.0 / SCALE
@@ -182,7 +184,7 @@
     summed, pull_x, pull_y = [own_sums[j * CH : (j + 1) * CH] + here[j] for j in range(3)]
     xs, ys, weights = packed[0:CH], packed[CH : 2 * CH], packed[W_ROW : W_ROW + CH]
     intensity = packed[BACK_ROW : BACK_ROW + 1] + summed
-    alive = packed[TIME_ROW : TIME_ROW + 1] >= 0.0
+    alive = (packed[TIME_ROW : TIME_ROW + 1] >= 0.0) & (lane_ids() < QUAD * count)
     ratio = weights / intensity
     ratio_out[...] = ratio
     result[0:CH] = ratio * pull_x * UNSCALE
@@ -222,7 +224,22 @@
     lax.fori_loop(0, TILES, finish, 0)
 
 
-def own_push_kernel(info, own, result, ratio, child_b, child_t, part, log_t, ratio_b, times_q):
+def exact_dot(a, b):
+    return jnp.dot(a, b, precision=lax.Precision.HIGHEST, preferred_element_type=jnp.float32)
+
+
+def logs_by_slot(logs):
+    wide = jnp.concatenate([logs, jnp.zeros((LANES - CH, LANES), jnp.float32)], axis=0)
+    row = lax.broadcasted_iota(jnp.int32, (LANES, LANES), 0)
+    lane = lax.broadcasted_iota(jnp.int32, (LANES, LANES), 1)
+    by_child = exact_dot(jnp.transpose(wide), ((lane % BLK) // QUAD == row).astype(jnp.float32))
+    by_child = jnp.where(lane % QUAD == row % QUAD, by_child, 0.0)
+    slot = lax.broadcasted_iota(jnp.int32, (SLOTS, LANES), 0)
+    child = lax.broadcasted_iota(jnp.int32, (SLOTS, LANES), 1)
+    return exact_dot((child // QUAD == slot).astype(jnp.float32), by_child)
+
+
+def own_push_kernel(info, own, result, ratio, child_b, child_t, part, log_t, ratio_b, times_q, slot_logs):
     count = slots_of(info)
     lane = lane_ids()
     spread_lanes(ratio_b, ratio[...] * -UNSCALE)
@@ -235,7 +252,7 @@
     lax.fori_loop(0, count, times, 0)
 
     def clear(q, carry):
-        part[q] = jnp.zeros((3 * CH, LANES), jnp.float32)
+        part[q] = jnp.zeros((BACK_ROWS, LANES), jnp.float32)
         return carry
 
     lax.fori_loop(0, TILES, clear, 0)
@@ -261,12 +278,16 @@
 
     lax.fori_loop(0, count, slot, 0)
 
+    slot_logs[...] = logs_by_slot(result[2 * CH :])
     for s in range(SLOTS):
         first = first_of(info, s)
         tile, at = first // LANES - TILES, lax.rem(first, LANES)
-        moved = pltpu.roll(result[...], lax.rem(at + LANES - QUAD * s, LANES), 1)
+        moved = pltpu.roll(result[0 : 2 * CH], lax.rem(at + LANES - QUAD * s, LANES), 1)
         here = (lane >= at) & (lane < jnp.where(s < count, at + QUAD, at))
-        part[tile] = part[tile] + jnp.where(here, moved, 0.0)
+        part[tile, 0 : 2 * CH] = part[tile, 0 : 2 * CH] + jnp.where(here, moved, 0.0)
+        half = jnp.where(s < count, at // BLK, 2)
+        row = part[tile, LOG_ROW : LOG_ROW + 1]
+        part[tile, LOG_ROW : LOG_ROW + 1] = row + jnp.where(lane // BLK == half, slot_logs[s : s + 1], 0.0)
 
 
 def call(kernel, out_rows, scratch, scalars, *operands, mib=24):
@@ -287,7 +308,14 @@
 SUMS = (LANES, 3 * CH, LANES)
 
 
-def pack_kernel(window, live, locations, times, background, weights, out):
+def pack_kernel(*refs):
+    operands, out, scratch, arrived = refs[:6], refs[6], refs[7:13], refs[13]
+    copies = [pltpu.make_async_copy(operands[i], scratch[i], arrived.at[i]) for i in range(6)]
+    for copy in copies:
+        copy.start()
+    for copy in copies:
+        copy.wait()
+    window, live, locations, times, background, weights = scratch
     lane = lane_ids()
     alive = lane < live[0]
     numbers = (live[0], window[0], window[1])
@@ -304,8 +332,52 @@
         out[to] = chunk
 
 
-def pack(window, live, *operands):
-    return call(pack_kernel, [(TILES, ROWS, LANES)], [], (window, live), *operands)[0]
+def pack(*operands):
+    spaces = [pltpu.SMEM] * 2 + [pltpu.VMEM] * 4
+    return pl.pallas_call(
+        pack_kernel,
+        out_shape=jax.ShapeDtypeStruct((TILES, ROWS, LANES), jnp.float32),
+        in_specs=[pl.BlockSpec(memory_space=pltpu.HBM)] * 6,
+        out_specs=pl.BlockSpec(memory_space=pltpu.VMEM),
+        scratch_shapes=[space(x.shape, x.dtype) for space, x in zip(spaces, operands)]
+        + [pltpu.SemaphoreType.DMA((6,))],
+        compiler_params=pltpu.CompilerParams(vmem_limit_bytes=24 * 2**20),
+    )(*operands)
+
+
+def collect_kernel(info, received, grad, logs, log_rows):
+    log_rows[...] = jnp.zeros((LANES, LANES), jnp.float32)
+    total = received[0, 0 : 2 * CH]
+    log_rows[0:1] = received[0, LOG_ROW : LOG_ROW + 1]
+    for source in range(1, TILES):
+        total = total + received[source, 0 : 2 * CH]
+        log_rows[source : source + 1] = received[source, LOG_ROW : LOG_ROW + 1]
+    grad[:, 0, :] = total[0:CH]
+    grad[:, 1, :] = total[CH:]
+    row = lax.broadcasted_iota(jnp.int32, (LANES, LANES), 0)
+    lane = lax.broadcasted_iota(jnp.int32, (LANES, LANES), 1)
+    number = jnp.where(lane < BLK, info[BEFORE, 0], info[BEFORE, 1]) + (lane % BLK) // QUAD
+    source = (number - HALF * ((number // TILES) % 2)) % TILES
+    chosen = exact_dot(jnp.transpose(log_rows[...]), (row == source).astype(jnp.float32))
+    chosen = jnp.where((row // BLK == lane // BLK) & (row % QUAD == lane % QUAD), chosen, 0.0)
+    chain = lax.broadcasted_iota(jnp.int32, (CH, LANES), 0)
+    place = lax.broadcasted_iota(jnp.int32, (CH, LANES), 1)
+    logs[...] = exact_dot(((place % BLK) // QUAD == chain).astype(jnp.float32), chosen)
+
+
+def collect(info, received):
+    vmem = pl.BlockSpec(memory_space=pltpu.VMEM)
+    return pl.pallas_call(
+        collect_kernel,
+        out_shape=[
+            jax.ShapeDtypeStruct((CH, 2, LANES), jnp.float32),
+            jax.ShapeDtypeStruct((CH, LANES), jnp.float32),
+        ],
+        in_specs=[pl.BlockSpec(memory_space=pltpu.SMEM), vmem],
+        out_specs=[vmem] * 2,
+        scratch_shapes=[pltpu.VMEM((LANES, LANES), jnp.float32)],
+        compiler_params=pltpu.CompilerParams(vmem_limit_bytes=24 * 2**20),
+    )(info, received)
 
 
 def own_sums(info, own):
@@ -324,7 +396,12 @@
 
 
 def own_push(info, *operands):
-    return call(own_push_kernel, [(TILES, 3 * CH, LANES)], [LOG_T, (LANES, CH, LANES), TIMES], (info,), *operands)[0]
+    return call(
+        own_push_kernel,
+        [(TILES, BACK_ROWS, LANES)],
+        [LOG_T, (LANES, CH, LANES), TIMES, (SLOTS, LANES)],
+        (info,), *operands,
+    )[0]
 
 
 def plan(meta, me, no_prev):
@@ -341,8 +418,11 @@
     offset = number[:, None] - before[None, :]
     mine = (offset >= 0) & (offset < quads[None, :])
     first = TILES * LANES + block[None, :] * BLK + QUAD * offset
-    values = jnp.stack([jnp.ones_like(first), first, jnp.broadcast_to(low[None, :], first.shape)])
-    return jnp.sum(jnp.where(mine[None], values, 0), axis=2)
+    own_block = block[None, :] == 2 * me + rounds[:, None] % 2
+    every = [jnp.broadcast_to(value[None, :], first.shape) for value in (low, before)]
+    values = jnp.stack([jnp.ones_like(first), first, *every])
+    mine = jnp.stack([mine, mine, mine, own_block])
+    return jnp.sum(jnp.where(mine, values, 0), axis=2)
 
 
 def per_device(locations, times, background, weights, window_start, live):
@@ -355,9 +435,8 @@
     back = from_behind(part_prev, "tm", -1)
     part_own = own_push(info, own, result, ratio, child_b, child_t)
     part = jnp.concatenate([part_own[:, 0 : 2 * CH] + back, part_own[:, 2 * CH :]], axis=1)
-    total = jnp.sum(lax.all_to_all(part, "grp", 0, 0), axis=0)
-    grad = total[0 : 2 * CH].reshape(2, CH, LANES).transpose(1, 0, 2)
-    return (grad, total[2 * CH :])
+    grad, log_intensity = collect(info, lax.all_to_all(part, "grp", 0, 0))
+    return (grad, log_intensity)
 
 
 def solution(mesh):

time: 110 us -> 108 us (0.982)
  the two profiles are of different devices: /device:TPU:40 before, /device:TPU:9 now
where the time goes in v5:
time: 108 us; the launch traced here: 107 us
  Pallas kernels  33.3 us (31%)
  blocking collectives  23.7 us (22%)
  waiting for transfers between devices  23.3 us (22%)
  starting transfers between devices  21 us (19%)
  local copies, waits for them, and re-layouts  3.91 us (4%)
  between operations  1.43 us (1%)
    pallas_call x3, Pallas kernels, call(): pl.pallas_call(kernel, out_shape=[jax.ShapeDtypeStruct(shape, jnp.float32...  30 us
    all_to_all x1, blocking collectives, per_device(): grad, log_intensity = collect(info, lax.all_to_all(part, 'grp', 0, 0))  23.7 us
    all_to_all x1, waiting for transfers between devices, per_device(): own = lax.all_to_all(sent, 'grp', 0, 0)  23.3 us
    all_to_all x1, starting transfers between devices, per_device(): own = lax.all_to_all(sent, 'grp', 0, 0)  12.9 us
    ppermute x2, starting transfers between devices, from_behind(): return lax.ppermute(value, axis, pairs)  8.11 us
    unnamed x10, local copies, waits for them, and re-layouts  3.37 us
  transfers between devices with their start and end apart: 3, of which 1 were waited for; matrix products, arithmetic and copies ran while one was open for 1% of the time, Pallas kernels for 19%

profile of v5, /device:TPU:9, one launch (start us, length us, event | category | flops | bytes accessed | tf_op | source)
XLA Modules:
  0.0 107.4 jit_solution(7760801759047162304)
XLA Ops:
  1.3 0.0 copy-start
  1.3 0.7 copy-done
  2.0 0.7 copy-done.1
  2.7 0.0 copy-start.2
  2.7 0.7 copy-done.2
  3.3 0.0 copy-start.3
  3.4 0.7 copy-done.3
  4.0 0.0 copy-start.4
  4.0 0.7 copy-done.4
  4.7 1.6 %shard_map.77 = f32[32,56,128]{2,1,0:T(8,128)} custom-call(s32[2]{0:T(128)S(1)} %copy-done.2, s32[1]{0:T(128)S(6)} %copy.14.refs_1_, f32[16,2,128]{2,1,0:T(2,128)S(1)} %copy-done, f32[1,128]{1,0:T(1,128)S(1)} %bitcast.6, f32[1,128]{1,0:T(1,128)S(1)} %bitcast.7, f32[16,128]{1,0:T(8,128)S(1)} %copy-done.1), custom_call_target="tpu_custom_call" | custom-call | tf_op jit(solution)/shard_map/pallas_call | solution.py:337
  6.3 12.9 %all-to-all-start = ((f32[32,56,128]{2,1,0:T(8,128)}), f32[32,56,128]{2,1,0:T(8,128)S(1)}, u32[]{:S(2)}, u32[]{:S(2)}) async-start(f32[32,56,128]{2,1,0:T(8,128)} %shard_map.77), calls=%async_computation | async-start | bytes 1835008 | tf_op jit(solution)/shard_map/all_to_all | solution.py:430
  19.3 0.1 iota_compare_fusion
  19.3 23.3 %all-to-all-done.own = f32[32,56,128]{2,1,0:T(8,128)S(1)} async-done(((f32[32,56,128]{2,1,0:T(8,128)}), f32[32,56,128]{2,1,0:T(8,128)S(1)}, u32[]{:S(2)}, u32[]{:S(2)}) %all-to-all-start) | async-done | bytes 917536 | tf_op jit(solution)/shard_map/all_to_all | solution.py:430
  42.7 0.1 copy.12
  42.8 0.1 copy.13
  42.8 0.1 max.25
  43.0 0.1 broadcast_in_dim.38
  43.0 0.1 convert_element_type.33
  43.2 6.2 %collective-permute-start = (f32[32,40,128]{2,1,0:T(8,128)S(1)}, f32[32,40,128]{2,1,0:T(8,128)S(1)}, u32[]{:S(2)}, u32[]{:S(2)}) collective-permute-start(f32[32,40,128]{2,1,0:T(8,128)S(1)} %slice.25), channel_id=1, source_target_pairs={{0,32},{32,64},{64,96},{96,128},{128,160},{160,192},{192,224},{224... | collective-permute-start | bytes 1966088 | tf_op jit(solution)/shard_map/ppermute | solution.py:40
  49.4 0.1 select_reduce_fusion
  49.5 0.1 fusion.2
  49.6 0.1 fusion.1
  49.7 0.2 fusion.info
  49.9 10.1 %shard_map.78 = (f32[56,128]{1,0:T(8,128)S(1)}, f32[48,128]{1,0:T(8,128)S(1)}, f32[128,32,128]{2,1,0:T(8,128)S(1)}, f32[128,128]{1,0:T(8,128)S(1)}) custom-call(s32[4,32]{1,0:T(4,128)S(1)} %fusion.info, f32[32,56,128]{2,1,0:T(8,128)S(1)} %all-to-all-done.own), custom_call_target="tpu_custom_call" | custom-call | tf_op jit(solution)/shard_map/pallas_call | solution.py:295
  60.0 0.0 collective-permute-done.prev
  60.0 9.8 %shard_map.79 = (f32[32,32,128]{2,1,0:T(8,128)S(1)}, f32[48,128]{1,0:T(8,128)S(1)}, f32[16,128]{1,0:T(8,128)S(1)}) custom-call(s32[4,32]{1,0:T(4,128)S(1)} %fusion.info, f32[32,40,128]{2,1,0:T(8,128)S(1)} %collective-permute-done.prev, f32[56,128]{1,0:T(8,128)S(1)} %get-tuple-element.9.packed, f32[48,128]{1,0:T(8,128)S(1)} %get-tuple-element.10.own_sums, ...), custom_call_target="tpu_custom_call" | custom-call | tf_op jit(solution)/shard_map/pallas_call | solution.py:295
  69.8 1.9 %collective-permute-start.1 = (f32[32,32,128]{2,1,0:T(8,128)S(1)}, f32[32,32,128]{2,1,0:T(8,128)S(1)}, u32[]{:S(2)}, u32[]{:S(2)}) collective-permute-start(f32[32,32,128]{2,1,0:T(8,128)S(1)} %get-tuple-element.15), channel_id=1, source_target_pairs={{32,0},{64,32},{96,64},{128,96},{160,128},{192,160},{224,192},{256... | collective-permute-start | bytes 1572872 | tf_op jit(solution)/shard_map/ppermute | solution.py:40
  71.7 10.1 %shard_map.80 = f32[32,40,128]{2,1,0:T(8,128)S(1)} custom-call(s32[4,32]{1,0:T(4,128)S(1)} %fusion.info, f32[32,56,128]{2,1,0:T(8,128)S(1)} %all-to-all-done.own, f32[48,128]{1,0:T(8,128)S(1)} %get-tuple-element.13.result, f32[16,128]{1,0:T(8,128)S(1)} %get-tuple-element.14.ratio, f32[128,32,128]{2,1,0:T(8,128)S(1)} %get-tuple-element.11.child_b, ...), custom_call_target="tpu_custom_call" | custom-call | tf_op jit(solution)/shard_map/pallas_call | solution.py:295
  81.8 0.0 collective-permute-done.1
  81.8 0.1 slice_add_fusion
  82.0 23.7 %all_to_all.10.received = f32[32,40,128]{2,1,0:T(8,128)S(1)} all-to-all(f32[32,40,128]{2,1,0:T(8,128)S(1)} %pad_maximum_fusion), channel_id=1, replica_groups=mesh['tm'=16,'grp'=32] {'grp'}, dimensions={0} | all-to-all | bytes 1310720 | tf_op jit(solution)/shard_map/all_to_all | solution.py:438
  105.7 1.7 %shard_map.81 = (f32[16,2,128]{2,1,0:T(2,128)}, f32[16,128]{1,0:T(8,128)}) custom-call(s32[4,32]{1,0:T(4,128)S(1)} %fusion.info, f32[32,40,128]{2,1,0:T(8,128)S(1)} %all_to_all.10.received), custom_call_target="tpu_custom_call" | custom-call | tf_op jit(solution)/shard_map/pallas_call | solution.py:370
  (14 shorter events, 0.2 us)
Async XLA Ops:
  1.3 0.7 copy-start
  2.0 0.7 copy-start.1
  2.7 0.7 copy-start.2
  3.3 0.7 copy-start.3
  4.0 0.7 copy-start.4
  6.3 36.4 %all-to-all-start = ((f32[32,56,128]{2,1,0:T(8,128)}), f32[32,56,128]{2,1,0:T(8,128)S(1)}, u32[]{:S(2)}, u32[]{:S(2)}) async-start(f32[32,56,128]{2,1,0:T(8,128)} %shard_map.77), calls=%async_computation | async-start | bytes 1835008 | tf_op jit(solution)/shard_map/all_to_all | solution.py:430
  43.2 16.8 %collective-permute-start = (f32[32,40,128]{2,1,0:T(8,128)S(1)}, f32[32,40,128]{2,1,0:T(8,128)S(1)}, u32[]{:S(2)}, u32[]{:S(2)}) collective-permute-start(f32[32,40,128]{2,1,0:T(8,128)S(1)} %slice.25), channel_id=1, source_target_pairs={{0,32},{32,64},{64,96},{96,128},{128,160},{160,192},{192,224},{224... | collective-permute-start | bytes 1966088 | tf_op jit(solution)/shard_map/ppermute | solution.py:40
  69.8 12.0 %collective-permute-start.1 = (f32[32,32,128]{2,1,0:T(8,128)S(1)}, f32[32,32,128]{2,1,0:T(8,128)S(1)}, u32[]{:S(2)}, u32[]{:S(2)}) collective-permute-start(f32[32,32,128]{2,1,0:T(8,128)S(1)} %get-tuple-element.15), channel_id=1, source_target_pairs={{32,0},{64,32},{96,64},{128,96},{160,128},{192,160},{224,192},{256... | collective-permute-start | bytes 1572872 | tf_op jit(solution)/shard_map/ppermute | solution.py:40

commit v6 on v5

--- a/solution.py
+++ b/solution.py
@@ -21,10 +21,10 @@
 
 HALF = TILES // 2
 
-TIME_ROW, BACK_ROW, META_ROW = range(2 * CH, 2 * CH + 3)
-W_ROW = 40
-ROWS = W_ROW + CH
-VALID, FIRST, LOW, BEFORE = range(4)
+TIME_ROW, BACK_ROW, META_ROW, QUAD_ROW = range(2 * CH, 2 * CH + 4)
+ROWS = 40
+W_ROW = ROWS
+VALID, FIRST, LOW = range(3)
 LOG_ROW = 2 * CH
 BACK_ROWS = LOG_ROW + 8
 
@@ -67,15 +67,23 @@
     return [collected[j * CH : (j + 1) * CH] for j in range(3)]
 
 
-def slots_of(info):
-    count = info[VALID, 0]
-    for s in range(1, SLOTS):
-        count = count + info[VALID, s]
-    return count
-
-
-def first_of(info, s):
-    return jnp.maximum(info[FIRST, s], TILES * LANES)
+def mirrored(tile):
+    return ((tile & 1) << 4) | ((tile & 2) << 2) | (tile & 4) | ((tile & 8) >> 2) | ((tile & 16) >> 4)
+
+
+def deal(live, first_window, second_window):
+    quads = [jnp.clip((live - BLK * i + QUAD - 1) // QUAD, 0, BLK // QUAD) for i in range(2)]
+    second = (first_window >= second_window).astype(jnp.int32)
+    swap = second * (quads[1] - quads[0])
+    return second, quads[0] + swap, quads[1] - swap
+
+
+def quad_at(place, live, first_window, second_window):
+    first, ahead, behind = deal(live, first_window, second_window)
+    later = (place >= ahead).astype(jnp.int32)
+    block = first + later * (1 - 2 * first)
+    valid = place < ahead + behind
+    return jnp.where(valid, block * (BLK // QUAD) + place - later * ahead, 0), valid
 
 
 def set_times(times_q, tiles):
@@ -129,31 +137,62 @@
     return jnp.minimum(info[LOW, s] // (2 * LANES), HALF)
 
 
-def own_sums_kernel(info, own, packed, collected, child_b, child_t, log_t, sums, times_q):
-    count = slots_of(info)
+def exact_dot(a, b):
+    return jnp.dot(a, b, precision=lax.Precision.HIGHEST, preferred_element_type=jnp.float32)
+
+
+def square():
+    return lax.broadcasted_iota(jnp.int32, (LANES, LANES), 0), lax.broadcasted_iota(jnp.int32, (LANES, LANES), 1)
+
+
+def rows_of_quads(values):
+    wide = jnp.concatenate([values, jnp.zeros((LANES - CH, LANES), jnp.float32)], axis=0)
+    row, lane = square()
+    by_lane = exact_dot(jnp.transpose(wide), (lane // QUAD == row).astype(jnp.float32))
+    by_lane = jnp.where(lane % QUAD == row % QUAD, by_lane, 0.0)
+    slot = lax.broadcasted_iota(jnp.int32, (SLOTS, LANES), 0)
+    child = lax.broadcasted_iota(jnp.int32, (SLOTS, LANES), 1)
+    return exact_dot((child // QUAD == slot).astype(jnp.float32), by_lane)
+
+
+def place_quads(rows, source):
+    row, lane = square()
+    chosen = exact_dot(jnp.transpose(rows), (row == source).astype(jnp.float32))
+    chosen = jnp.where(row % QUAD == lane % QUAD, chosen, 0.0)
+    chain = lax.broadcasted_iota(jnp.int32, (CH, LANES), 0)
+    place = lax.broadcasted_iota(jnp.int32, (CH, LANES), 1)
+    return exact_dot((place // QUAD == chain).astype(jnp.float32), chosen)
+
+
+def own_sums_kernel(info, own, packed, collected, child_b, child_t, log_t, sums, times_q, quad_rows):
     lane = lane_ids()
     mine = jnp.zeros((ROWS, LANES), jnp.float32)
+    quad_rows[...] = jnp.zeros((LANES, LANES), jnp.float32)
     for s in range(SLOTS):
-        first = first_of(info, s)
-        moved = pltpu.roll(own[first // LANES - TILES], lax.rem(QUAD * s + LANES - lax.rem(first, LANES), LANES), 1)
-        mine = jnp.where(slot_lanes(lane, s), moved, mine)
-    packed[...] = mine
+        shift = lax.rem(QUAD * s + LANES - lax.rem(info[FIRST, s], LANES), LANES)
+        mine = jnp.where(slot_lanes(lane, s), pltpu.roll(own[s], shift, 1), mine)
+        quad_rows[s : s + 1] = own[s, QUAD_ROW : QUAD_ROW + 1]
+    packed[0:ROWS] = mine
+    packed[W_ROW:] = place_quads(quad_rows[...], lane // QUAD)
     spread_lanes(child_b, mine[0 : 2 * CH])
     child_t[...] = jnp.transpose(jnp.broadcast_to(mine[TIME_ROW : TIME_ROW + 1], (LANES, LANES)))
     set_times(times_q, own)
 
     def times(s, carry):
-        time_rows(info, s, log_t, child_t, times_q, True)
-        return carry
-
-    lax.fori_loop(0, count, times, 0)
+        @pl.when(info[VALID, s] > 0)
+        def _():
+            time_rows(info, s, log_t, child_t, times_q, True)
+
+        return carry
+
+    lax.fori_loop(0, SLOTS, times, 0)
 
     def slot(s, carry):
         start, end = own_steps(info, s)
         slot_sums(own, s, start, end, child_b, log_t, sums)
         return carry
 
-    lax.fori_loop(0, count, slot, 0)
+    lax.fori_loop(0, SLOTS, slot, 0)
     for j, part in enumerate(gather_lanes(sums)):
         collected[j * CH : (j + 1) * CH] = part
 
@@ -162,7 +201,6 @@
     info, prev, packed, own_sums, child_b, child_t, part, result, ratio_out,
     log_t, kern, sums, total, times_q
 ):
-    count = slots_of(info)
     set_times(times_q, prev)
 
     def times(s, carry):
@@ -172,19 +210,19 @@
 
         return carry
 
-    lax.fori_loop(0, count, times, 0)
+    lax.fori_loop(0, SLOTS, times, 0)
 
     def slot(s, carry):
         slot_sums(prev, s, prev_start(info, s), HALF, child_b, log_t, sums, kern)
         return carry
 
-    lax.fori_loop(0, count, slot, 0)
+    lax.fori_loop(0, SLOTS, slot, 0)
 
     here = gather_lanes(sums)
     summed, pull_x, pull_y = [own_sums[j * CH : (j + 1) * CH] + here[j] for j in range(3)]
     xs, ys, weights = packed[0:CH], packed[CH : 2 * CH], packed[W_ROW : W_ROW + CH]
     intensity = packed[BACK_ROW : BACK_ROW + 1] + summed
-    alive = (packed[TIME_ROW : TIME_ROW + 1] >= 0.0) & (lane_ids() < QUAD * count)
+    alive = packed[TIME_ROW : TIME_ROW + 1] >= 0.0
     ratio = weights / intensity
     ratio_out[...] = ratio
     result[0:CH] = ratio * pull_x * UNSCALE
@@ -212,7 +250,7 @@
         lax.fori_loop(prev_start(info, s), HALF, body, 0)
         return carry
 
-    lax.fori_loop(0, count, push, 0)
+    lax.fori_loop(0, SLOTS, push, 0)
 
     def finish(q, carry):
         weight = total[q, 0:CH]
@@ -224,32 +262,19 @@
     lax.fori_loop(0, TILES, finish, 0)
 
 
-def exact_dot(a, b):
-    return jnp.dot(a, b, precision=lax.Precision.HIGHEST, preferred_element_type=jnp.float32)
-
-
-def logs_by_slot(logs):
-    wide = jnp.concatenate([logs, jnp.zeros((LANES - CH, LANES), jnp.float32)], axis=0)
-    row = lax.broadcasted_iota(jnp.int32, (LANES, LANES), 0)
-    lane = lax.broadcasted_iota(jnp.int32, (LANES, LANES), 1)
-    by_child = exact_dot(jnp.transpose(wide), ((lane % BLK) // QUAD == row).astype(jnp.float32))
-    by_child = jnp.where(lane % QUAD == row % QUAD, by_child, 0.0)
-    slot = lax.broadcasted_iota(jnp.int32, (SLOTS, LANES), 0)
-    child = lax.broadcasted_iota(jnp.int32, (SLOTS, LANES), 1)
-    return exact_dot((child // QUAD == slot).astype(jnp.float32), by_child)
-
-
 def own_push_kernel(info, own, result, ratio, child_b, child_t, part, log_t, ratio_b, times_q, slot_logs):
-    count = slots_of(info)
     lane = lane_ids()
     spread_lanes(ratio_b, ratio[...] * -UNSCALE)
     set_times(times_q, own)
 
     def times(s, carry):
-        time_rows(info, s, log_t, child_t, times_q, True)
-        return carry
-
-    lax.fori_loop(0, count, times, 0)
+        @pl.when(info[VALID, s] > 0)
+        def _():
+            time_rows(info, s, log_t, child_t, times_q, True)
+
+        return carry
+
+    lax.fori_loop(0, SLOTS, times, 0)
 
     def clear(q, carry):
         part[q] = jnp.zeros((BACK_ROWS, LANES), jnp.float32)
@@ -276,18 +301,15 @@
         lax.fori_loop(start, end, body, 0)
         return carry
 
-    lax.fori_loop(0, count, slot, 0)
-
-    slot_logs[...] = logs_by_slot(result[2 * CH :])
+    lax.fori_loop(0, SLOTS, slot, 0)
+
+    slot_logs[...] = rows_of_quads(result[2 * CH :])
     for s in range(SLOTS):
-        first = first_of(info, s)
-        tile, at = first // LANES - TILES, lax.rem(first, LANES)
+        at = lax.rem(info[FIRST, s], LANES)
         moved = pltpu.roll(result[0 : 2 * CH], lax.rem(at + LANES - QUAD * s, LANES), 1)
-        here = (lane >= at) & (lane < jnp.where(s < count, at + QUAD, at))
-        part[tile, 0 : 2 * CH] = part[tile, 0 : 2 * CH] + jnp.where(here, moved, 0.0)
-        half = jnp.where(s < count, at // BLK, 2)
-        row = part[tile, LOG_ROW : LOG_ROW + 1]
-        part[tile, LOG_ROW : LOG_ROW + 1] = row + jnp.where(lane // BLK == half, slot_logs[s : s + 1], 0.0)
+        here = (lane >= at) & (lane < at + QUAD)
+        part[s, 0 : 2 * CH] = part[s, 0 : 2 * CH] + jnp.where(here, moved, 0.0)
+        part[s, LOG_ROW : LOG_ROW + 1] = jnp.where(info[VALID, s] > 0, slot_logs[s : s + 1], 0.0)
 
 
 def call(kernel, out_rows, scratch, scalars, *operands, mib=24):
@@ -309,7 +331,7 @@
 
 
 def pack_kernel(*refs):
-    operands, out, scratch, arrived = refs[:6], refs[6], refs[7:13], refs[13]
+    operands, out, scratch, arrived, quad_rows = refs[:6], refs[6], refs[7:13], refs[13], refs[14]
     copies = [pltpu.make_async_copy(operands[i], scratch[i], arrived.at[i]) for i in range(6)]
     for copy in copies:
         copy.start()
@@ -323,13 +345,15 @@
     for i, number in enumerate(numbers):
         meta = jnp.where(lane == i, number.astype(jnp.float32), meta)
     rows = jnp.concatenate([jnp.where(alive, times[...], DEAD), background[...], meta], axis=0)
-    rest = jnp.zeros((W_ROW - META_ROW - 1, LANES), jnp.float32)
-    chunk = jnp.concatenate(
-        [locations[:, 0, :] * SCALE, locations[:, 1, :] * SCALE, rows, rest, jnp.where(alive, weights[...], 0.0)],
-        axis=0,
-    )
+    quad_rows[0:SLOTS] = rows_of_quads(jnp.where(alive, weights[...], 0.0))
+    quad_rows[SLOTS:] = jnp.zeros((8, LANES), jnp.float32)
+    rest = jnp.zeros((ROWS - META_ROW - 1, LANES), jnp.float32)
+    chunk = jnp.concatenate([locations[:, 0, :] * SCALE, locations[:, 1, :] * SCALE, rows, rest], axis=0)
+    turn = mirrored(lax.axis_index("grp"))
     for to in range(TILES):
         out[to] = chunk
+        quad, valid = quad_at(to ^ turn, live[0], window[0], window[1])
+        out[to, QUAD_ROW : QUAD_ROW + 1] = quad_rows[pl.ds(jnp.where(valid, quad, SLOTS), 1)]
 
 
 def pack(*operands):
@@ -340,12 +364,12 @@
         in_specs=[pl.BlockSpec(memory_space=pltpu.HBM)] * 6,
         out_specs=pl.BlockSpec(memory_space=pltpu.VMEM),
         scratch_shapes=[space(x.shape, x.dtype) for space, x in zip(spaces, operands)]
-        + [pltpu.SemaphoreType.DMA((6,))],
-        compiler_params=pltpu.CompilerParams(vmem_limit_bytes=24 * 2**20),
+        + [pltpu.SemaphoreType.DMA((6,)), pltpu.VMEM((SLOTS + 8, LANES), jnp.float32)],
+        compiler_params=pltpu.CompilerParams(vmem_limit_bytes=60 * 2**20),
     )(*operands)
 
 
-def collect_kernel(info, received, grad, logs, log_rows):
+def collect_kernel(window, live, received, grad, logs, log_rows):
     log_rows[...] = jnp.zeros((LANES, LANES), jnp.float32)
     total = received[0, 0 : 2 * CH]
     log_rows[0:1] = received[0, LOG_ROW : LOG_ROW + 1]
@@ -354,18 +378,17 @@
         log_rows[source : source + 1] = received[source, LOG_ROW : LOG_ROW + 1]
     grad[:, 0, :] = total[0:CH]
     grad[:, 1, :] = total[CH:]
-    row = lax.broadcasted_iota(jnp.int32, (LANES, LANES), 0)
-    lane = lax.broadcasted_iota(jnp.int32, (LANES, LANES), 1)
-    number = jnp.where(lane < BLK, info[BEFORE, 0], info[BEFORE, 1]) + (lane % BLK) // QUAD
-    source = (number - HALF * ((number // TILES) % 2)) % TILES
-    chosen = exact_dot(jnp.transpose(log_rows[...]), (row == source).astype(jnp.float32))
-    chosen = jnp.where((row // BLK == lane // BLK) & (row % QUAD == lane % QUAD), chosen, 0.0)
-    chain = lax.broadcasted_iota(jnp.int32, (CH, LANES), 0)
-    place = lax.broadcasted_iota(jnp.int32, (CH, LANES), 1)
-    logs[...] = exact_dot(((place % BLK) // QUAD == chain).astype(jnp.float32), chosen)
-
-
-def collect(info, received):
+    first, ahead, behind = deal(live[0], window[0], window[1])
+    lane = lane_ids()
+    quad = (lane % BLK) // QUAD
+    sooner = lane // BLK == first
+    valid = quad < jnp.where(sooner, ahead, behind)
+    place = jnp.where(sooner, quad, quad + ahead)
+    source = place ^ mirrored(lax.axis_index("grp"))
+    logs[...] = place_quads(log_rows[...], jnp.where(valid, source, -1))
+
+
+def collect(window, live, received):
     vmem = pl.BlockSpec(memory_space=pltpu.VMEM)
     return pl.pallas_call(
         collect_kernel,
@@ -373,16 +396,19 @@
             jax.ShapeDtypeStruct((CH, 2, LANES), jnp.float32),
             jax.ShapeDtypeStruct((CH, LANES), jnp.float32),
         ],
-        in_specs=[pl.BlockSpec(memory_space=pltpu.SMEM), vmem],
+        in_specs=[pl.BlockSpec(memory_space=pltpu.SMEM)] * 2 + [vmem],
         out_specs=[vmem] * 2,
         scratch_shapes=[pltpu.VMEM((LANES, LANES), jnp.float32)],
         compiler_params=pltpu.CompilerParams(vmem_limit_bytes=24 * 2**20),
-    )(info, received)
+    )(window, live, received)
 
 
 def own_sums(info, own):
     return call(
-        own_sums_kernel, [(ROWS, LANES), (3 * CH, LANES), CHILD_B, (LANES, LANES)], [LOG_T, SUMS, TIMES], (info,), own
+        own_sums_kernel,
+        [(ROWS + CH, LANES), (3 * CH, LANES), CHILD_B, (LANES, LANES)],
+        [LOG_T, SUMS, TIMES, (LANES, LANES)],
+        (info,), own,
     )
 
 
@@ -405,37 +431,26 @@
 
 
 def plan(meta, me, no_prev):
-    blocks = 2 * TILES
-    block = jnp.arange(blocks, dtype=jnp.int32)
-    rounds = jnp.arange(SLOTS, dtype=jnp.int32)
-    live = jnp.repeat(meta[:, 0], 2).astype(jnp.int32)
-    window = meta[:, 1:3].reshape(-1).astype(jnp.int32)
+    live, first_window, second_window = [meta[:, i].astype(jnp.int32) for i in range(3)]
+    tile = jnp.arange(TILES, dtype=jnp.int32)
+    quad, valid = quad_at(me ^ mirrored(tile), live, first_window, second_window)
+    window = jnp.where(quad < BLK // QUAD, first_window, second_window)
     low = jnp.maximum(window * BLK, jnp.where(no_prev, TILES * LANES, 0))
-    quads = jnp.clip((live - BLK * (block % 2) + QUAD - 1) // QUAD, 0, BLK // QUAD)
-    key = (low - block * BLK) * blocks + block
-    before = jnp.sum(jnp.where(key[:, None] < key[None, :], quads[:, None], 0), axis=0)
-    number = rounds * TILES + (me + TILES // 2 * (rounds % 2)) % TILES
-    offset = number[:, None] - before[None, :]
-    mine = (offset >= 0) & (offset < quads[None, :])
-    first = TILES * LANES + block[None, :] * BLK + QUAD * offset
-    own_block = block[None, :] == 2 * me + rounds[:, None] % 2
-    every = [jnp.broadcast_to(value[None, :], first.shape) for value in (low, before)]
-    values = jnp.stack([jnp.ones_like(first), first, *every])
-    mine = jnp.stack([mine, mine, mine, own_block])
-    return jnp.sum(jnp.where(mine, values, 0), axis=2)
+    first = (TILES + tile) * LANES + QUAD * quad
+    return jnp.stack([valid.astype(jnp.int32), first, jnp.where(valid, low, 2 * TILES * LANES)])
 
 
 def per_device(locations, times, background, weights, window_start, live):
     sent = pack(window_start, live, locations, times[None], background[None], weights)
     own = lax.all_to_all(sent, "grp", 0, 0)
-    prev = from_behind(own[:, 0:W_ROW], "tm", 1)
+    prev = from_behind(own, "tm", 1)
     info = plan(own[:, META_ROW, 0:3], lax.axis_index("grp").astype(jnp.int32), lax.axis_index("tm") == 0)
     packed, collected, child_b, child_t = own_sums(info, own)
     part_prev, result, ratio = prev_pairs(info, prev, packed, collected, child_b, child_t)
     back = from_behind(part_prev, "tm", -1)
     part_own = own_push(info, own, result, ratio, child_b, child_t)
     part = jnp.concatenate([part_own[:, 0 : 2 * CH] + back, part_own[:, 2 * CH :]], axis=1)
-    grad, log_intensity = collect(info, lax.all_to_all(part, "grp", 0, 0))
+    grad, log_intensity = collect(window_start, live, lax.all_to_all(part, "grp", 0, 0))
     return (grad, log_intensity)
 
 

time: 108 us -> 100 us (0.926)
  the two profiles are of different devices: /device:TPU:9 before, /device:TPU:32 now
where the time goes in v6:
time: 100 us
  Pallas kernels  33.6 us (34%)
  blocking collectives  24.2 us (24%)
  waiting for transfers between devices  21.9 us (22%)
  starting transfers between devices  18.7 us (19%)
  between operations  1.41 us (1%)
    pallas_call x3, Pallas kernels, call(): pl.pallas_call(kernel, out_shape=[jax.ShapeDtypeStruct(shape, jnp.float32...  29.6 us
    all_to_all x1, blocking collectives, per_device(): lax.all_to_all(part, 'grp', 0, 0)  24.2 us
    all_to_all x1, waiting for transfers between devices, per_device(): own = lax.all_to_all(sent, 'grp', 0, 0)  20.2 us
    all_to_all x1, starting transfers between devices, per_device(): own = lax.all_to_all(sent, 'grp', 0, 0)  13.2 us
    ppermute x2, starting transfers between devices, from_behind(): return lax.ppermute(value, axis, pairs)  5.49 us
    pallas_call x1, Pallas kernels, pack(): pl.pallas_call(pack_kernel, out_shape=jax.ShapeDtypeStruct((TILES, ROWS,...  2.26 us
  transfers between devices with their start and end apart: 3, of which 2 were waited for; matrix products, arithmetic and copies ran while one was open for 0% of the time, Pallas kernels for 19%

profile of v6, /device:TPU:32, one launch (start us, length us, event | category | flops | bytes accessed | tf_op | source)
XLA Modules:
  0.0 100.0 jit_solution(17322253395885498339)
XLA Ops:
  1.3 2.3 %shard_map.77 = f32[32,40,128]{2,1,0:T(8,128)} custom-call(s32[2]{0:T(128)} %window.1, s32[1]{0:T(128)S(6)} %copy.9.refs_1_.live, f32[16,2,128]{2,1,0:T(2,128)} %refs_2_.1, f32[1,128]{1,0:T(1,128)} %bitcast.50, f32[1,128]{1,0:T(1,128)} %bitcast.51, f32[16,128]{1,0:T(8,128)} %refs_5_.1), custom_call_target="tpu_custom_call" | custom-call | tf_op jit(solution)/shard_map/pallas_call | solution.py:361
  3.5 13.2 %all-to-all-start = ((f32[32,40,128]{2,1,0:T(8,128)}), f32[32,40,128]{2,1,0:T(8,128)S(1)}, u32[]{:S(2)}, u32[]{:S(2)}) async-start(f32[32,40,128]{2,1,0:T(8,128)} %shard_map.77), calls=%async_computation | async-start | bytes 1310720 | tf_op jit(solution)/shard_map/all_to_all | solution.py:445
  16.7 20.2 %all-to-all-done.own = f32[32,40,128]{2,1,0:T(8,128)S(1)} async-done(((f32[32,40,128]{2,1,0:T(8,128)}), f32[32,40,128]{2,1,0:T(8,128)S(1)}, u32[]{:S(2)}, u32[]{:S(2)}) %all-to-all-start) | async-done | bytes 655392 | tf_op jit(solution)/shard_map/all_to_all | solution.py:445
  36.9 0.1 copy.8
  37.0 1.9 %collective-permute-start = (f32[32,40,128]{2,1,0:T(8,128)S(1)}, f32[32,40,128]{2,1,0:T(8,128)S(1)}, u32[]{:S(2)}, u32[]{:S(2)}) collective-permute-start(f32[32,40,128]{2,1,0:T(8,128)S(1)} %all-to-all-done.own), channel_id=1, source_target_pairs={{0,32},{32,64},{64,96},{96,128},{128,160},{160,192},{192,224},{224... | collective-permute-start | bytes 1966088 | tf_op jit(solution)/shard_map/ppermute | solution.py:40
  39.0 9.4 %shard_map.78 = (f32[56,128]{1,0:T(8,128)S(1)}, f32[48,128]{1,0:T(8,128)S(1)}, f32[128,32,128]{2,1,0:T(8,128)S(1)}, f32[128,128]{1,0:T(8,128)S(1)}) custom-call(s32[3,32]{1,0:T(4,128)S(1)} %pad_add_fusion.info, f32[32,40,128]{2,1,0:T(8,128)S(1)} %all-to-all-done.own), custom_call_target="tpu_custom_call" | custom-call | tf_op jit(solution)/shard_map/pallas_call | solution.py:317
  48.5 1.7 %collective-permute-done.prev = f32[32,40,128]{2,1,0:T(8,128)S(1)} collective-permute-done((f32[32,40,128]{2,1,0:T(8,128)S(1)}, f32[32,40,128]{2,1,0:T(8,128)S(1)}, u32[]{:S(2)}, u32[]{:S(2)}) %collective-permute-start) | collective-permute-done | bytes 655392 | tf_op jit(solution)/shard_map/ppermute | solution.py:40
  50.1 10.7 %shard_map.79 = (f32[32,32,128]{2,1,0:T(8,128)S(1)}, f32[48,128]{1,0:T(8,128)S(1)}, f32[16,128]{1,0:T(8,128)S(1)}) custom-call(s32[3,32]{1,0:T(4,128)S(1)} %pad_add_fusion.info, f32[32,40,128]{2,1,0:T(8,128)S(1)} %collective-permute-done.prev, f32[56,128]{1,0:T(8,128)S(1)} %get-tuple-element.9.packed, f32[48,128]{1,0:T(8,128)S(1)} %get-tuple-element.10.own_sums, ...), custom_call_target="tpu_custom_call" | custom-call | tf_op jit(solution)/shard_map/pallas_call | solution.py:317
  60.9 3.6 %collective-permute-start.1 = (f32[32,32,128]{2,1,0:T(8,128)S(1)}, f32[32,32,128]{2,1,0:T(8,128)S(1)}, u32[]{:S(2)}, u32[]{:S(2)}) collective-permute-start(f32[32,32,128]{2,1,0:T(8,128)S(1)} %get-tuple-element.15), channel_id=1, source_target_pairs={{32,0},{64,32},{96,64},{128,96},{160,128},{192,160},{224,192},{256... | collective-permute-start | bytes 1572872 | tf_op jit(solution)/shard_map/ppermute | solution.py:40
  64.5 9.5 %shard_map.80 = f32[32,40,128]{2,1,0:T(8,128)S(1)} custom-call(s32[3,32]{1,0:T(4,128)S(1)} %pad_add_fusion.info, f32[32,40,128]{2,1,0:T(8,128)S(1)} %all-to-all-done.own, f32[48,128]{1,0:T(8,128)S(1)} %get-tuple-element.13.result, f32[16,128]{1,0:T(8,128)S(1)} %get-tuple-element.14.ratio, f32[128,32,128]{2,1,0:T(8,128)S(1)} %get-tuple-element.11.child_b, ...), custom_call_target="tpu_custom_call" | custom-call | tf_op jit(solution)/shard_map/pallas_call | solution.py:317
  74.0 0.0 copy-start
  74.0 0.0 collective-permute-done.1
  74.0 0.1 slice_add_fusion
  74.1 24.2 %all_to_all.10.received = f32[32,40,128]{2,1,0:T(8,128)S(1)} all-to-all(f32[32,40,128]{2,1,0:T(8,128)S(1)} %pad_maximum_fusion), channel_id=1, replica_groups=mesh['tm'=16,'grp'=32] {'grp'}, dimensions={0} | all-to-all | bytes 1310720 | tf_op jit(solution)/shard_map/all_to_all | solution.py:453
  98.4 0.0 copy-done
  98.4 1.7 %shard_map.81 = (f32[16,2,128]{2,1,0:T(2,128)}, f32[16,128]{1,0:T(8,128)}) custom-call(s32[2]{0:T(128)S(1)} %copy-done, s32[1]{0:T(128)S(6)} %copy.9.refs_1_.live, f32[32,40,128]{2,1,0:T(8,128)S(1)} %all_to_all.10.received), custom_call_target="tpu_custom_call" | custom-call | tf_op jit(solution)/shard_map/pallas_call | solution.py:393
  (7 shorter events, 0.1 us)
Async XLA Ops:
  3.5 33.4 %all-to-all-start = ((f32[32,40,128]{2,1,0:T(8,128)}), f32[32,40,128]{2,1,0:T(8,128)S(1)}, u32[]{:S(2)}, u32[]{:S(2)}) async-start(f32[32,40,128]{2,1,0:T(8,128)} %shard_map.77), calls=%async_computation | async-start | bytes 1310720 | tf_op jit(solution)/shard_map/all_to_all | solution.py:445
  37.0 13.1 %collective-permute-start = (f32[32,40,128]{2,1,0:T(8,128)S(1)}, f32[32,40,128]{2,1,0:T(8,128)S(1)}, u32[]{:S(2)}, u32[]{:S(2)}) collective-permute-start(f32[32,40,128]{2,1,0:T(8,128)S(1)} %all-to-all-done.own), channel_id=1, source_target_pairs={{0,32},{32,64},{64,96},{96,128},{128,160},{160,192},{192,224},{224... | collective-permute-start | bytes 1966088 | tf_op jit(solution)/shard_map/ppermute | solution.py:40
  60.9 13.1 %collective-permute-start.1 = (f32[32,32,128]{2,1,0:T(8,128)S(1)}, f32[32,32,128]{2,1,0:T(8,128)S(1)}, u32[]{:S(2)}, u32[]{:S(2)}) collective-permute-start(f32[32,32,128]{2,1,0:T(8,128)S(1)} %get-tuple-element.15), channel_id=1, source_target_pairs={{32,0},{64,32},{96,64},{128,96},{160,128},{192,160},{224,192},{256... | collective-permute-start | bytes 1572872 | tf_op jit(solution)/shard_map/ppermute | solution.py:40
  74.0 24.4 %copy-start = (s32[2]{0:T(128)S(1)}, s32[2]{0:T(128)}, u32[]{:S(2)}) copy-start(s32[2]{0:T(128)} %window.1) | copy-start | bytes 28

commit v7 on v6

--- a/solution.py
+++ b/solution.py
@@ -21,12 +21,14 @@
 
 HALF = TILES // 2
 
-TIME_ROW, BACK_ROW, META_ROW, QUAD_ROW = range(2 * CH, 2 * CH + 4)
-ROWS = 40
-W_ROW = ROWS
+TIME_ROW, QUAD_ROW = 2 * CH, 2 * CH + 1
+ROWS = 2 * CH + 2
+META_LANE = (CH + 1) * QUAD
+BACK_ROW, W_ROW = TIME_ROW + 1, 40
 VALID, FIRST, LOW = range(3)
 LOG_ROW = 2 * CH
-BACK_ROWS = LOG_ROW + 8
+BACK_ROWS = LOG_ROW + 1
+PLACED = 24
 
 SCALE = math.sqrt(0.5 / math.log(2.0))
 UNSCALE = 1.0 / SCALE
@@ -86,9 +88,10 @@
     return jnp.where(valid, block * (BLK // QUAD) + place - later * ahead, 0), valid
 
 
-def set_times(times_q, tiles):
+def unpack_tiles(flat, tiles, times_q):
     for q in range(TILES):
-        times_q[q : q + 1] = tiles[q, TIME_ROW : TIME_ROW + 1]
+        tiles[q] = flat[ROWS * q : ROWS * q + 2 * CH]
+        times_q[q : q + 1] = flat[ROWS * q + TIME_ROW : ROWS * q + TIME_ROW + 1]
 
 
 def time_rows(info, s, log_t, child_t, times_q, own):
@@ -146,7 +149,7 @@
 
 
 def rows_of_quads(values):
-    wide = jnp.concatenate([values, jnp.zeros((LANES - CH, LANES), jnp.float32)], axis=0)
+    wide = jnp.concatenate([values, jnp.zeros((LANES - values.shape[0], LANES), jnp.float32)], axis=0)
     row, lane = square()
     by_lane = exact_dot(jnp.transpose(wide), (lane // QUAD == row).astype(jnp.float32))
     by_lane = jnp.where(lane % QUAD == row % QUAD, by_lane, 0.0)
@@ -159,24 +162,29 @@
     row, lane = square()
     chosen = exact_dot(jnp.transpose(rows), (row == source).astype(jnp.float32))
     chosen = jnp.where(row % QUAD == lane % QUAD, chosen, 0.0)
-    chain = lax.broadcasted_iota(jnp.int32, (CH, LANES), 0)
-    place = lax.broadcasted_iota(jnp.int32, (CH, LANES), 1)
+    chain = lax.broadcasted_iota(jnp.int32, (PLACED, LANES), 0)
+    place = lax.broadcasted_iota(jnp.int32, (PLACED, LANES), 1)
     return exact_dot((place // QUAD == chain).astype(jnp.float32), chosen)
 
 
-def own_sums_kernel(info, own, packed, collected, child_b, child_t, log_t, sums, times_q, quad_rows):
+def own_sums_kernel(info, flat, packed, collected, child_b, child_t, own, times_q, log_t, sums, quad_rows):
     lane = lane_ids()
-    mine = jnp.zeros((ROWS, LANES), jnp.float32)
+    unpack_tiles(flat, own, times_q)
+    mine = jnp.zeros((2 * CH, LANES), jnp.float32)
+    child_times = jnp.zeros((1, LANES), jnp.float32)
     quad_rows[...] = jnp.zeros((LANES, LANES), jnp.float32)
     for s in range(SLOTS):
         shift = lax.rem(QUAD * s + LANES - lax.rem(info[FIRST, s], LANES), LANES)
         mine = jnp.where(slot_lanes(lane, s), pltpu.roll(own[s], shift, 1), mine)
-        quad_rows[s : s + 1] = own[s, QUAD_ROW : QUAD_ROW + 1]
-    packed[0:ROWS] = mine
-    packed[W_ROW:] = place_quads(quad_rows[...], lane // QUAD)
-    spread_lanes(child_b, mine[0 : 2 * CH])
-    child_t[...] = jnp.transpose(jnp.broadcast_to(mine[TIME_ROW : TIME_ROW + 1], (LANES, LANES)))
-    set_times(times_q, own)
+        child_times = jnp.where(slot_lanes(lane, s), pltpu.roll(times_q[s : s + 1], shift, 1), child_times)
+        quad_rows[s : s + 1] = flat[ROWS * s + QUAD_ROW : ROWS * s + QUAD_ROW + 1]
+    placed = place_quads(quad_rows[...], lane // QUAD)
+    packed[0 : 2 * CH] = mine
+    packed[TIME_ROW : TIME_ROW + 1] = child_times
+    packed[BACK_ROW : BACK_ROW + 1] = placed[CH : CH + 1]
+    packed[W_ROW:] = placed[0:CH]
+    spread_lanes(child_b, mine)
+    child_t[...] = jnp.transpose(jnp.broadcast_to(child_times, (LANES, LANES)))
 
     def times(s, carry):
         @pl.when(info[VALID, s] > 0)
@@ -198,10 +206,10 @@
 
 
 def prev_kernel(
-    info, prev, packed, own_sums, child_b, child_t, part, result, ratio_out,
-    log_t, kern, sums, total, times_q
+    info, flat, packed, own_sums, child_b, child_t, part, result, ratio_out,
+    log_t, kern, sums, total, times_q, prev
 ):
-    set_times(times_q, prev)
+    unpack_tiles(flat, prev, times_q)
 
     def times(s, carry):
         @pl.when(info[LOW, s] < TILES * LANES)
@@ -252,20 +260,17 @@
 
     lax.fori_loop(0, SLOTS, push, 0)
 
-    def finish(q, carry):
+    for q in range(TILES):
         weight = total[q, 0:CH]
         for j in range(2):
-            at = slice(j * CH, (j + 1) * CH)
-            part[q, at] = (total[q, (j + 1) * CH : (j + 2) * CH] - prev[q, at] * weight) * UNSCALE
-        return carry
-
-    lax.fori_loop(0, TILES, finish, 0)
-
-
-def own_push_kernel(info, own, result, ratio, child_b, child_t, part, log_t, ratio_b, times_q, slot_logs):
+            pulled = total[q, (j + 1) * CH : (j + 2) * CH] - prev[q, j * CH : (j + 1) * CH] * weight
+            part[BACK_ROWS * q + j * CH : BACK_ROWS * q + (j + 1) * CH] = pulled * UNSCALE
+        part[BACK_ROWS * q + LOG_ROW : BACK_ROWS * (q + 1)] = jnp.zeros((1, LANES), jnp.float32)
+
+
+def own_push_kernel(info, own, times_q, result, ratio, child_b, child_t, flat, log_t, ratio_b, part, slot_logs):
     lane = lane_ids()
     spread_lanes(ratio_b, ratio[...] * -UNSCALE)
-    set_times(times_q, own)
 
     def times(s, carry):
         @pl.when(info[VALID, s] > 0)
@@ -277,7 +282,7 @@
     lax.fori_loop(0, SLOTS, times, 0)
 
     def clear(q, carry):
-        part[q] = jnp.zeros((BACK_ROWS, LANES), jnp.float32)
+        part[q] = jnp.zeros((2 * CH, LANES), jnp.float32)
         return carry
 
     lax.fori_loop(0, TILES, clear, 0)
@@ -308,8 +313,9 @@
         at = lax.rem(info[FIRST, s], LANES)
         moved = pltpu.roll(result[0 : 2 * CH], lax.rem(at + LANES - QUAD * s, LANES), 1)
         here = (lane >= at) & (lane < at + QUAD)
-        part[s, 0 : 2 * CH] = part[s, 0 : 2 * CH] + jnp.where(here, moved, 0.0)
-        part[s, LOG_ROW : LOG_ROW + 1] = jnp.where(info[VALID, s] > 0, slot_logs[s : s + 1], 0.0)
+        at = BACK_ROWS * s
+        flat[at : at + 2 * CH] = part[s] + jnp.where(here, moved, 0.0)
+        flat[at + LOG_ROW : at + BACK_ROWS] = jnp.where(info[VALID, s] > 0, slot_logs[s : s + 1], 0.0)
 
 
 def call(kernel, out_rows, scratch, scalars, *operands, mib=24):
@@ -325,6 +331,7 @@
 
 
 TIMES = (TILES, LANES)
+XY = (TILES, 2 * CH, LANES)
 LOG_T = (LANES, TILES, LANES)
 CHILD_B = (LANES, 2 * CH, LANES)
 SUMS = (LANES, 3 * CH, LANES)
@@ -340,27 +347,29 @@
     window, live, locations, times, background, weights = scratch
     lane = lane_ids()
     alive = lane < live[0]
-    numbers = (live[0], window[0], window[1])
     meta = jnp.zeros((1, LANES), jnp.float32)
-    for i, number in enumerate(numbers):
-        meta = jnp.where(lane == i, number.astype(jnp.float32), meta)
-    rows = jnp.concatenate([jnp.where(alive, times[...], DEAD), background[...], meta], axis=0)
-    quad_rows[0:SLOTS] = rows_of_quads(jnp.where(alive, weights[...], 0.0))
-    quad_rows[SLOTS:] = jnp.zeros((8, LANES), jnp.float32)
-    rest = jnp.zeros((ROWS - META_ROW - 1, LANES), jnp.float32)
-    chunk = jnp.concatenate([locations[:, 0, :] * SCALE, locations[:, 1, :] * SCALE, rows, rest], axis=0)
+    for i, number in enumerate((live[0], window[0], window[1])):
+        meta = jnp.where(lane == META_LANE + i, number.astype(jnp.float32), meta)
+    quad_rows[0:SLOTS] = rows_of_quads(jnp.concatenate([jnp.where(alive, weights[...], 0.0), background[...]], axis=0))
+    none = ((lane >= CH * QUAD) & (lane < META_LANE)).astype(jnp.float32)
+    quad_rows[SLOTS:] = jnp.broadcast_to(none, (8, LANES))
+    xs, ys = locations[:, 0, :] * SCALE, locations[:, 1, :] * SCALE
+    time = jnp.where(alive, times[...], DEAD)
     turn = mirrored(lax.axis_index("grp"))
     for to in range(TILES):
-        out[to] = chunk
+        at = ROWS * to
+        out[at : at + CH] = xs
+        out[at + CH : at + 2 * CH] = ys
+        out[at + TIME_ROW : at + TIME_ROW + 1] = time
         quad, valid = quad_at(to ^ turn, live[0], window[0], window[1])
-        out[to, QUAD_ROW : QUAD_ROW + 1] = quad_rows[pl.ds(jnp.where(valid, quad, SLOTS), 1)]
+        out[at + QUAD_ROW : at + ROWS] = quad_rows[pl.ds(jnp.where(valid, quad, SLOTS), 1)] + meta
 
 
 def pack(*operands):
     spaces = [pltpu.SMEM] * 2 + [pltpu.VMEM] * 4
     return pl.pallas_call(
         pack_kernel,
-        out_shape=jax.ShapeDtypeStruct((TILES, ROWS, LANES), jnp.float32),
+        out_shape=jax.ShapeDtypeStruct((TILES * ROWS, LANES), jnp.float32),
         in_specs=[pl.BlockSpec(memory_space=pltpu.HBM)] * 6,
         out_specs=pl.BlockSpec(memory_space=pltpu.VMEM),
         scratch_shapes=[space(x.shape, x.dtype) for space, x in zip(spaces, operands)]
@@ -371,11 +380,11 @@
 
 def collect_kernel(window, live, received, grad, logs, log_rows):
     log_rows[...] = jnp.zeros((LANES, LANES), jnp.float32)
-    total = received[0, 0 : 2 * CH]
-    log_rows[0:1] = received[0, LOG_ROW : LOG_ROW + 1]
-    for source in range(1, TILES):
-        total = total + received[source, 0 : 2 * CH]
-        log_rows[source : source + 1] = received[source, LOG_ROW : LOG_ROW + 1]
+    total = jnp.zeros((2 * CH, LANES), jnp.float32)
+    for source in range(TILES):
+        at = BACK_ROWS * source
+        total = total + received[at : at + 2 * CH]
+        log_rows[source : source + 1] = received[at + LOG_ROW : at + BACK_ROWS]
     grad[:, 0, :] = total[0:CH]
     grad[:, 1, :] = total[CH:]
     first, ahead, behind = deal(live[0], window[0], window[1])
@@ -385,7 +394,7 @@
     valid = quad < jnp.where(sooner, ahead, behind)
     place = jnp.where(sooner, quad, quad + ahead)
     source = place ^ mirrored(lax.axis_index("grp"))
-    logs[...] = place_quads(log_rows[...], jnp.where(valid, source, -1))
+    logs[...] = place_quads(log_rows[...], jnp.where(valid, source, -1))[0:CH]
 
 
 def collect(window, live, received):
@@ -403,20 +412,20 @@
     )(window, live, received)
 
 
-def own_sums(info, own):
+def own_sums(info, flat):
     return call(
         own_sums_kernel,
-        [(ROWS + CH, LANES), (3 * CH, LANES), CHILD_B, (LANES, LANES)],
-        [LOG_T, SUMS, TIMES, (LANES, LANES)],
-        (info,), own,
+        [(W_ROW + CH, LANES), (3 * CH, LANES), CHILD_B, (LANES, LANES), XY, TIMES],
+        [LOG_T, SUMS, (LANES, LANES)],
+        (info,), flat,
     )
 
 
 def prev_pairs(info, *operands):
     return call(
         prev_kernel,
-        [(TILES, 2 * CH, LANES), (3 * CH, LANES), (CH, LANES)],
-        [LOG_T, (LANES, TILES, CH, LANES), SUMS, (TILES, 3 * CH, LANES), TIMES],
+        [(TILES * BACK_ROWS, LANES), (3 * CH, LANES), (CH, LANES)],
+        [LOG_T, (LANES, TILES, CH, LANES), SUMS, (TILES, 3 * CH, LANES), TIMES, XY],
         (info,), *operands, mib=48,
     )
 
@@ -424,8 +433,8 @@
 def own_push(info, *operands):
     return call(
         own_push_kernel,
-        [(TILES, BACK_ROWS, LANES)],
-        [LOG_T, (LANES, CH, LANES), TIMES, (SLOTS, LANES)],
+        [(TILES * BACK_ROWS, LANES)],
+        [LOG_T, (LANES, CH, LANES), XY, (SLOTS, LANES)],
         (info,), *operands,
     )[0]
 
@@ -442,15 +451,17 @@
 
 def per_device(locations, times, background, weights, window_start, live):
     sent = pack(window_start, live, locations, times[None], background[None], weights)
-    own = lax.all_to_all(sent, "grp", 0, 0)
-    prev = from_behind(own, "tm", 1)
-    info = plan(own[:, META_ROW, 0:3], lax.axis_index("grp").astype(jnp.int32), lax.axis_index("tm") == 0)
-    packed, collected, child_b, child_t = own_sums(info, own)
+    own = lax.all_to_all(sent.reshape(TILES, ROWS // 2, 2, LANES), "grp", 0, 0)
+    flat = own.reshape(TILES * ROWS, LANES)
+    prev = from_behind(flat, "tm", 1)
+    meta = own[:, QUAD_ROW // 2, QUAD_ROW % 2, META_LANE : META_LANE + 3]
+    info = plan(meta, lax.axis_index("grp").astype(jnp.int32), lax.axis_index("tm") == 0)
+    packed, collected, child_b, child_t, tiles, times_q = own_sums(info, flat)
     part_prev, result, ratio = prev_pairs(info, prev, packed, collected, child_b, child_t)
     back = from_behind(part_prev, "tm", -1)
-    part_own = own_push(info, own, result, ratio, child_b, child_t)
-    part = jnp.concatenate([part_own[:, 0 : 2 * CH] + back, part_own[:, 2 * CH :]], axis=1)
-    grad, log_intensity = collect(window_start, live, lax.all_to_all(part, "grp", 0, 0))
+    part = own_push(info, tiles, times_q, result, ratio, child_b, child_t) + back
+    received = lax.all_to_all(part.reshape(TILES, BACK_ROWS, 1, LANES), "grp", 0, 0)
+    grad, log_intensity = collect(window_start, live, received.reshape(TILES * BACK_ROWS, LANES))
     return (grad, log_intensity)
 
 

time: 100 us -> 95.8 us (0.958)
  the two profiles are of different devices: /device:TPU:32 before, /device:TPU:17 now
where the time goes in v7:
time: 95.8 us; the launch traced here: 95.4 us
  Pallas kernels  33 us (34%)
  blocking collectives  23.6 us (25%)
  starting transfers between devices  20.4 us (21%)
  waiting for transfers between devices  16.8 us (18%)
  between operations  1.4 us (1%)
    pallas_call x3, Pallas kernels, call(): pl.pallas_call(kernel, out_shape=[jax.ShapeDtypeStruct(shape, jnp.float32...  29.1 us
    all_to_all x1, blocking collectives, per_device(): lax.all_to_all(part.reshape(TILES, BACK_ROWS, 1, LANES), 'grp', 0, 0)  23.6 us
    all_to_all x1, waiting for transfers between devices, per_device(): own = lax.all_to_all(sent.reshape(TILES, ROWS // 2, 2, LANES), 'grp', 0, 0)  16.8 us
    all_to_all x1, starting transfers between devices, per_device(): own = lax.all_to_all(sent.reshape(TILES, ROWS // 2, 2, LANES), 'grp', 0, 0)  12.9 us
    ppermute x2, starting transfers between devices, from_behind(): return lax.ppermute(value, axis, pairs)  7.47 us
    pallas_call x1, Pallas kernels, pack(): pl.pallas_call(pack_kernel, out_shape=jax.ShapeDtypeStruct((TILES * ROWS,...  2.23 us
  transfers between devices with their start and end apart: 3, of which 1 were waited for; matrix products, arithmetic and copies ran while one was open for 0% of the time, Pallas kernels for 21%

profile of v7, /device:TPU:17, one launch (start us, length us, event | category | flops | bytes accessed | tf_op | source)
XLA Modules:
  0.0 95.4 jit_solution(11904296096569473409)
XLA Ops:
  1.3 2.2 %shard_map.77 = f32[1088,128]{1,0:T(8,128)} custom-call(s32[2]{0:T(128)} %window.1, s32[1]{0:T(128)S(6)} %copy.14.refs_1_.live, f32[16,2,128]{2,1,0:T(2,128)} %refs_2_.1, f32[1,128]{1,0:T(1,128)} %bitcast.59, f32[1,128]{1,0:T(1,128)} %bitcast.60, f32[16,128]{1,0:T(8,128)} %refs_5_.1), custom_call_target="tpu_custom_call" | custom-call | tf_op jit(solution)/shard_map/pallas_call | solution.py:370
  3.5 12.9 %all-to-all-start = ((f32[32,17,2,128]{3,2,1,0:T(2,128)}), f32[32,17,2,128]{3,2,1,0:T(2,128)S(1)}, u32[]{:S(2)}, u32[]{:S(2)}) async-start(f32[32,17,2,128]{3,2,1,0:T(2,128)} %bitcast.54), calls=%async_computation | async-start | bytes 1114112 | tf_op jit(solution)/shard_map/all_to_all | solution.py:454
  16.4 16.8 %all-to-all-done = f32[32,17,2,128]{3,2,1,0:T(2,128)S(1)} async-done(((f32[32,17,2,128]{3,2,1,0:T(2,128)}), f32[32,17,2,128]{3,2,1,0:T(2,128)S(1)}, u32[]{:S(2)}, u32[]{:S(2)}) %all-to-all-start) | async-done | bytes 557088 | tf_op jit(solution)/shard_map/all_to_all | solution.py:454
  33.3 0.1 slice.16
  33.4 0.1 copy.12
  33.4 5.5 %collective-permute-start = (f32[1088,128]{1,0:T(8,128)S(1)}, f32[1088,128]{1,0:T(8,128)S(1)}, u32[]{:S(2)}, u32[]{:S(2)}) collective-permute-start(f32[1088,128]{1,0:T(8,128)S(1)} %bitcast.51), channel_id=1, source_target_pairs={{0,32},{32,64},{64,96},{96,128},{128,160},{160,192},{192,224},{224... | collective-permute-start | bytes 1671176 | tf_op jit(solution)/shard_map/ppermute | solution.py:42
  39.1 10.2 %shard_map.78 = (f32[56,128]{1,0:T(8,128)S(1)}, f32[48,128]{1,0:T(8,128)S(1)}, f32[128,32,128]{2,1,0:T(8,128)S(1)}, f32[128,128]{1,0:T(8,128)S(1)}, f32[32,32,128]{2,1,0:T(8,128)S(1)}, /*index=5*/f32[32,128]{1,0:T(8,128)S(1)}) custom-call(s32[3,32]{1,0:T(4,128)S(1)} %pad_add_fusion.info, f32[1088,128]{1,0:T(8,128)S(1)} %bitcast.52), custom_call_target="tpu_custom_call" | custom-call | tf_op jit(solution)/shard_map/pallas_call | solution.py:323
  49.3 0.0 collective-permute-done.flat
  49.3 9.2 %shard_map.79 = (f32[1056,128]{1,0:T(8,128)S(1)}, f32[48,128]{1,0:T(8,128)S(1)}, f32[16,128]{1,0:T(8,128)S(1)}) custom-call(s32[3,32]{1,0:T(4,128)S(1)} %pad_add_fusion.info, f32[1088,128]{1,0:T(8,128)S(1)} %collective-permute-done.flat, f32[56,128]{1,0:T(8,128)S(1)} %get-tuple-element.13.packed, f32[48,128]{1,0:T(8,128)S(1)} %get-tuple-element.14.own_sums, ...), custom_call_target="tpu_custom_call" | custom-call | tf_op jit(solution)/shard_map/pallas_call | solution.py:323
  58.5 1.9 %collective-permute-start.1 = (f32[1056,128]{1,0:T(8,128)S(1)}, f32[1056,128]{1,0:T(8,128)S(1)}, u32[]{:S(2)}, u32[]{:S(2)}) collective-permute-start(f32[1056,128]{1,0:T(8,128)S(1)} %get-tuple-element.19), channel_id=1, source_target_pairs={{32,0},{64,32},{96,64},{128,96},{160,128},{192,160},{224,192},{256... | collective-permute-start | bytes 1622024 | tf_op jit(solution)/shard_map/ppermute | solution.py:42
  60.4 9.7 %shard_map.80 = f32[1056,128]{1,0:T(8,128)S(1)} custom-call(s32[3,32]{1,0:T(4,128)S(1)} %pad_add_fusion.info, f32[32,32,128]{2,1,0:T(8,128)S(1)} %get-tuple-element.11.own, f32[32,128]{1,0:T(8,128)S(1)} %get-tuple-element.12.times_q, f32[48,128]{1,0:T(8,128)S(1)} %get-tuple-element.17.result, f32[16,128]{1,0:T(8,128)S(1)} %get-tuple-element.18.ratio, ...), custom_call_target="tpu_custom_call" | custom-call | tf_op jit(solution)/shard_map/pallas_call | solution.py:323
  70.1 0.0 copy-start
  70.1 0.0 collective-permute-done.1
  70.1 0.1 add.185
  70.2 23.6 %all_to_all.10 = f32[32,33,1,128]{3,2,1,0:T(1,128)S(1)} all-to-all(f32[32,33,1,128]{3,2,1,0:T(1,128)S(1)} %bitcast.55), channel_id=1, replica_groups=mesh['tm'=16,'grp'=32] {'grp'}, dimensions={0} | all-to-all | bytes 1081344 | tf_op jit(solution)/shard_map/all_to_all | solution.py:463
  93.8 0.0 copy-done
  93.8 1.7 %shard_map.81 = (f32[16,2,128]{2,1,0:T(2,128)}, f32[16,128]{1,0:T(8,128)}) custom-call(s32[2]{0:T(128)S(1)} %copy-done, s32[1]{0:T(128)S(6)} %copy.14.refs_1_.live, f32[1056,128]{1,0:T(8,128)S(1)} %bitcast.53), custom_call_target="tpu_custom_call" | custom-call | tf_op jit(solution)/shard_map/pallas_call | solution.py:402
  (4 shorter events, 0.1 us)
Async XLA Ops:
  3.5 29.8 %all-to-all-start = ((f32[32,17,2,128]{3,2,1,0:T(2,128)}), f32[32,17,2,128]{3,2,1,0:T(2,128)S(1)}, u32[]{:S(2)}, u32[]{:S(2)}) async-start(f32[32,17,2,128]{3,2,1,0:T(2,128)} %bitcast.54), calls=%async_computation | async-start | bytes 1114112 | tf_op jit(solution)/shard_map/all_to_all | solution.py:454
  33.4 15.9 %collective-permute-start = (f32[1088,128]{1,0:T(8,128)S(1)}, f32[1088,128]{1,0:T(8,128)S(1)}, u32[]{:S(2)}, u32[]{:S(2)}) collective-permute-start(f32[1088,128]{1,0:T(8,128)S(1)} %bitcast.51), channel_id=1, source_target_pairs={{0,32},{32,64},{64,96},{96,128},{128,160},{160,192},{192,224},{224... | collective-permute-start | bytes 1671176 | tf_op jit(solution)/shard_map/ppermute | solution.py:42
  58.5 11.6 %collective-permute-start.1 = (f32[1056,128]{1,0:T(8,128)S(1)}, f32[1056,128]{1,0:T(8,128)S(1)}, u32[]{:S(2)}, u32[]{:S(2)}) collective-permute-start(f32[1056,128]{1,0:T(8,128)S(1)} %get-tuple-element.19), channel_id=1, source_target_pairs={{32,0},{64,32},{96,64},{128,96},{160,128},{192,160},{224,192},{256... | collective-permute-start | bytes 1622024 | tf_op jit(solution)/shard_map/ppermute | solution.py:42
  70.1 23.7 %copy-start = (s32[2]{0:T(128)S(1)}, s32[2]{0:T(128)}, u32[]{:S(2)}) copy-start(s32[2]{0:T(128)} %window.1) | copy-start | bytes 28

commit v8 on v7

--- a/solution.py
+++ b/solution.py
@@ -112,24 +112,43 @@
     return jnp.exp2((lt - dx * dx) - dy * dy), dx, dy
 
 
-def slot_sums(tiles, s, start, end, child_b, log_t, sums, kern=None):
-    for i in range(QUAD):
-        sums[QUAD * s + i] = jnp.zeros((3 * CH, LANES), jnp.float32)
-
-    def body(step, carry):
+def short_steps(start, end, body):
+    def once(step, carry):
+        body([2 * step, 2 * step + 1])
+        return carry
+
+    lax.fori_loop(start, end, once, 0)
+
+
+def steps(start, end, body):
+    count = jnp.maximum(end - start, 0)
+
+    def twice(i, carry):
+        tile = 2 * start + 4 * i
+        body([tile + u for u in range(4)])
+        return carry
+
+    lax.fori_loop(0, count // 2, twice, 0)
+
+    @pl.when(count % 2 == 1)
+    def _():
+        body([2 * end - 2, 2 * end - 1])
+
+
+def slot_sums(tiles, s, start, end, child_b, log_t, sums, steps, kern=None):
+    def body(qs):
         for i in range(QUAD):
             at = QUAD * s + i
-            k0, dx0, dy0 = kernel_of(tiles, 2 * step, child_b, log_t, at)
-            k1, dx1, dy1 = kernel_of(tiles, 2 * step + 1, child_b, log_t, at)
-            if kern is not None:
-                kern[at, 2 * step] = k0
-                kern[at, 2 * step + 1] = k1
-            sums[at, 0:CH] = (sums[at, 0:CH] + k0) + k1
-            sums[at, CH : 2 * CH] = (sums[at, CH : 2 * CH] + k0 * dx0) + k1 * dx1
-            sums[at, 2 * CH :] = (sums[at, 2 * CH :] + k0 * dy0) + k1 * dy1
-        return carry
-
-    lax.fori_loop(start, end, body, 0)
+            acc = [sums[at, j * CH : (j + 1) * CH] for j in range(3)]
+            for q in qs:
+                k, dx, dy = kernel_of(tiles, q, child_b, log_t, at)
+                if kern is not None:
+                    kern[at, q] = k
+                acc = [acc[0] + k, acc[1] + k * dx, acc[2] + k * dy]
+            for j in range(3):
+                sums[at, j * CH : (j + 1) * CH] = acc[j]
+
+    steps(start, end, body)
 
 
 def own_steps(info, s):
@@ -167,7 +186,7 @@
     return exact_dot((place // QUAD == chain).astype(jnp.float32), chosen)
 
 
-def own_sums_kernel(info, flat, packed, collected, child_b, child_t, own, times_q, log_t, sums, quad_rows):
+def own_sums_kernel(info, flat, packed, sums, child_b, child_t, own, times_q, log_t, quad_rows):
     lane = lane_ids()
     unpack_tiles(flat, own, times_q)
     mine = jnp.zeros((2 * CH, LANES), jnp.float32)
@@ -195,14 +214,19 @@
 
     lax.fori_loop(0, SLOTS, times, 0)
 
+    def clear(s, carry):
+        for i in range(QUAD):
+            sums[QUAD * s + i] = jnp.zeros((3 * CH, LANES), jnp.float32)
+        return carry
+
+    lax.fori_loop(0, SLOTS, clear, 0)
+
     def slot(s, carry):
         start, end = own_steps(info, s)
-        slot_sums(own, s, start, end, child_b, log_t, sums)
+        slot_sums(own, s, start, end, child_b, log_t, sums, steps)
         return carry
 
     lax.fori_loop(0, SLOTS, slot, 0)
-    for j, part in enumerate(gather_lanes(sums)):
-        collected[j * CH : (j + 1) * CH] = part
 
 
 def prev_kernel(
@@ -221,13 +245,14 @@
     lax.fori_loop(0, SLOTS, times, 0)
 
     def slot(s, carry):
-        slot_sums(prev, s, prev_start(info, s), HALF, child_b, log_t, sums, kern)
+        for i in range(QUAD):
+            sums[QUAD * s + i] = own_sums[QUAD * s + i]
+        slot_sums(prev, s, prev_start(info, s), HALF, child_b, log_t, sums, short_steps, kern)
         return carry
 
     lax.fori_loop(0, SLOTS, slot, 0)
 
-    here = gather_lanes(sums)
-    summed, pull_x, pull_y = [own_sums[j * CH : (j + 1) * CH] + here[j] for j in range(3)]
+    summed, pull_x, pull_y = gather_lanes(sums)
     xs, ys, weights = packed[0:CH], packed[CH : 2 * CH], packed[W_ROW : W_ROW + CH]
     intensity = packed[BACK_ROW : BACK_ROW + 1] + summed
     alive = packed[TIME_ROW : TIME_ROW + 1] >= 0.0
@@ -245,17 +270,15 @@
     lax.fori_loop(0, TILES, clear, 0)
 
     def push(s, carry):
-        def body(step, inner):
-            for u in range(2):
-                q = 2 * step + u
+        def body(qs):
+            for q in qs:
                 ks = [kern[QUAD * s + i, q] for i in range(QUAD)]
                 for j in range(3):
                     at = slice(j * CH, (j + 1) * CH)
                     add = [ks[i] * sums[QUAD * s + i, at] for i in range(QUAD)]
                     total[q, at] = total[q, at] + ((add[0] + add[1]) + (add[2] + add[3]))
-            return inner
-
-        lax.fori_loop(prev_start(info, s), HALF, body, 0)
+
+        short_steps(prev_start(info, s), HALF, body)
         return carry
 
     lax.fori_loop(0, SLOTS, push, 0)
@@ -290,9 +313,8 @@
     def slot(s, carry):
         start, end = own_steps(info, s)
 
-        def body(step, inner):
-            for u in range(2):
-                q = 2 * step + u
+        def body(qs):
+            for q in qs:
                 xs, ys = [], []
                 for i in range(QUAD):
                     k, dx, dy = kernel_of(own, q, child_b, log_t, QUAD * s + i)
@@ -301,9 +323,8 @@
                     ys.append(weighted * dy)
                 part[q, 0:CH] = part[q, 0:CH] + ((xs[0] + xs[1]) + (xs[2] + xs[3]))
                 part[q, CH : 2 * CH] = part[q, CH : 2 * CH] + ((ys[0] + ys[1]) + (ys[2] + ys[3]))
-            return inner
-
-        lax.fori_loop(start, end, body, 0)
+
+        steps(start, end, body)
         return carry
 
     lax.fori_loop(0, SLOTS, slot, 0)
@@ -318,7 +339,7 @@
         flat[at + LOG_ROW : at + BACK_ROWS] = jnp.where(info[VALID, s] > 0, slot_logs[s : s + 1], 0.0)
 
 
-def call(kernel, out_rows, scratch, scalars, *operands, mib=24):
+def call(kernel, out_rows, scratch, scalars, *operands, mib=8):
     vmem = pl.BlockSpec(memory_space=pltpu.VMEM)
     return pl.pallas_call(
         kernel,
@@ -415,8 +436,8 @@
 def own_sums(info, flat):
     return call(
         own_sums_kernel,
-        [(W_ROW + CH, LANES), (3 * CH, LANES), CHILD_B, (LANES, LANES), XY, TIMES],
-        [LOG_T, SUMS, (LANES, LANES)],
+        [(W_ROW + CH, LANES), SUMS, CHILD_B, (LANES, LANES), XY, TIMES],
+        [LOG_T, (LANES, LANES)],
         (info,), flat,
     )
 
@@ -426,7 +447,7 @@
         prev_kernel,
         [(TILES * BACK_ROWS, LANES), (3 * CH, LANES), (CH, LANES)],
         [LOG_T, (LANES, TILES, CH, LANES), SUMS, (TILES, 3 * CH, LANES), TIMES, XY],
-        (info,), *operands, mib=48,
+        (info,), *operands, mib=42,
     )
 
 
@@ -456,8 +477,8 @@
     prev = from_behind(flat, "tm", 1)
     meta = own[:, QUAD_ROW // 2, QUAD_ROW % 2, META_LANE : META_LANE + 3]
     info = plan(meta, lax.axis_index("grp").astype(jnp.int32), lax.axis_index("tm") == 0)
-    packed, collected, child_b, child_t, tiles, times_q = own_sums(info, flat)
-    part_prev, result, ratio = prev_pairs(info, prev, packed, collected, child_b, child_t)
+    packed, sums, child_b, child_t, tiles, times_q = own_sums(info, flat)
+    part_prev, result, ratio = prev_pairs(info, prev, packed, sums, child_b, child_t)
     back = from_behind(part_prev, "tm", -1)
     part = own_push(info, tiles, times_q, result, ratio, child_b, child_t) + back
     received = lax.all_to_all(part.reshape(TILES, BACK_ROWS, 1, LANES), "grp", 0, 0)

time: 95.8 us -> 94.2 us (0.983)
  the two profiles are of different devices: /device:TPU:17 before, /device:TPU:25 now
where the time goes in v8:
time: 94.2 us; the launch traced here: 93.9 us
  Pallas kernels  29.8 us (32%)
  blocking collectives  22 us (23%)
  starting transfers between devices  21.6 us (23%)
  waiting for transfers between devices  18.8 us (20%)
  between operations  1.39 us (1%)
    pallas_call x3, Pallas kernels, call(): pl.pallas_call(kernel, out_shape=[jax.ShapeDtypeStruct(shape, jnp.float32...  25.9 us
    all_to_all x1, blocking collectives, per_device(): lax.all_to_all(part.reshape(TILES, BACK_ROWS, 1, LANES), 'grp', 0, 0)  22 us
    all_to_all x1, waiting for transfers between devices, per_device(): own = lax.all_to_all(sent.reshape(TILES, ROWS // 2, 2, LANES), 'grp', 0, 0)  16.8 us
    all_to_all x1, starting transfers between devices, per_device(): own = lax.all_to_all(sent.reshape(TILES, ROWS // 2, 2, LANES), 'grp', 0, 0)  12.9 us
    ppermute x2, starting transfers between devices, from_behind(): return lax.ppermute(value, axis, pairs)  8.68 us
    pallas_call x1, Pallas kernels, pack(): pl.pallas_call(pack_kernel, out_shape=jax.ShapeDtypeStruct((TILES * ROWS,...  2.23 us
    ppermute x2, waiting for transfers between devices, from_behind(): return lax.ppermute(value, axis, pairs)  1.96 us
  transfers between devices with their start and end apart: 3, of which 2 were waited for; matrix products, arithmetic and copies ran while one was open for 0% of the time, Pallas kernels for 17%

profile of v8, /device:TPU:25, one launch (start us, length us, event | category | flops | bytes accessed | tf_op | source)
XLA Modules:
  0.0 93.9 jit_solution(15552633604531398107)
XLA Ops:
  1.3 2.2 %shard_map.77 = f32[1088,128]{1,0:T(8,128)} custom-call(s32[2]{0:T(128)} %window.1, s32[1]{0:T(128)S(6)} %copy.14.refs_1_.live, f32[16,2,128]{2,1,0:T(2,128)} %refs_2_.1, f32[1,128]{1,0:T(1,128)} %bitcast.59, f32[1,128]{1,0:T(1,128)} %bitcast.60, f32[16,128]{1,0:T(8,128)} %refs_5_.1), custom_call_target="tpu_custom_call" | custom-call | tf_op jit(solution)/shard_map/pallas_call | solution.py:391
  3.5 12.9 %all-to-all-start = ((f32[32,17,2,128]{3,2,1,0:T(2,128)}), f32[32,17,2,128]{3,2,1,0:T(2,128)S(1)}, u32[]{:S(2)}, u32[]{:S(2)}) async-start(f32[32,17,2,128]{3,2,1,0:T(2,128)} %bitcast.54), calls=%async_computation | async-start | bytes 1114112 | tf_op jit(solution)/shard_map/all_to_all | solution.py:475
  16.4 16.8 %all-to-all-done = f32[32,17,2,128]{3,2,1,0:T(2,128)S(1)} async-done(((f32[32,17,2,128]{3,2,1,0:T(2,128)}), f32[32,17,2,128]{3,2,1,0:T(2,128)S(1)}, u32[]{:S(2)}, u32[]{:S(2)}) %all-to-all-start) | async-done | bytes 557088 | tf_op jit(solution)/shard_map/all_to_all | solution.py:475
  33.3 0.1 slice.16
  33.4 0.1 copy.12
  33.4 6.8 %collective-permute-start = (f32[1088,128]{1,0:T(8,128)S(1)}, f32[1088,128]{1,0:T(8,128)S(1)}, u32[]{:S(2)}, u32[]{:S(2)}) collective-permute-start(f32[1088,128]{1,0:T(8,128)S(1)} %bitcast.51), channel_id=1, source_target_pairs={{0,32},{32,64},{64,96},{96,128},{128,160},{160,192},{192,224},{224... | collective-permute-start | bytes 1671176 | tf_op jit(solution)/shard_map/ppermute | solution.py:42
  40.3 8.3 %shard_map.78 = (f32[56,128]{1,0:T(8,128)S(1)}, f32[128,48,128]{2,1,0:T(8,128)S(1)}, f32[128,32,128]{2,1,0:T(8,128)S(1)}, f32[128,128]{1,0:T(8,128)S(1)}, f32[32...) custom-call(s32[3,32]{1,0:T(4,128)S(1)} %pad_add_fusion.info, f32[1088,128]{1,0:T(8,128)S(1)} %bitcast.52), custom_call_target="tpu_custom_call" | custom-call | tf_op jit(solution)/shard_map/pallas_call | solution.py:344
  48.6 0.0 collective-permute-done.flat
  48.6 9.6 %shard_map.79 = (f32[1056,128]{1,0:T(8,128)S(1)}, f32[48,128]{1,0:T(8,128)S(1)}, f32[16,128]{1,0:T(8,128)S(1)}) custom-call(s32[3,32]{1,0:T(4,128)S(1)} %pad_add_fusion.info, f32[1088,128]{1,0:T(8,128)S(1)} %collective-permute-done.flat, f32[56,128]{1,0:T(8,128)S(1)} %get-tuple-element.13.packed, f32[128,48,128]{2,1,0:T(8,128)S(1)} %get-tuple-element.14.own_sums, ...), custom_call_target="tpu_custom_call" | custom-call | tf_op jit(solution)/shard_map/pallas_call | solution.py:344
  58.2 0.0 copy-start
  58.3 1.9 %collective-permute-start.1 = (f32[1056,128]{1,0:T(8,128)S(1)}, f32[1056,128]{1,0:T(8,128)S(1)}, u32[]{:S(2)}, u32[]{:S(2)}) collective-permute-start(f32[1056,128]{1,0:T(8,128)S(1)} %get-tuple-element.19), channel_id=1, source_target_pairs={{32,0},{64,32},{96,64},{128,96},{160,128},{192,160},{224,192},{256... | collective-permute-start | bytes 1622024 | tf_op jit(solution)/shard_map/ppermute | solution.py:42
  60.2 8.0 %shard_map.80 = f32[1056,128]{1,0:T(8,128)S(1)} custom-call(s32[3,32]{1,0:T(4,128)S(1)} %pad_add_fusion.info, f32[32,32,128]{2,1,0:T(8,128)S(1)} %get-tuple-element.11.own, f32[32,128]{1,0:T(8,128)S(1)} %get-tuple-element.12.times_q, f32[48,128]{1,0:T(8,128)S(1)} %get-tuple-element.17.result, f32[16,128]{1,0:T(8,128)S(1)} %get-tuple-element.18.ratio, ...), custom_call_target="tpu_custom_call" | custom-call | tf_op jit(solution)/shard_map/pallas_call | solution.py:344
  68.2 2.0 %collective-permute-done.1 = f32[1056,128]{1,0:T(8,128)S(1)} collective-permute-done((f32[1056,128]{1,0:T(8,128)S(1)}, f32[1056,128]{1,0:T(8,128)S(1)}, u32[]{:S(2)}, u32[]{:S(2)}) %collective-permute-start.1) | collective-permute-done | bytes 540704 | tf_op jit(solution)/shard_map/ppermute | solution.py:42
  70.1 0.1 add.185
  70.2 22.0 %all_to_all.10 = f32[32,33,1,128]{3,2,1,0:T(1,128)S(1)} all-to-all(f32[32,33,1,128]{3,2,1,0:T(1,128)S(1)} %bitcast.55), channel_id=1, replica_groups=mesh['tm'=16,'grp'=32] {'grp'}, dimensions={0} | all-to-all | bytes 1081344 | tf_op jit(solution)/shard_map/all_to_all | solution.py:484
  92.2 0.0 copy-done
  92.2 1.7 %shard_map.81 = (f32[16,2,128]{2,1,0:T(2,128)}, f32[16,128]{1,0:T(8,128)}) custom-call(s32[2]{0:T(128)S(1)} %copy-done, s32[1]{0:T(128)S(6)} %copy.14.refs_1_.live, f32[1056,128]{1,0:T(8,128)S(1)} %bitcast.53), custom_call_target="tpu_custom_call" | custom-call | tf_op jit(solution)/shard_map/pallas_call | solution.py:423
  (4 shorter events, 0.1 us)
Async XLA Ops:
  3.5 29.8 %all-to-all-start = ((f32[32,17,2,128]{3,2,1,0:T(2,128)}), f32[32,17,2,128]{3,2,1,0:T(2,128)S(1)}, u32[]{:S(2)}, u32[]{:S(2)}) async-start(f32[32,17,2,128]{3,2,1,0:T(2,128)} %bitcast.54), calls=%async_computation | async-start | bytes 1114112 | tf_op jit(solution)/shard_map/all_to_all | solution.py:475
  33.4 15.1 %collective-permute-start = (f32[1088,128]{1,0:T(8,128)S(1)}, f32[1088,128]{1,0:T(8,128)S(1)}, u32[]{:S(2)}, u32[]{:S(2)}) collective-permute-start(f32[1088,128]{1,0:T(8,128)S(1)} %bitcast.51), channel_id=1, source_target_pairs={{0,32},{32,64},{64,96},{96,128},{128,160},{160,192},{192,224},{224... | collective-permute-start | bytes 1671176 | tf_op jit(solution)/shard_map/ppermute | solution.py:42
  58.2 34.0 %copy-start = (s32[2]{0:T(128)S(1)}, s32[2]{0:T(128)}, u32[]{:S(2)}) copy-start(s32[2]{0:T(128)} %window.1) | copy-start | bytes 28
  58.3 11.9 %collective-permute-start.1 = (f32[1056,128]{1,0:T(8,128)S(1)}, f32[1056,128]{1,0:T(8,128)S(1)}, u32[]{:S(2)}, u32[]{:S(2)}) collective-permute-start(f32[1056,128]{1,0:T(8,128)S(1)} %get-tuple-element.19), channel_id=1, source_target_pairs={{32,0},{64,32},{96,64},{128,96},{160,128},{192,160},{224,192},{256... | collective-permute-start | bytes 1622024 | tf_op jit(solution)/shard_map/ppermute | solution.py:42

commit v9 on v8

--- a/solution.py
+++ b/solution.py
@@ -186,7 +186,7 @@
     return exact_dot((place // QUAD == chain).astype(jnp.float32), chosen)
 
 
-def own_sums_kernel(info, flat, packed, sums, child_b, child_t, own, times_q, log_t, quad_rows):
+def own_sums_kernel(info, flat, packed, sums, child_b, child_t, own, log_t, times_q, quad_rows):
     lane = lane_ids()
     unpack_tiles(flat, own, times_q)
     mine = jnp.zeros((2 * CH, LANES), jnp.float32)
@@ -291,18 +291,9 @@
         part[BACK_ROWS * q + LOG_ROW : BACK_ROWS * (q + 1)] = jnp.zeros((1, LANES), jnp.float32)
 
 
-def own_push_kernel(info, own, times_q, result, ratio, child_b, child_t, flat, log_t, ratio_b, part, slot_logs):
+def own_push_kernel(info, own, log_t, result, ratio, child_b, flat, ratio_b, part, slot_logs):
     lane = lane_ids()
     spread_lanes(ratio_b, ratio[...] * -UNSCALE)
-
-    def times(s, carry):
-        @pl.when(info[VALID, s] > 0)
-        def _():
-            time_rows(info, s, log_t, child_t, times_q, True)
-
-        return carry
-
-    lax.fori_loop(0, SLOTS, times, 0)
 
     def clear(q, carry):
         part[q] = jnp.zeros((2 * CH, LANES), jnp.float32)
@@ -359,7 +350,7 @@
 
 
 def pack_kernel(*refs):
-    operands, out, scratch, arrived, quad_rows = refs[:6], refs[6], refs[7:13], refs[13], refs[14]
+    operands, out, source, scratch, arrived, quad_rows = refs[:6], refs[6], refs[7], refs[8:14], refs[14], refs[15]
     copies = [pltpu.make_async_copy(operands[i], scratch[i], arrived.at[i]) for i in range(6)]
     for copy in copies:
         copy.start()
@@ -384,22 +375,31 @@
         out[at + TIME_ROW : at + TIME_ROW + 1] = time
         quad, valid = quad_at(to ^ turn, live[0], window[0], window[1])
         out[at + QUAD_ROW : at + ROWS] = quad_rows[pl.ds(jnp.where(valid, quad, SLOTS), 1)] + meta
+    first, ahead, behind = deal(live[0], window[0], window[1])
+    quad = (lane % BLK) // QUAD
+    sooner = lane // BLK == first
+    valid = quad < jnp.where(sooner, ahead, behind)
+    dealt = jnp.where(valid, jnp.where(sooner, quad, quad + ahead) ^ turn, -1)
+    source[...] = jnp.broadcast_to(dealt, (8, LANES))
 
 
 def pack(*operands):
     spaces = [pltpu.SMEM] * 2 + [pltpu.VMEM] * 4
     return pl.pallas_call(
         pack_kernel,
-        out_shape=jax.ShapeDtypeStruct((TILES * ROWS, LANES), jnp.float32),
+        out_shape=[
+            jax.ShapeDtypeStruct((TILES * ROWS, LANES), jnp.float32),
+            jax.ShapeDtypeStruct((8, LANES), jnp.int32),
+        ],
         in_specs=[pl.BlockSpec(memory_space=pltpu.HBM)] * 6,
-        out_specs=pl.BlockSpec(memory_space=pltpu.VMEM),
+        out_specs=[pl.BlockSpec(memory_space=pltpu.VMEM)] * 2,
         scratch_shapes=[space(x.shape, x.dtype) for space, x in zip(spaces, operands)]
         + [pltpu.SemaphoreType.DMA((6,)), pltpu.VMEM((SLOTS + 8, LANES), jnp.float32)],
         compiler_params=pltpu.CompilerParams(vmem_limit_bytes=60 * 2**20),
     )(*operands)
 
 
-def collect_kernel(window, live, received, grad, logs, log_rows):
+def collect_kernel(dealt, received, grad, logs, log_rows):
     log_rows[...] = jnp.zeros((LANES, LANES), jnp.float32)
     total = jnp.zeros((2 * CH, LANES), jnp.float32)
     for source in range(TILES):
@@ -408,17 +408,10 @@
         log_rows[source : source + 1] = received[at + LOG_ROW : at + BACK_ROWS]
     grad[:, 0, :] = total[0:CH]
     grad[:, 1, :] = total[CH:]
-    first, ahead, behind = deal(live[0], window[0], window[1])
-    lane = lane_ids()
-    quad = (lane % BLK) // QUAD
-    sooner = lane // BLK == first
-    valid = quad < jnp.where(sooner, ahead, behind)
-    place = jnp.where(sooner, quad, quad + ahead)
-    source = place ^ mirrored(lax.axis_index("grp"))
-    logs[...] = place_quads(log_rows[...], jnp.where(valid, source, -1))[0:CH]
-
-
-def collect(window, live, received):
+    logs[...] = place_quads(log_rows[...], dealt[0:1])[0:CH]
+
+
+def collect(dealt, received):
     vmem = pl.BlockSpec(memory_space=pltpu.VMEM)
     return pl.pallas_call(
         collect_kernel,
@@ -426,18 +419,18 @@
             jax.ShapeDtypeStruct((CH, 2, LANES), jnp.float32),
             jax.ShapeDtypeStruct((CH, LANES), jnp.float32),
         ],
-        in_specs=[pl.BlockSpec(memory_space=pltpu.SMEM)] * 2 + [vmem],
+        in_specs=[vmem] * 2,
         out_specs=[vmem] * 2,
         scratch_shapes=[pltpu.VMEM((LANES, LANES), jnp.float32)],
         compiler_params=pltpu.CompilerParams(vmem_limit_bytes=24 * 2**20),
-    )(window, live, received)
+    )(dealt, received)
 
 
 def own_sums(info, flat):
     return call(
         own_sums_kernel,
-        [(W_ROW + CH, LANES), SUMS, CHILD_B, (LANES, LANES), XY, TIMES],
-        [LOG_T, (LANES, LANES)],
+        [(W_ROW + CH, LANES), SUMS, CHILD_B, (LANES, LANES), XY, LOG_T],
+        [TIMES, (LANES, LANES)],
         (info,), flat,
     )
 
@@ -455,7 +448,7 @@
     return call(
         own_push_kernel,
         [(TILES * BACK_ROWS, LANES)],
-        [LOG_T, (LANES, CH, LANES), XY, (SLOTS, LANES)],
+        [(LANES, CH, LANES), XY, (SLOTS, LANES)],
         (info,), *operands,
     )[0]
 
@@ -471,18 +464,18 @@
 
 
 def per_device(locations, times, background, weights, window_start, live):
-    sent = pack(window_start, live, locations, times[None], background[None], weights)
+    sent, dealt = pack(window_start, live, locations, times[None], background[None], weights)
     own = lax.all_to_all(sent.reshape(TILES, ROWS // 2, 2, LANES), "grp", 0, 0)
     flat = own.reshape(TILES * ROWS, LANES)
     prev = from_behind(flat, "tm", 1)
     meta = own[:, QUAD_ROW // 2, QUAD_ROW % 2, META_LANE : META_LANE + 3]
     info = plan(meta, lax.axis_index("grp").astype(jnp.int32), lax.axis_index("tm") == 0)
-    packed, sums, child_b, child_t, tiles, times_q = own_sums(info, flat)
+    packed, sums, child_b, child_t, tiles, log_t = own_sums(info, flat)
     part_prev, result, ratio = prev_pairs(info, prev, packed, sums, child_b, child_t)
     back = from_behind(part_prev, "tm", -1)
-    part = own_push(info, tiles, times_q, result, ratio, child_b, child_t) + back
+    part = own_push(info, tiles, log_t, result, ratio, child_b) + back
     received = lax.all_to_all(part.reshape(TILES, BACK_ROWS, 1, LANES), "grp", 0, 0)
-    grad, log_intensity = collect(window_start, live, received.reshape(TILES * BACK_ROWS, LANES))
+    grad, log_intensity = collect(dealt, received.reshape(TILES * BACK_ROWS, LANES))
     return (grad, log_intensity)
 
 

time: 94.2 us -> 93.6 us (level)
  blocking collectives: 22 us -> 19.6 us
  Pallas kernels: 29.8 us -> 31.3 us
    all_to_all x1, blocking collectives: 22 us -> 19.6 us  [per_device(): lax.all_to_all(part.reshape(TILES, BACK_ROWS, 1, LANES), 'grp', 0, 0)]
    pallas_call x3, Pallas kernels: 25.9 us -> 27.9 us  [call(): pl.pallas_call(kernel, out_shape=[jax.ShapeDtypeStruct(shape, jnp.float32...]
  transfers between devices with their start and end apart: 3 -> 3, of which waited for: 2 -> 2; matrix products, arithmetic and copies ran while one was open for 0% -> 0% of each run, Pallas kernels for 17% -> 18%
where the time goes in v9:
time: 93.6 us; the launch traced here: 93.3 us
  Pallas kernels  31.3 us (33%)
  starting transfers between devices  21.6 us (23%)
  blocking collectives  19.6 us (21%)
  waiting for transfers between devices  19.2 us (21%)
  between operations  1.39 us (1%)
    pallas_call x3, Pallas kernels, call(): pl.pallas_call(kernel, out_shape=[jax.ShapeDtypeStruct(shape, jnp.float32...  27.9 us
    all_to_all x1, blocking collectives, per_device(): lax.all_to_all(part.reshape(TILES, BACK_ROWS, 1, LANES), 'grp', 0, 0)  19.6 us
    all_to_all x1, waiting for transfers between devices, per_device(): own = lax.all_to_all(sent.reshape(TILES, ROWS // 2, 2, LANES), 'grp', 0, 0)  16.8 us
    all_to_all x1, starting transfers between devices, per_device(): own = lax.all_to_all(sent.reshape(TILES, ROWS // 2, 2, LANES), 'grp', 0, 0)  12.9 us
    ppermute x2, starting transfers between devices, from_behind(): return lax.ppermute(value, axis, pairs)  8.68 us
    ppermute x2, waiting for transfers between devices, from_behind(): return lax.ppermute(value, axis, pairs)  2.32 us
    pallas_call x1, Pallas kernels, pack(): pl.pallas_call(pack_kernel, out_shape=[jax.ShapeDtypeStruct((TILES * ROWS...  2.22 us
  transfers between devices with their start and end apart: 3, of which 2 were waited for; matrix products, arithmetic and copies ran while one was open for 0% of the time, Pallas kernels for 18%

profile of v9, /device:TPU:25, one launch (start us, length us, event | category | flops | bytes accessed | tf_op | source)
XLA Modules:
  0.0 93.3 jit_solution(17323450792425744379)
XLA Ops:
  1.3 2.2 %shard_map.77 = (f32[1088,128]{1,0:T(8,128)}, s32[8,128]{1,0:T(8,128)}) custom-call(s32[2]{0:T(128)} %refs_0_.1, s32[1]{0:T(128)S(6)} %copy.14.refs_1_, f32[16,2,128]{2,1,0:T(2,128)} %refs_2_.1, f32[1,128]{1,0:T(1,128)} %bitcast.59, f32[1,128]{1,0:T(1,128)} %bitcast.60, f32[16,128]{1,0:T(8,128)} %refs_5_.1), custom_call_target="tpu_custom_call" | custom-call | tf_op jit(solution)/shard_map/pallas_call | solution.py:388
  3.5 12.9 %all-to-all-start = ((f32[32,17,2,128]{3,2,1,0:T(2,128)}), f32[32,17,2,128]{3,2,1,0:T(2,128)S(1)}, u32[]{:S(2)}, u32[]{:S(2)}) async-start(f32[32,17,2,128]{3,2,1,0:T(2,128)} %bitcast.55), calls=%async_computation | async-start | bytes 1114112 | tf_op jit(solution)/shard_map/all_to_all | solution.py:468
  16.4 16.8 %all-to-all-done = f32[32,17,2,128]{3,2,1,0:T(2,128)S(1)} async-done(((f32[32,17,2,128]{3,2,1,0:T(2,128)}), f32[32,17,2,128]{3,2,1,0:T(2,128)S(1)}, u32[]{:S(2)}, u32[]{:S(2)}) %all-to-all-start) | async-done | bytes 557088 | tf_op jit(solution)/shard_map/all_to_all | solution.py:468
  33.3 0.1 slice.16
  33.4 0.1 copy.12
  33.4 6.8 %collective-permute-start = (f32[1088,128]{1,0:T(8,128)S(1)}, f32[1088,128]{1,0:T(8,128)S(1)}, u32[]{:S(2)}, u32[]{:S(2)}) collective-permute-start(f32[1088,128]{1,0:T(8,128)S(1)} %bitcast.51), channel_id=1, source_target_pairs={{0,32},{32,64},{64,96},{96,128},{128,160},{160,192},{192,224},{224... | collective-permute-start | bytes 1671176 | tf_op jit(solution)/shard_map/ppermute | solution.py:42
  40.3 9.4 %shard_map.78 = (f32[56,128]{1,0:T(8,128)S(1)}, f32[128,48,128]{2,1,0:T(8,128)S(1)}, f32[128,32,128]{2,1,0:T(8,128)S(1)}, f32[128,128]{1,0:T(8,128)S(1)}, f32[32...) custom-call(s32[3,32]{1,0:T(4,128)S(1)} %pad_add_fusion.info, f32[1088,128]{1,0:T(8,128)S(1)} %bitcast.52), custom_call_target="tpu_custom_call" | custom-call | tf_op jit(solution)/shard_map/pallas_call | solution.py:335
  49.7 0.0 collective-permute-done.flat
  49.7 10.9 %shard_map.79 = (f32[1056,128]{1,0:T(8,128)S(1)}, f32[48,128]{1,0:T(8,128)S(1)}, f32[16,128]{1,0:T(8,128)S(1)}) custom-call(s32[3,32]{1,0:T(4,128)S(1)} %pad_add_fusion.info, f32[1088,128]{1,0:T(8,128)S(1)} %collective-permute-done.flat, f32[56,128]{1,0:T(8,128)S(1)} %get-tuple-element.17.packed, f32[128,48,128]{2,1,0:T(8,128)S(1)} %get-tuple-element.18.own_sums, ...), custom_call_target="tpu_custom_call" | custom-call | tf_op jit(solution)/shard_map/pallas_call | solution.py:335
  60.6 1.9 %collective-permute-start.1 = (f32[1056,128]{1,0:T(8,128)S(1)}, f32[1056,128]{1,0:T(8,128)S(1)}, u32[]{:S(2)}, u32[]{:S(2)}) collective-permute-start(f32[1056,128]{1,0:T(8,128)S(1)} %get-tuple-element.23), channel_id=1, source_target_pairs={{32,0},{64,32},{96,64},{128,96},{160,128},{192,160},{224,192},{256... | collective-permute-start | bytes 1622024 | tf_op jit(solution)/shard_map/ppermute | solution.py:42
  62.5 7.6 %shard_map.80 = f32[1056,128]{1,0:T(8,128)S(1)} custom-call(s32[3,32]{1,0:T(4,128)S(1)} %pad_add_fusion.info, f32[32,32,128]{2,1,0:T(8,128)S(1)} %get-tuple-element.15.own, f32[128,32,128]{2,1,0:T(8,128)S(1)} %get-tuple-element.16.log_t, f32[48,128]{1,0:T(8,128)S(1)} %get-tuple-element.21.result, f32[16,128]{1,0:T(8,128)S(1)} %get-tuple-element.22.ratio, ...), custom_call_target="tpu_custom_call" | custom-call | tf_op jit(solution)/shard_map/pallas_call | solution.py:335
  70.2 0.0 copy-start
  70.2 2.3 %collective-permute-done.1 = f32[1056,128]{1,0:T(8,128)S(1)} collective-permute-done((f32[1056,128]{1,0:T(8,128)S(1)}, f32[1056,128]{1,0:T(8,128)S(1)}, u32[]{:S(2)}, u32[]{:S(2)}) %collective-permute-start.1) | collective-permute-done | bytes 540704 | tf_op jit(solution)/shard_map/ppermute | solution.py:42
  72.5 0.1 add.185
  72.6 19.6 %all_to_all.10 = f32[32,33,1,128]{3,2,1,0:T(1,128)S(1)} all-to-all(f32[32,33,1,128]{3,2,1,0:T(1,128)S(1)} %bitcast.54), channel_id=1, replica_groups=mesh['tm'=16,'grp'=32] {'grp'}, dimensions={0} | all-to-all | bytes 1081344 | tf_op jit(solution)/shard_map/all_to_all | solution.py:477
  92.2 0.0 copy-done
  92.2 1.1 %shard_map.81 = (f32[16,2,128]{2,1,0:T(2,128)}, f32[16,128]{1,0:T(8,128)}) custom-call(s32[8,128]{1,0:T(8,128)S(1)} %copy-done, f32[1056,128]{1,0:T(8,128)S(1)} %bitcast.53), custom_call_target="tpu_custom_call" | custom-call | tf_op jit(solution)/shard_map/pallas_call | solution.py:416
  (4 shorter events, 0.1 us)
Async XLA Ops:
  3.5 29.8 %all-to-all-start = ((f32[32,17,2,128]{3,2,1,0:T(2,128)}), f32[32,17,2,128]{3,2,1,0:T(2,128)S(1)}, u32[]{:S(2)}, u32[]{:S(2)}) async-start(f32[32,17,2,128]{3,2,1,0:T(2,128)} %bitcast.55), calls=%async_computation | async-start | bytes 1114112 | tf_op jit(solution)/shard_map/all_to_all | solution.py:468
  33.4 16.3 %collective-permute-start = (f32[1088,128]{1,0:T(8,128)S(1)}, f32[1088,128]{1,0:T(8,128)S(1)}, u32[]{:S(2)}, u32[]{:S(2)}) collective-permute-start(f32[1088,128]{1,0:T(8,128)S(1)} %bitcast.51), channel_id=1, source_target_pairs={{0,32},{32,64},{64,96},{96,128},{128,160},{160,192},{192,224},{224... | collective-permute-start | bytes 1671176 | tf_op jit(solution)/shard_map/ppermute | solution.py:42
  60.6 11.9 %collective-permute-start.1 = (f32[1056,128]{1,0:T(8,128)S(1)}, f32[1056,128]{1,0:T(8,128)S(1)}, u32[]{:S(2)}, u32[]{:S(2)}) collective-permute-start(f32[1056,128]{1,0:T(8,128)S(1)} %get-tuple-element.23), channel_id=1, source_target_pairs={{32,0},{64,32},{96,64},{128,96},{160,128},{192,160},{224,192},{256... | collective-permute-start | bytes 1622024 | tf_op jit(solution)/shard_map/ppermute | solution.py:42
  70.2 22.0 %copy-start = (s32[8,128]{1,0:T(8,128)S(1)}, s32[8,128]{1,0:T(8,128)}, u32[]{:S(2)}) copy-start(s32[8,128]{1,0:T(8,128)} %get-tuple-element.13.dealt) | copy-start | bytes 12292

commit v10 on v9

--- a/solution.py
+++ b/solution.py
@@ -61,12 +61,12 @@
         out[child] = jnp.broadcast_to(values[:, child : child + 1], (rows, LANES))
 
 
-def gather_lanes(sums):
+def gather_lanes(sums, rows):
     lane = lane_ids()
-    collected = jnp.zeros(sums.shape[1:], jnp.float32)
+    collected = jnp.zeros((rows.stop - rows.start, LANES), jnp.float32)
     for child in range(LANES):
-        collected = jnp.where(lane == child, jnp.sum(sums[child], axis=1, keepdims=True), collected)
-    return [collected[j * CH : (j + 1) * CH] for j in range(3)]
+        collected = jnp.where(lane == child, jnp.sum(sums[child, rows], axis=1, keepdims=True), collected)
+    return collected
 
 
 def mirrored(tile):
@@ -230,8 +230,8 @@
 
 
 def prev_kernel(
-    info, flat, packed, own_sums, child_b, child_t, part, result, ratio_out,
-    log_t, kern, sums, total, times_q, prev
+    info, flat, packed, own_sums, child_b, child_t, part, logs, ratio_out, sums,
+    log_t, kern, terms, total, times_q, prev
 ):
     unpack_tiles(flat, prev, times_q)
 
@@ -252,16 +252,14 @@
 
     lax.fori_loop(0, SLOTS, slot, 0)
 
-    summed, pull_x, pull_y = gather_lanes(sums)
+    summed = gather_lanes(sums, slice(0, CH))
     xs, ys, weights = packed[0:CH], packed[CH : 2 * CH], packed[W_ROW : W_ROW + CH]
     intensity = packed[BACK_ROW : BACK_ROW + 1] + summed
     alive = packed[TIME_ROW : TIME_ROW + 1] >= 0.0
     ratio = weights / intensity
     ratio_out[...] = ratio
-    result[0:CH] = ratio * pull_x * UNSCALE
-    result[CH : 2 * CH] = ratio * pull_y * UNSCALE
-    result[2 * CH :] = jnp.where(alive, jnp.log(intensity), 0.0)
-    spread_lanes(sums, jnp.concatenate([ratio, ratio * xs, ratio * ys], axis=0))
+    logs[...] = jnp.where(alive, jnp.log(intensity), 0.0)
+    spread_lanes(terms, jnp.concatenate([ratio, ratio * xs, ratio * ys], axis=0))
 
     def clear(q, carry):
         total[q] = jnp.zeros((3 * CH, LANES), jnp.float32)
@@ -275,7 +273,7 @@
                 ks = [kern[QUAD * s + i, q] for i in range(QUAD)]
                 for j in range(3):
                     at = slice(j * CH, (j + 1) * CH)
-                    add = [ks[i] * sums[QUAD * s + i, at] for i in range(QUAD)]
+                    add = [ks[i] * terms[QUAD * s + i, at] for i in range(QUAD)]
                     total[q, at] = total[q, at] + ((add[0] + add[1]) + (add[2] + add[3]))
 
         short_steps(prev_start(info, s), HALF, body)
@@ -291,7 +289,7 @@
         part[BACK_ROWS * q + LOG_ROW : BACK_ROWS * (q + 1)] = jnp.zeros((1, LANES), jnp.float32)
 
 
-def own_push_kernel(info, own, log_t, result, ratio, child_b, flat, ratio_b, part, slot_logs):
+def own_push_kernel(info, own, log_t, logs, ratio, sums, child_b, flat, ratio_b, part, slot_logs):
     lane = lane_ids()
     spread_lanes(ratio_b, ratio[...] * -UNSCALE)
 
@@ -320,10 +318,11 @@
 
     lax.fori_loop(0, SLOTS, slot, 0)
 
-    slot_logs[...] = rows_of_quads(result[2 * CH :])
+    slot_logs[...] = rows_of_quads(logs[...])
+    side = jnp.concatenate([ratio[...], ratio[...]], axis=0) * gather_lanes(sums, slice(CH, 3 * CH)) * UNSCALE
     for s in range(SLOTS):
         at = lax.rem(info[FIRST, s], LANES)
-        moved = pltpu.roll(result[0 : 2 * CH], lax.rem(at + LANES - QUAD * s, LANES), 1)
+        moved = pltpu.roll(side, lax.rem(at + LANES - QUAD * s, LANES), 1)
         here = (lane >= at) & (lane < at + QUAD)
         at = BACK_ROWS * s
         flat[at : at + 2 * CH] = part[s] + jnp.where(here, moved, 0.0)
@@ -438,7 +437,7 @@
 def prev_pairs(info, *operands):
     return call(
         prev_kernel,
-        [(TILES * BACK_ROWS, LANES), (3 * CH, LANES), (CH, LANES)],
+        [(TILES * BACK_ROWS, LANES), (CH, LANES), (CH, LANES), SUMS],
         [LOG_T, (LANES, TILES, CH, LANES), SUMS, (TILES, 3 * CH, LANES), TIMES, XY],
         (info,), *operands, mib=42,
     )
@@ -471,9 +470,9 @@
     meta = own[:, QUAD_ROW // 2, QUAD_ROW % 2, META_LANE : META_LANE + 3]
     info = plan(meta, lax.axis_index("grp").astype(jnp.int32), lax.axis_index("tm") == 0)
     packed, sums, child_b, child_t, tiles, log_t = own_sums(info, flat)
-    part_prev, result, ratio = prev_pairs(info, prev, packed, sums, child_b, child_t)
+    part_prev, logs, ratio, pulls = prev_pairs(info, prev, packed, sums, child_b, child_t)
     back = from_behind(part_prev, "tm", -1)
-    part = own_push(info, tiles, log_t, result, ratio, child_b) + back
+    part = own_push(info, tiles, log_t, logs, ratio, pulls, child_b) + back
     received = lax.all_to_all(part.reshape(TILES, BACK_ROWS, 1, LANES), "grp", 0, 0)
     grad, log_intensity = collect(dealt, received.reshape(TILES * BACK_ROWS, LANES))
     return (grad, log_intensity)

time: 93.6 us -> 92.6 us (0.989)
  Pallas kernels: 31.3 us -> 28.2 us
  blocking collectives: 19.6 us -> 21.4 us
    pallas_call x3, Pallas kernels: 27.9 us -> 24.8 us  [call(): pl.pallas_call(kernel, out_shape=[jax.ShapeDtypeStruct(shape, jnp.float32...]
    all_to_all x1, blocking collectives: 19.6 us -> 21.4 us  [per_device(): lax.all_to_all(part.reshape(TILES, BACK_ROWS, 1, LANES), 'grp', 0, 0)]
  transfers between devices with their start and end apart: 3 -> 3, of which waited for: 2 -> 2; matrix products, arithmetic and copies ran while one was open for 0% -> 0% of each run, Pallas kernels for 18% -> 17%
where the time goes in v10:
time: 92.6 us; the launch traced here: 92.2 us
  Pallas kernels  28.2 us (30%)
  starting transfers between devices  21.6 us (23%)
  blocking collectives  21.4 us (23%)
  waiting for transfers between devices  19.4 us (21%)
  between operations  1.39 us (2%)
    pallas_call x3, Pallas kernels, call(): pl.pallas_call(kernel, out_shape=[jax.ShapeDtypeStruct(shape, jnp.float32...  24.8 us
    all_to_all x1, blocking collectives, per_device(): lax.all_to_all(part.reshape(TILES, BACK_ROWS, 1, LANES), 'grp', 0, 0)  21.4 us
    all_to_all x1, waiting for transfers between devices, per_device(): own = lax.all_to_all(sent.reshape(TILES, ROWS // 2, 2, LANES), 'grp', 0, 0)  16.8 us
    all_to_all x1, starting transfers between devices, per_device(): own = lax.all_to_all(sent.reshape(TILES, ROWS // 2, 2, LANES), 'grp', 0, 0)  12.9 us
    ppermute x2, starting transfers between devices, from_behind(): return lax.ppermute(value, axis, pairs)  8.68 us
    ppermute x2, waiting for transfers between devices, from_behind(): return lax.ppermute(value, axis, pairs)  2.57 us
    pallas_call x1, Pallas kernels, pack(): pl.pallas_call(pack_kernel, out_shape=[jax.ShapeDtypeStruct((TILES * ROWS...  2.22 us
  transfers between devices with their start and end apart: 3, of which 2 were waited for; matrix products, arithmetic and copies ran while one was open for 0% of the time, Pallas kernels for 17%

profile of v10, /device:TPU:25, one launch (start us, length us, event | category | flops | bytes accessed | tf_op | source)
XLA Modules:
  0.0 92.2 jit_solution(9576405015511791274)
XLA Ops:
  1.3 2.2 %shard_map.77 = (f32[1088,128]{1,0:T(8,128)}, s32[8,128]{1,0:T(8,128)}) custom-call(s32[2]{0:T(128)} %refs_0_.1, s32[1]{0:T(128)S(6)} %copy.14.refs_1_, f32[16,2,128]{2,1,0:T(2,128)} %refs_2_.1, f32[1,128]{1,0:T(1,128)} %bitcast.59, f32[1,128]{1,0:T(1,128)} %bitcast.60, f32[16,128]{1,0:T(8,128)} %refs_5_.1), custom_call_target="tpu_custom_call" | custom-call | tf_op jit(solution)/shard_map/pallas_call | solution.py:387
  3.5 12.9 %all-to-all-start = ((f32[32,17,2,128]{3,2,1,0:T(2,128)}), f32[32,17,2,128]{3,2,1,0:T(2,128)S(1)}, u32[]{:S(2)}, u32[]{:S(2)}) async-start(f32[32,17,2,128]{3,2,1,0:T(2,128)} %bitcast.55), calls=%async_computation | async-start | bytes 1114112 | tf_op jit(solution)/shard_map/all_to_all | solution.py:467
  16.4 16.8 %all-to-all-done = f32[32,17,2,128]{3,2,1,0:T(2,128)S(1)} async-done(((f32[32,17,2,128]{3,2,1,0:T(2,128)}), f32[32,17,2,128]{3,2,1,0:T(2,128)S(1)}, u32[]{:S(2)}, u32[]{:S(2)}) %all-to-all-start) | async-done | bytes 557088 | tf_op jit(solution)/shard_map/all_to_all | solution.py:467
  33.3 0.1 slice.16
  33.4 0.1 copy.12
  33.4 6.8 %collective-permute-start = (f32[1088,128]{1,0:T(8,128)S(1)}, f32[1088,128]{1,0:T(8,128)S(1)}, u32[]{:S(2)}, u32[]{:S(2)}) collective-permute-start(f32[1088,128]{1,0:T(8,128)S(1)} %bitcast.51), channel_id=1, source_target_pairs={{0,32},{32,64},{64,96},{96,128},{128,160},{160,192},{192,224},{224... | collective-permute-start | bytes 1671176 | tf_op jit(solution)/shard_map/ppermute | solution.py:42
  40.3 8.7 %shard_map.78 = (f32[56,128]{1,0:T(8,128)S(1)}, f32[128,48,128]{2,1,0:T(8,128)S(1)}, f32[128,32,128]{2,1,0:T(8,128)S(1)}, f32[128,128]{1,0:T(8,128)S(1)}, f32[32...) custom-call(s32[3,32]{1,0:T(4,128)S(1)} %pad_add_fusion.info, f32[1088,128]{1,0:T(8,128)S(1)} %bitcast.52), custom_call_target="tpu_custom_call" | custom-call | tf_op jit(solution)/shard_map/pallas_call | solution.py:334
  49.0 0.0 collective-permute-done.flat
  49.0 8.8 %shard_map.79 = (f32[1056,128]{1,0:T(8,128)S(1)}, f32[16,128]{1,0:T(8,128)S(1)}, f32[16,128]{1,0:T(8,128)S(1)}, f32[128,48,128]{2,1,0:T(8,128)S(1)}) custom-call(s32[3,32]{1,0:T(4,128)S(1)} %pad_add_fusion.info, f32[1088,128]{1,0:T(8,128)S(1)} %collective-permute-done.flat, f32[56,128]{1,0:T(8,128)S(1)} %get-tuple-element.18.packed, ...), custom_call_target="tpu_custom_call" | custom-call | tf_op jit(solution)/shard_map/pallas_call | solution.py:334
  57.8 1.9 %collective-permute-start.1 = (f32[1056,128]{1,0:T(8,128)S(1)}, f32[1056,128]{1,0:T(8,128)S(1)}, u32[]{:S(2)}, u32[]{:S(2)}) collective-permute-start(f32[1056,128]{1,0:T(8,128)S(1)} %get-tuple-element.25), channel_id=1, source_target_pairs={{32,0},{64,32},{96,64},{128,96},{160,128},{192,160},{224,192},{256... | collective-permute-start | bytes 1622024 | tf_op jit(solution)/shard_map/ppermute | solution.py:42
  59.7 0.0 copy-start
  59.7 7.4 %shard_map.80 = f32[1056,128]{1,0:T(8,128)S(1)} custom-call(s32[3,32]{1,0:T(4,128)S(1)} %pad_add_fusion.info, f32[32,32,128]{2,1,0:T(8,128)S(1)} %get-tuple-element.16.own, f32[128,32,128]{2,1,0:T(8,128)S(1)} %get-tuple-element.17.log_t, f32[16,128]{1,0:T(8,128)S(1)} %get-tuple-element.22.logs, f32[16,128]{1,0:T(8,128)S(1)} %get-tuple-element.23.ratio, ...), custom_call_target="tpu_custom_call" | custom-call | tf_op jit(solution)/shard_map/pallas_call | solution.py:334
  67.1 2.6 %collective-permute-done.1 = f32[1056,128]{1,0:T(8,128)S(1)} collective-permute-done((f32[1056,128]{1,0:T(8,128)S(1)}, f32[1056,128]{1,0:T(8,128)S(1)}, u32[]{:S(2)}, u32[]{:S(2)}) %collective-permute-start.1) | collective-permute-done | bytes 540704 | tf_op jit(solution)/shard_map/ppermute | solution.py:42
  69.7 0.1 add.185
  69.7 21.4 %all_to_all.10 = f32[32,33,1,128]{3,2,1,0:T(1,128)S(1)} all-to-all(f32[32,33,1,128]{3,2,1,0:T(1,128)S(1)} %bitcast.54), channel_id=1, replica_groups=mesh['tm'=16,'grp'=32] {'grp'}, dimensions={0} | all-to-all | bytes 1081344 | tf_op jit(solution)/shard_map/all_to_all | solution.py:476
  91.1 0.0 copy-done
  91.1 1.1 %shard_map.81 = (f32[16,2,128]{2,1,0:T(2,128)}, f32[16,128]{1,0:T(8,128)}) custom-call(s32[8,128]{1,0:T(8,128)S(1)} %copy-done, f32[1056,128]{1,0:T(8,128)S(1)} %bitcast.53), custom_call_target="tpu_custom_call" | custom-call | tf_op jit(solution)/shard_map/pallas_call | solution.py:415
  (4 shorter events, 0.1 us)
Async XLA Ops:
  3.5 29.8 %all-to-all-start = ((f32[32,17,2,128]{3,2,1,0:T(2,128)}), f32[32,17,2,128]{3,2,1,0:T(2,128)S(1)}, u32[]{:S(2)}, u32[]{:S(2)}) async-start(f32[32,17,2,128]{3,2,1,0:T(2,128)} %bitcast.55), calls=%async_computation | async-start | bytes 1114112 | tf_op jit(solution)/shard_map/all_to_all | solution.py:467
  33.4 15.5 %collective-permute-start = (f32[1088,128]{1,0:T(8,128)S(1)}, f32[1088,128]{1,0:T(8,128)S(1)}, u32[]{:S(2)}, u32[]{:S(2)}) collective-permute-start(f32[1088,128]{1,0:T(8,128)S(1)} %bitcast.51), channel_id=1, source_target_pairs={{0,32},{32,64},{64,96},{96,128},{128,160},{160,192},{192,224},{224... | collective-permute-start | bytes 1671176 | tf_op jit(solution)/shard_map/ppermute | solution.py:42
  57.8 11.9 %collective-permute-start.1 = (f32[1056,128]{1,0:T(8,128)S(1)}, f32[1056,128]{1,0:T(8,128)S(1)}, u32[]{:S(2)}, u32[]{:S(2)}) collective-permute-start(f32[1056,128]{1,0:T(8,128)S(1)} %get-tuple-element.25), channel_id=1, source_target_pairs={{32,0},{64,32},{96,64},{128,96},{160,128},{192,160},{224,192},{256... | collective-permute-start | bytes 1622024 | tf_op jit(solution)/shard_map/ppermute | solution.py:42
  59.7 31.4 %copy-start = (s32[8,128]{1,0:T(8,128)S(1)}, s32[8,128]{1,0:T(8,128)}, u32[]{:S(2)}) copy-start(s32[8,128]{1,0:T(8,128)} %get-tuple-element.14.dealt) | copy-start | bytes 12292

commit v11 on v9

--- a/solution.py
+++ b/solution.py
@@ -94,15 +94,15 @@
         times_q[q : q + 1] = flat[ROWS * q + TIME_ROW : ROWS * q + TIME_ROW + 1]
 
 
-def time_rows(info, s, log_t, child_t, times_q, own):
-    pos = lax.broadcasted_iota(jnp.int32, (TILES, LANES), 0) * LANES + (TILES * LANES if own else 0)
-    pos = pos + lax.broadcasted_iota(jnp.int32, (TILES, LANES), 1)
+def time_rows(info, s, log_t, child_t, times_q, own, first, last):
+    pos = lax.broadcasted_iota(jnp.int32, (last - first, LANES), 0) * LANES + (first + (TILES if own else 0)) * LANES
+    pos = pos + lax.broadcasted_iota(jnp.int32, (last - first, LANES), 1)
     ok = pos >= info[LOW, s]
     for i in range(QUAD):
         at = QUAD * s + i
-        delta = jnp.maximum(child_t[pl.ds(at, 1)] - times_q[...], 0.0)
+        delta = jnp.maximum(child_t[pl.ds(at, 1)] - times_q[first:last], 0.0)
         allowed = ok & (pos < info[FIRST, s] + i) if own else ok
-        log_t[at] = jnp.where(allowed, log2_time_kernel(delta), DEAD)
+        log_t[at, first:last] = jnp.where(allowed, log2_time_kernel(delta), DEAD)
 
 
 def kernel_of(tiles, q, child_b, log_t, at):
@@ -205,14 +205,16 @@
     spread_lanes(child_b, mine)
     child_t[...] = jnp.transpose(jnp.broadcast_to(child_times, (LANES, LANES)))
 
-    def times(s, carry):
-        @pl.when(info[VALID, s] > 0)
-        def _():
-            time_rows(info, s, log_t, child_t, times_q, True)
-
-        return carry
-
-    lax.fori_loop(0, SLOTS, times, 0)
+    for begin, last in ((0, HALF), (HALF, TILES)):
+
+        def times(s, carry, last=last):
+            @pl.when(info[VALID, s] > 0)
+            def _():
+                time_rows(info, s, log_t, child_t, times_q, True, 0, last)
+
+            return carry
+
+        lax.fori_loop(begin, begin + HALF, times, 0)
 
     def clear(s, carry):
         for i in range(QUAD):
@@ -235,14 +237,16 @@
 ):
     unpack_tiles(flat, prev, times_q)
 
-    def times(s, carry):
-        @pl.when(info[LOW, s] < TILES * LANES)
-        def _():
-            time_rows(info, s, log_t, child_t, times_q, False)
-
-        return carry
-
-    lax.fori_loop(0, SLOTS, times, 0)
+    for begin in (0, HALF):
+
+        def times(s, carry, first=begin):
+            @pl.when(info[LOW, s] < TILES * LANES)
+            def _():
+                time_rows(info, s, log_t, child_t, times_q, False, first, TILES)
+
+            return carry
+
+        lax.fori_loop(begin, begin + HALF, times, 0)
 
     def slot(s, carry):
         for i in range(QUAD):

time: 93.6 us -> 92.2 us (0.985)
  transfers between devices with their start and end apart: 3 -> 3, of which waited for: 2 -> 2; matrix products, arithmetic and copies ran while one was open for 0% -> 0% of each run, Pallas kernels for 18% -> 17%
where the time goes in v11:
time: 92.2 us; the launch traced here: 92.6 us
  Pallas kernels  30.4 us (33%)
  starting transfers between devices  21.6 us (23%)
  waiting for transfers between devices  19.5 us (21%)
  blocking collectives  19.3 us (21%)
  between operations  1.39 us (2%)
    pallas_call x3, Pallas kernels, call(): pl.pallas_call(kernel, out_shape=[jax.ShapeDtypeStruct(shape, jnp.float32...  27.1 us
    all_to_all x1, blocking collectives, per_device(): lax.all_to_all(part.reshape(TILES, BACK_ROWS, 1, LANES), 'grp', 0, 0)  19.3 us
    all_to_all x1, waiting for transfers between devices, per_device(): own = lax.all_to_all(sent.reshape(TILES, ROWS // 2, 2, LANES), 'grp', 0, 0)  16.8 us
    all_to_all x1, starting transfers between devices, per_device(): own = lax.all_to_all(sent.reshape(TILES, ROWS // 2, 2, LANES), 'grp', 0, 0)  12.9 us
    ppermute x2, starting transfers between devices, from_behind(): return lax.ppermute(value, axis, pairs)  8.68 us
    ppermute x2, waiting for transfers between devices, from_behind(): return lax.ppermute(value, axis, pairs)  2.67 us
    pallas_call x1, Pallas kernels, pack(): pl.pallas_call(pack_kernel, out_shape=[jax.ShapeDtypeStruct((TILES * ROWS...  2.22 us
  transfers between devices with their start and end apart: 3, of which 2 were waited for; matrix products, arithmetic and copies ran while one was open for 0% of the time, Pallas kernels for 17%

profile of v11, /device:TPU:25, one launch (start us, length us, event | category | flops | bytes accessed | tf_op | source)
XLA Modules:
  0.0 92.6 jit_solution(8487170069180283610)
XLA Ops:
  1.3 2.2 %shard_map.77 = (f32[1088,128]{1,0:T(8,128)}, s32[8,128]{1,0:T(8,128)}) custom-call(s32[2]{0:T(128)} %refs_0_.1, s32[1]{0:T(128)S(6)} %copy.14.refs_1_, f32[16,2,128]{2,1,0:T(2,128)} %refs_2_.1, f32[1,128]{1,0:T(1,128)} %bitcast.59, f32[1,128]{1,0:T(1,128)} %bitcast.60, f32[16,128]{1,0:T(8,128)} %refs_5_.1), custom_call_target="tpu_custom_call" | custom-call | tf_op jit(solution)/shard_map/pallas_call | solution.py:392
  3.5 12.9 %all-to-all-start = ((f32[32,17,2,128]{3,2,1,0:T(2,128)}), f32[32,17,2,128]{3,2,1,0:T(2,128)S(1)}, u32[]{:S(2)}, u32[]{:S(2)}) async-start(f32[32,17,2,128]{3,2,1,0:T(2,128)} %bitcast.55), calls=%async_computation | async-start | bytes 1114112 | tf_op jit(solution)/shard_map/all_to_all | solution.py:472
  16.4 16.8 %all-to-all-done = f32[32,17,2,128]{3,2,1,0:T(2,128)S(1)} async-done(((f32[32,17,2,128]{3,2,1,0:T(2,128)}), f32[32,17,2,128]{3,2,1,0:T(2,128)S(1)}, u32[]{:S(2)}, u32[]{:S(2)}) %all-to-all-start) | async-done | bytes 557088 | tf_op jit(solution)/shard_map/all_to_all | solution.py:472
  33.3 0.1 slice.16
  33.4 0.1 copy.12
  33.4 6.8 %collective-permute-start = (f32[1088,128]{1,0:T(8,128)S(1)}, f32[1088,128]{1,0:T(8,128)S(1)}, u32[]{:S(2)}, u32[]{:S(2)}) collective-permute-start(f32[1088,128]{1,0:T(8,128)S(1)} %bitcast.51), channel_id=1, source_target_pairs={{0,32},{32,64},{64,96},{96,128},{128,160},{160,192},{192,224},{224... | collective-permute-start | bytes 1671176 | tf_op jit(solution)/shard_map/ppermute | solution.py:42
  40.3 8.6 %shard_map.78 = (f32[56,128]{1,0:T(8,128)S(1)}, f32[128,48,128]{2,1,0:T(8,128)S(1)}, f32[128,32,128]{2,1,0:T(8,128)S(1)}, f32[128,128]{1,0:T(8,128)S(1)}, f32[32...) custom-call(s32[3,32]{1,0:T(4,128)S(1)} %pad_add_fusion.info, f32[1088,128]{1,0:T(8,128)S(1)} %bitcast.52), custom_call_target="tpu_custom_call" | custom-call | tf_op jit(solution)/shard_map/pallas_call | solution.py:339
  48.9 0.0 collective-permute-done.flat
  49.0 11.2 %shard_map.79 = (f32[1056,128]{1,0:T(8,128)S(1)}, f32[48,128]{1,0:T(8,128)S(1)}, f32[16,128]{1,0:T(8,128)S(1)}) custom-call(s32[3,32]{1,0:T(4,128)S(1)} %pad_add_fusion.info, f32[1088,128]{1,0:T(8,128)S(1)} %collective-permute-done.flat, f32[56,128]{1,0:T(8,128)S(1)} %get-tuple-element.17.packed, f32[128,48,128]{2,1,0:T(8,128)S(1)} %get-tuple-element.18.own_sums, ...), custom_call_target="tpu_custom_call" | custom-call | tf_op jit(solution)/shard_map/pallas_call | solution.py:339
  60.1 1.9 %collective-permute-start.1 = (f32[1056,128]{1,0:T(8,128)S(1)}, f32[1056,128]{1,0:T(8,128)S(1)}, u32[]{:S(2)}, u32[]{:S(2)}) collective-permute-start(f32[1056,128]{1,0:T(8,128)S(1)} %get-tuple-element.23), channel_id=1, source_target_pairs={{32,0},{64,32},{96,64},{128,96},{160,128},{192,160},{224,192},{256... | collective-permute-start | bytes 1622024 | tf_op jit(solution)/shard_map/ppermute | solution.py:42
  62.1 7.3 %shard_map.80 = f32[1056,128]{1,0:T(8,128)S(1)} custom-call(s32[3,32]{1,0:T(4,128)S(1)} %pad_add_fusion.info, f32[32,32,128]{2,1,0:T(8,128)S(1)} %get-tuple-element.15.own, f32[128,32,128]{2,1,0:T(8,128)S(1)} %get-tuple-element.16.log_t, f32[48,128]{1,0:T(8,128)S(1)} %get-tuple-element.21.result, f32[16,128]{1,0:T(8,128)S(1)} %get-tuple-element.22.ratio, ...), custom_call_target="tpu_custom_call" | custom-call | tf_op jit(solution)/shard_map/pallas_call | solution.py:339
  69.3 0.0 copy-start
  69.4 2.7 %collective-permute-done.1 = f32[1056,128]{1,0:T(8,128)S(1)} collective-permute-done((f32[1056,128]{1,0:T(8,128)S(1)}, f32[1056,128]{1,0:T(8,128)S(1)}, u32[]{:S(2)}, u32[]{:S(2)}) %collective-permute-start.1) | collective-permute-done | bytes 540704 | tf_op jit(solution)/shard_map/ppermute | solution.py:42
  72.0 0.1 add.185
  72.1 19.3 %all_to_all.10 = f32[32,33,1,128]{3,2,1,0:T(1,128)S(1)} all-to-all(f32[32,33,1,128]{3,2,1,0:T(1,128)S(1)} %bitcast.54), channel_id=1, replica_groups=mesh['tm'=16,'grp'=32] {'grp'}, dimensions={0} | all-to-all | bytes 1081344 | tf_op jit(solution)/shard_map/all_to_all | solution.py:481
  91.4 0.0 copy-done
  91.4 1.1 %shard_map.81 = (f32[16,2,128]{2,1,0:T(2,128)}, f32[16,128]{1,0:T(8,128)}) custom-call(s32[8,128]{1,0:T(8,128)S(1)} %copy-done, f32[1056,128]{1,0:T(8,128)S(1)} %bitcast.53), custom_call_target="tpu_custom_call" | custom-call | tf_op jit(solution)/shard_map/pallas_call | solution.py:420
  (4 shorter events, 0.1 us)
Async XLA Ops:
  3.5 29.8 %all-to-all-start = ((f32[32,17,2,128]{3,2,1,0:T(2,128)}), f32[32,17,2,128]{3,2,1,0:T(2,128)S(1)}, u32[]{:S(2)}, u32[]{:S(2)}) async-start(f32[32,17,2,128]{3,2,1,0:T(2,128)} %bitcast.55), calls=%async_computation | async-start | bytes 1114112 | tf_op jit(solution)/shard_map/all_to_all | solution.py:472
  33.4 15.5 %collective-permute-start = (f32[1088,128]{1,0:T(8,128)S(1)}, f32[1088,128]{1,0:T(8,128)S(1)}, u32[]{:S(2)}, u32[]{:S(2)}) collective-permute-start(f32[1088,128]{1,0:T(8,128)S(1)} %bitcast.51), channel_id=1, source_target_pairs={{0,32},{32,64},{64,96},{96,128},{128,160},{160,192},{192,224},{224... | collective-permute-start | bytes 1671176 | tf_op jit(solution)/shard_map/ppermute | solution.py:42
  60.1 11.9 %collective-permute-start.1 = (f32[1056,128]{1,0:T(8,128)S(1)}, f32[1056,128]{1,0:T(8,128)S(1)}, u32[]{:S(2)}, u32[]{:S(2)}) collective-permute-start(f32[1056,128]{1,0:T(8,128)S(1)} %get-tuple-element.23), channel_id=1, source_target_pairs={{32,0},{64,32},{96,64},{128,96},{160,128},{192,160},{224,192},{256... | collective-permute-start | bytes 1622024 | tf_op jit(solution)/shard_map/ppermute | solution.py:42
  69.3 22.1 %copy-start = (s32[8,128]{1,0:T(8,128)S(1)}, s32[8,128]{1,0:T(8,128)}, u32[]{:S(2)}) copy-start(s32[8,128]{1,0:T(8,128)} %get-tuple-element.13.dealt) | copy-start | bytes 12292
